TPU v7x, 32 devices: a whole 2x2x4 slice. The times are simulated.
32 devices in a mesh: voxel: 2 (over x), feature: 4 (over z), tm: 4 (over y, core).
Axes of the slice: x: 2, y: 2, z: 4, core: 2. Of those that a mesh axis runs over, the one named last changes fastest.
Arguments:
- hidden: bfloat16 [3072, 8192], P('tm', 'feature'), may hold values from -6 to 6
- bold: bfloat16 [3072, 256], P('tm', 'voxel'), may hold values from -6 to 6
- panel: bfloat16 [65536, 128], P(('feature', 'tm'), 'voxel'), may hold values from -0.0234375 to 0.0234375
- eigvals: float32 [128], replicated, may hold values from 0.05 to 2
- ridge_grid: int32 [24], replicated, may hold values from 0 to 16
- delays: int32 [8], replicated, may hold values from 1 to 12, as said below
- runs: int32 [3072], replicated, may hold values from 0 to 7, never falling along the last dimension, each value on 1 to 768 neighbouring positions
Outputs:
- scaled: bfloat16 [24, 128, 256], P(None, None, 'voxel')
Inputs may be any that keep to these rules, and one draw needn't show every extreme that they name: 8 distinct delays, 12 among them. `runs`: run numbers never fall along the TRs; a run holds 1 to 768 TRs.
All inputs are finite; a program needn't handle non-finite values.
Results may differ from a plain program's by a relative error of at most 0.022.
Values may be sent and summed in bfloat16 or wider, within the bound.
No kernel may reach another device: no remote copies, remote signals or barrier semaphores. Data moves between devices by JAX's collectives and lax.ppermute only.
A program may use at most 64 MiB of HBM per device.

v0:
```python
import math

import jax
import jax.numpy as jnp
from jax import lax
from jax.sharding import PartitionSpec as P

DELAYS = 8
MAXD = 12


def passed_along(value, axis, steps):
    count = lax.axis_size(axis)
    first, last = (max(0, -steps), min(count, count - steps))
    return lax.ppermute(value, axis, [(source, source + steps) for source in range(first, last)])


def contract_rows(left, right):
    return lax.dot_general(
        left, right, (((0,), (0,)), ((), ())), preferred_element_type=jnp.float32
    )


def shards(hidden, bold, panel, eigvals, ridge_grid, delays, runs):
    t_rows = hidden.shape[0]
    d_local = hidden.shape[1]
    v_cols = bold.shape[1]
    total_rows = t_rows * lax.axis_size("tm")
    first = lax.axis_index("tm") * t_rows
    ahead = passed_along(bold[:MAXD], "tm", -1)
    extended = jnp.concatenate([bold, ahead], 0)
    runs_pad = jnp.concatenate([runs, jnp.full((MAXD,), -1, jnp.int32)])
    own_runs = lax.dynamic_slice_in_dim(runs, first, t_rows)
    positions = first + jnp.arange(t_rows, dtype=jnp.int32)
    lagged_list = []
    for slot in range(DELAYS):
        offset = delays[slot]
        target_runs = lax.dynamic_slice_in_dim(runs_pad, first + offset, t_rows)
        valid = (positions + offset < total_rows) & (target_runs == own_runs)
        moved = lax.dynamic_slice_in_dim(extended, offset, t_rows, 0)
        lagged_list.append(jnp.where(valid[:, None], moved, jnp.zeros_like(moved)))
    stacked = jnp.stack(lagged_list, 1).reshape(t_rows, DELAYS * v_cols)
    cross = contract_rows(hidden, stacked)
    partial_cov = cross.reshape(d_local * DELAYS, v_cols).astype(jnp.bfloat16)
    panel_rows = lax.all_gather(panel, "tm", axis=0, tiled=True)
    rotated_part = contract_rows(
        lax.all_gather(panel_rows, "voxel", axis=1, tiled=True), partial_cov
    )
    rotated = lax.psum(rotated_part.astype(jnp.bfloat16), ("feature", "tm")).astype(jnp.float32)
    penalty = 2.0 ** ((ridge_grid.astype(jnp.float32) - 8.0) * 0.5)
    scaled = rotated[None] / (
        math.sqrt(total_rows) * (eigvals[None, :, None] + penalty[:, None, None])
    )
    return scaled.astype(jnp.bfloat16)


def solution(mesh):
    return jax.shard_map(
        shards,
        mesh=mesh,
        in_specs=(
            P("tm", "feature"),
            P("tm", "voxel"),
            P(("feature", "tm"), "voxel"),
            P(),
            P(),
            P(),
            P(),
        ),
        out_specs=P(None, None, "voxel"),
        check_vma=False,
    )
```

profile of v0, /device:TPU:0, one launch (start us, length us, event | category | flops | bytes accessed | tf_op | source)
XLA Modules:
  0.0 166.9 jit_solution(3137580492057806575)
XLA Ops:
  6.5 0.0 copy-start
  6.6 0.0 all-gather.3.cloned.1.call-start
  6.6 0.7 all-gather.3.cloned.1.call-update
  7.3 0.0 all-gather.5.cloned.1.call-start
  7.3 26.9 %all-gather.3.cloned.1.call-done = bf16[16384,64]{0,1:T(8,128)(2,1)} async-done(((bf16[4096,64]{0,1:T(8,128)(2,1)}), bf16[16384,64]{0,1:T(8,128)(2,1)}) %all-gather.3.cloned.1.call-update) | async-done | bytes 2097168 | tf_op jit(solution)/shard_map/all_gather | solution.py:45
  34.3 0.0 all-gather.5.cloned.1.call-update
  34.3 0.1 copy.9
  34.4 1.3 collective-permute-start
  35.7 0.0 copy-done.2
  35.8 0.7 fusion.49
  41.5 3.2 %fusion.48 = (pred[768]{0:T(1024)(128)(4,1)S(1)}, pred[768]{0:T(1024)(128)(4,1)S(1)}, pred[768]{0:T(1024)(128)(4,1)S(1)}, pred[768]{0:T(1024)(128)(4,1)S(1)}, pred[768]{0:T(1024)(128)(4,1)S(1)}) fusion(s32[]{:T(128)S(6)} %select_n.98, s32[3072]{0:T(1024)S(1)} %copy-done.1, s32[]{:T(128)} %bitcast.14, s32[]{:T(128)S(6)} %mul.17, s32[]{:T(128)S(6)} %select_n.77, ...), kind=kLoop, calls=%fused_computation.77 | loop fusion | flops 16128 | bytes 20272 | tf_op jit(solution)/shard_map/and | solution.py:39
  44.7 0.1 add_multiply_fusion
  44.8 2.0 %fusion.47 = (pred[768]{0:T(1024)(128)(4,1)S(1)}, pred[768]{0:T(1024)(128)(4,1)S(1)}, pred[768]{0:T(1024)(128)(4,1)S(1)}) fusion(s32[]{:T(128)S(6)} %select_n.95, s32[3072]{0:T(1024)S(1)} %copy-done.1, s32[]{:T(128)} %bitcast.12, s32[]{:T(128)S(6)} %mul.17, s32[]{:T(128)S(6)} %select_n.77, s32[]{:T(128)S(6)} %select_n.80, s32[]{:T(128)} %bitcast.2, ...), kind=kLoop, calls=%fused_computation.76 | loop fusion | flops 9984 | bytes 18720 | tf_op jit(solution)/shard_map/and | solution.py:39
  47.4 1.1 copy.10
  62.8 0.0 collective-permute-done
  62.8 0.2 fusion.8
  63.0 0.2 fusion.12
  63.2 0.2 fusion.16
  63.4 0.2 fusion.20
  63.7 0.2 fusion.24
  63.9 0.2 fusion.28
  64.1 0.2 fusion.32
  64.3 0.2 fusion.4
  64.5 0.0 copy-done
  64.5 5.0 %convert_bitcast_fusion = bf16[2048,1024]{0,1:T(8,128)(2,1)} fusion(bf16[768,1024]{0,1:T(8,128)(2,1)S(1)} %bitcast.49, bf16[768,2048]{1,0:T(8,128)(2,1)S(1)} %copy-done), kind=kOutput, calls=%fused_computation | convolution fusion | flops 3223322624 | bytes 8912896 | tf_op jit(solution)/shard_map/dot_general | solution.py:19
  69.5 6.3 %copy.11 = bf16[2048,1024]{1,0:T(8,128)(2,1)} copy(bf16[2048,1024]{0,1:T(8,128)(2,1)} %convert_bitcast_fusion) | data formatting | bytes 8388608 | tf_op jit(solution)/shard_map/convert_element_type | solution.py:44
  75.8 7.3 %convert_element_type.26 = bf16[16384,128]{1,0:T(8,128)(2,1)} reshape(bf16[2048,1024]{1,0:T(8,128)(2,1)} %copy.11) | data formatting | bytes 8388608 | tf_op jit(solution)/shard_map/convert_element_type | solution.py:44
  83.2 9.4 %all-gather.5.cloned.1.call-done = bf16[16384,128]{0,1:T(8,128)(2,1)} async-done(((bf16[16384,64]{0,1:T(8,128)(2,1)}), bf16[16384,128]{0,1:T(8,128)(2,1)}) %all-gather.5.cloned.1.call-update) | async-done | bytes 4194320 | tf_op jit(solution)/shard_map/all_gather | solution.py:47
  92.6 4.8 %fusion = bf16[128,128]{0,1:T(8,128)(2,1)S(1)} fusion(bf16[16384,128]{1,0:T(8,128)(2,1)} %convert_element_type.26, bf16[16384,128]{0,1:T(8,128)(2,1)} %all-gather.5.cloned.1.call-done), kind=kOutput, calls=%fused_computation.3 | convolution fusion | flops 536887296 | bytes 8421376 | tf_op jit(solution)/shard_map/dot_general | solution.py:19
  97.4 61.2 %psum.7 = bf16[128,128]{0,1:T(8,128)(2,1)S(1)} all-reduce(bf16[128,128]{0,1:T(8,128)(2,1)S(1)} %fusion), channel_id=1, replica_groups=mesh['voxel'=2,'feature'=4,'tm'=4] {'feature','tm'}, use_global_device_ids=true, to_apply=%region_0.1 | all-reduce | flops 16384 | bytes 65536 | tf_op jit(solution)/shard_map/psum | solution.py:49
  158.6 0.1 copy.12
  158.7 1.4 divide_convert_fusion
  (10 shorter events, 0.0 us)
Async XLA Ops:
  6.5 58.0 %copy-start = (bf16[768,2048]{1,0:T(8,128)(2,1)S(1)}, bf16[768,2048]{1,0:T(8,128)(2,1)}, u32[]{:S(2)}) copy-start(bf16[768,2048]{1,0:T(8,128)(2,1)} %param.7) | copy-start | bytes 9437188
  6.5 27.8 %slice-start = ((bf16[768,128]{1,0:T(8,128)(2,1)}), bf16[12,128]{1,0:T(8,128)(2,1)S(1)}, s32[]{:S(2)}) async-start(bf16[768,128]{1,0:T(8,128)(2,1)} %param.8), calls=%async_computation.2 | async-start | bytes 8192 | tf_op jit(solution)/shard_map/slice | solution.py:30
  6.5 29.2 %copy-start.2 = (s32[8]{0:T(128)S(1)}, s32[8]{0:T(128)}, u32[]{:S(2)}) copy-start(s32[8]{0:T(128)} %param.12) | copy-start | bytes 100
  6.5 34.9 %copy-start.1 = (s32[3072]{0:T(1024)S(1)}, s32[3072]{0:T(1024)}, u32[]{:S(2)}) copy-start(s32[3072]{0:T(1024)} %param.13) | copy-start | bytes 36868
  6.5 38.1 %copy-start.4 = (s32[24]{0:T(128)S(1)}, s32[24]{0:T(128)}, u32[]{:S(2)}) copy-start(s32[24]{0:T(128)} %param.11) | copy-start | bytes 292
  6.5 38.1 %copy-start.3 = (f32[128]{0:T(128)S(1)}, f32[128]{0:T(128)}, u32[]{:S(2)}) copy-start(f32[128]{0:T(128)} %param.10) | copy-start | bytes 1540
  6.6 27.7 %all-gather.3.cloned.1.call-start = ((), (), s32[]{:S(2)}) async-start(), calls=%async_computation | async-start | bytes 2621440 | tf_op jit(solution)/shard_map/all_gather | solution.py:45
  7.3 85.3 %all-gather.5.cloned.1.call-start = ((), (), s32[]{:S(2)}) async-start(), calls=%async_computation.1 | async-start | bytes 6291456 | tf_op jit(solution)/shard_map/all_gather | solution.py:47
  34.4 28.4 %collective-permute-start = (bf16[12,128]{0,1:T(8,128)(2,1)S(1)}, bf16[12,128]{0,1:T(8,128)(2,1)S(1)}, u32[]{:S(2)}, u32[]{:S(2)}) collective-permute-start(bf16[12,128]{0,1:T(8,128)(2,1)S(1)} %copy.9), channel_id=1, source_target_pairs={{1,0},{2,1},{3,2},{5,4},{6,5},{7,6},{9,8},{10,9},{11,10},{13,12},{... | collective-permute-start | bytes 9224 | tf_op jit(solution)/shard_map/ppermute | solution.py:15
Sparse Core Ops, SparseCore 0:
  9.0 25.2 all-gather.2
  35.8 56.7 all-gather.4
where the time goes:
time: 168 us; the launch traced here: 167 us
  blocking collectives  61.2 us (36%)
  waiting for transfers between devices  37.1 us (22%)
  between operations  33.5 us (20%)
  local copies, waits for them, and re-layouts  15.7 us (9%)
  matrix products  9.76 us (6%)
  other arithmetic  8.25 us (5%)
    psum x1, blocking collectives, shards(): lax.psum(rotated_part.astype(jnp.bfloat16), ('feature', 'tm'))  61.2 us
    all_gather x1, waiting for transfers between devices, shards(): panel_rows = lax.all_gather(panel, 'tm', axis=0, tiled=True)  26.9 us
    convert_element_type x2, local copies, waits for them, and re-layouts, shards(): partial_cov = cross.reshape(d_local * DELAYS, v_cols).astype(jnp.bfloat16)  13.7 us
    dot_general x2, matrix products, contract_rows(): lax.dot_general(left, right, (((0,), (0,)), ((), ())), preferred_element_...  9.76 us
    all_gather x1, waiting for transfers between devices, shards(): lax.all_gather(panel_rows, 'voxel', axis=1, tiled=True)  9.44 us
    and x2, other arithmetic, shards(): valid = (positions + offset < total_rows) & (target_runs == own_runs)  5.18 us
  transfers between devices with their start and end apart: 3, of which 2 were waited for; matrix products, arithmetic and copies ran while one was open for 16% of the time, Pallas kernels for 0%

commit v1 on v0

--- a/solution.py
+++ b/solution.py
@@ -1,12 +1,18 @@
+import functools
 import math
 
 import jax
 import jax.numpy as jnp
 from jax import lax
+from jax.experimental import pallas as pl
+from jax.experimental.pallas import tpu as pltpu
 from jax.sharding import PartitionSpec as P
 
 DELAYS = 8
 MAXD = 12
+LANES = 128
+F32 = jnp.float32
+BF16 = jnp.bfloat16
 
 
 def passed_along(value, axis, steps):
@@ -21,7 +27,15 @@
     )
 
 
-def shards(hidden, bold, panel, eigvals, ridge_grid, delays, runs):
+def scaled_by(rotated, eigvals, ridge_grid, total_rows):
+    penalty = 2.0 ** ((ridge_grid.astype(jnp.float32) - 8.0) * 0.5)
+    scaled = rotated[None] / (
+        math.sqrt(total_rows) * (eigvals[None, :, None] + penalty[:, None, None])
+    )
+    return scaled.astype(jnp.bfloat16)
+
+
+def gathered(hidden, bold, panel, eigvals, ridge_grid, delays, runs):
     t_rows = hidden.shape[0]
     d_local = hidden.shape[1]
     v_cols = bold.shape[1]
@@ -47,14 +61,185 @@
         lax.all_gather(panel_rows, "voxel", axis=1, tiled=True), partial_cov
     )
     rotated = lax.psum(rotated_part.astype(jnp.bfloat16), ("feature", "tm")).astype(jnp.float32)
-    penalty = 2.0 ** ((ridge_grid.astype(jnp.float32) - 8.0) * 0.5)
-    scaled = rotated[None] / (
-        math.sqrt(total_rows) * (eigvals[None, :, None] + penalty[:, None, None])
-    )
-    return scaled.astype(jnp.bfloat16)
+    return scaled_by(rotated, eigvals, ridge_grid, total_rows)
+
+
+def swapped(value, voxel, feature, tm):
+    sizes = (lax.axis_size("voxel"), lax.axis_size("feature"), lax.axis_size("tm"))
+    pairs = []
+    for v in range(sizes[0]):
+        for f in range(sizes[1]):
+            for t in range(sizes[2]):
+                source = (v * sizes[1] + f) * sizes[2] + t
+                target = ((v ^ voxel) * sizes[1] + (f ^ feature)) * sizes[2] + (t ^ tm)
+                pairs.append((source, target))
+    return lax.ppermute(value, ("voxel", "feature", "tm"), pairs)
+
+
+def lag_sums(scalars, panel_t, own, other, runs, sort, total, ordered, products):
+    p_cols = panel_t.shape[0]
+    rows, width = own.shape
+    block = DELAYS * LANES
+    groups = width // LANES
+    core = scalars[DELAYS]
+    stacked = jnp.concatenate([panel_t[:, g * block:(g + 1) * block] for g in range(groups)], 0)
+    by_slot = jnp.dot(stacked, sort[...], preferred_element_type=F32).astype(BF16)
+    for g in range(groups):
+        for k in range(DELAYS):
+            ordered[k * p_cols:(k + 1) * p_cols, g * LANES:(g + 1) * LANES] = by_slot[
+                g * p_cols:(g + 1) * p_cols, k * LANES:(k + 1) * LANES
+            ]
+    span = 2 * rows
+    products[:, :LANES] = jnp.zeros((DELAYS * p_cols, LANES), F32)
+    products[:, LANES + span:] = jnp.zeros((DELAYS * p_cols, LANES), F32)
+    for part, place in ((own, core), (other, 1 - core)):
+        products[:, pl.ds(pl.multiple_of(LANES + place * rows, LANES), rows)] = lax.dot_general(
+            ordered[...], part[...], (((1,), (1,)), ((), ())), preferred_element_type=F32
+        )
+    tiles = span // LANES + 1
+    lane = lax.broadcasted_iota(jnp.int32, (8, LANES), 1)
+    here = runs[...]
+    kept = []
+    for k in range(DELAYS):
+        kept.append((pltpu.roll(here, scalars[k], 1) == here).astype(F32))
+    for row in range(0, p_cols, 8):
+        sums = [total[row:row + 8, j * LANES:(j + 1) * LANES] for j in range(tiles)]
+        for k in range(DELAYS):
+            low = lane < scalars[k]
+            before = None
+            for j in range(tiles):
+                at = k * p_cols + row
+                now = pltpu.roll(
+                    products[at:at + 8, (j + 1) * LANES:(j + 2) * LANES], scalars[k], 1
+                )
+                if before is None:
+                    moved = jnp.where(low, 0.0, now)
+                else:
+                    moved = jnp.where(low, before, now)
+                before = now
+                sums[j] = sums[j] + moved * kept[k][:, j * LANES:(j + 1) * LANES]
+        for j in range(tiles):
+            total[row:row + 8, j * LANES:(j + 1) * LANES] = sums[j]
+
+
+def first_kernel(scalars, panel_t, own, other, runs, sort, total, ordered, products):
+    total[...] = jnp.zeros_like(total)
+    lag_sums(scalars, panel_t, own, other, runs, sort, total, ordered, products)
+
+
+def last_kernel(
+    scalars, panel_t, own, other, runs, sort, earlier, bold_own, bold_core, bold_x, bold_xcore, ahead,
+    out, total, ordered, products,
+):
+    total[...] = earlier[...]
+    lag_sums(scalars, panel_t, own, other, runs, sort, total, ordered, products)
+    rows = own.shape[0]
+    core = scalars[DELAYS]
+    v_cols = bold_own.shape[1]
+    mine = total[:, pl.ds(pl.multiple_of(core * rows, LANES), rows)].astype(BF16)
+    theirs = total[:, pl.ds(pl.multiple_of((1 - core) * rows, LANES), rows)].astype(BF16)
+    beyond = total[:, 2 * rows:2 * rows + LANES].astype(BF16)
+    for place, (a, b) in enumerate(((bold_own, bold_core), (bold_x, bold_xcore))):
+        out[:, place * v_cols:(place + 1) * v_cols] = (
+            jnp.dot(mine, a[...], preferred_element_type=F32)
+            + jnp.dot(theirs, b[...], preferred_element_type=F32)
+            + jnp.dot(
+                beyond, ahead[:, place * v_cols:(place + 1) * v_cols], preferred_element_type=F32
+            )
+        )
+
+
+def call(kernel, operands, out_shape, scratch, flops):
+    vmem = pl.BlockSpec(memory_space=pltpu.VMEM)
+    smem = pl.BlockSpec(memory_space=pltpu.SMEM)
+    return pl.pallas_call(
+        kernel,
+        out_shape=out_shape,
+        in_specs=[smem] + [vmem] * (len(operands) - 1),
+        out_specs=vmem,
+        scratch_shapes=scratch,
+        compiler_params=pltpu.CompilerParams(vmem_limit_bytes=40 * 1024 * 1024),
+        cost_estimate=pl.CostEstimate(flops=flops, bytes_accessed=8 * 1024 * 1024, transcendentals=0),
+    )(*operands)
+
+
+def exchanged(hidden, bold, panel, eigvals, ridge_grid, delays, runs):
+    t_rows, d_local = hidden.shape
+    v_cols = bold.shape[1]
+    p_cols = panel.shape[1]
+    tm_count = lax.axis_size("tm")
+    total_rows = t_rows * tm_count
+    width = d_local // tm_count
+    tm = lax.axis_index("tm")
+    chip, core = tm // 2, tm % 2
+    voxel = lax.axis_index("voxel")
+
+    panel_t = panel.T
+    late_t = swapped(panel_t, 0, 0, 2)
+
+    def columns(block):
+        return lax.dynamic_slice_in_dim(hidden, block * width, width, 1)
+
+    early_other = swapped(columns(tm ^ 1), 0, 0, 1)
+    late_other = swapped(columns(tm ^ 3), 0, 0, 1)
+    bold_x = swapped(bold, 1, 0, 0)
+    bold_core = swapped(bold, 0, 0, 1)
+    bold_xcore = swapped(bold_x, 0, 0, 1)
+    head = jnp.concatenate([
+        jnp.where(core == 0, bold[:16], bold_core[:16]),
+        jnp.where(core == 0, bold_x[:16], bold_xcore[:16]),
+    ], 1)
+    head = lax.ppermute(head, "tm", [(t, t - 2) for t in range(2, tm_count)])
+    ahead = jnp.concatenate([head, jnp.zeros((LANES - 16, 2 * v_cols), BF16)], 0)
+
+    span = 2 * t_rows
+    runs_pad = jnp.concatenate([runs, jnp.full((LANES,), -1, jnp.int32)])
+    chip_runs = lax.dynamic_slice_in_dim(runs_pad, chip * span, span + LANES)
+    chip_runs = jnp.broadcast_to(chip_runs[None], (8, span + LANES))
+    scalars = jnp.concatenate([delays, jnp.full((8,), core, jnp.int32)])
+    block = DELAYS * LANES
+    row = lax.broadcasted_iota(jnp.int32, (block, block), 0)
+    col = lax.broadcasted_iota(jnp.int32, (block, block), 1)
+    sort = ((row % DELAYS) * LANES + row // DELAYS == col).astype(BF16)
+
+    scratch = [
+        pltpu.VMEM((DELAYS * p_cols, width), BF16),
+        pltpu.VMEM((DELAYS * p_cols, span + 2 * LANES), F32),
+    ]
+    flops = 2 * DELAYS * p_cols * width * span
+    total = jax.ShapeDtypeStruct((p_cols, span + LANES), F32)
+    early = call(
+        first_kernel,
+        (scalars, panel_t, columns(tm), early_other, chip_runs, sort),
+        total, scratch, flops,
+    )
+    part = call(
+        last_kernel,
+        (scalars, late_t, columns(tm ^ 2), late_other, chip_runs, sort, early,
+         bold, bold_core, bold_x, bold_xcore, ahead),
+        jax.ShapeDtypeStruct((p_cols, 2 * v_cols), F32),
+        [pltpu.VMEM((p_cols, span + LANES), F32)] + scratch, flops,
+    )
+
+    part = part + swapped(part.astype(BF16), 0, 0, 1).astype(F32)
+    mine, theirs = part[:, :v_cols], part[:, v_cols:]
+    mine_b, theirs_b = mine.astype(BF16), theirs.astype(BF16)
+    from_y = swapped(mine_b, 0, 0, 2)
+    from_x = swapped(theirs_b, 1, 0, 0)
+    from_xy = swapped(theirs_b, 1, 0, 2)
+    near = mine + from_y.astype(F32)
+    far = from_x.astype(F32) + from_xy.astype(F32)
+    rotated = jnp.where(
+        voxel == 0, jnp.concatenate([near, far], 0), jnp.concatenate([far, near], 0)
+    )
+    rotated = rotated + swapped(rotated.astype(BF16), 0, 1, 0).astype(F32)
+    rotated = rotated + swapped(rotated.astype(BF16), 0, 2, 0).astype(F32)
+    return scaled_by(rotated, eigvals, ridge_grid, total_rows)
 
 
 def solution(mesh):
+    sizes = (mesh.shape["voxel"], mesh.shape["feature"], mesh.shape["tm"])
+    shards = exchanged if sizes == (2, 4, 4) else gathered
     return jax.shard_map(
         shards,
         mesh=mesh,

time: 168 us -> 48.1 us (0.29)
  blocking collectives: 61.2 us -> 0 us
  between operations: 33.5 us -> 0.21 us
  waiting for transfers between devices: 37.1 us -> 15.9 us
  starting transfers between devices: 1.36 us -> 14.9 us
  local copies, waits for them, and re-layouts: 15.7 us -> 4.6 us
  matrix products: 9.76 us -> 0 us
  Pallas kernels: 0 us -> 7.93 us
  other arithmetic: 8.25 us -> 4.3 us
    psum x1 -> x0, blocking collectives: 61.2 us -> none  [shards(): lax.psum(rotated_part.astype(jnp.bfloat16), ('feature', 'tm'))]
    all_gather x2 -> x0, waiting for transfers between devices: 36.4 us -> none  [the longest x1 26.9 us: shards(): panel_rows = lax.all_gather(panel, 'tm', axis=0, tiled=True)]
    ppermute x1 -> x13, waiting for transfers between devices: 0.01 us -> 15.9 us  [the longest x12 7.98 us: swapped(): return lax.ppermute(value, ('voxel', 'feature', 'tm'), pairs)]
    convert_element_type x3 -> x0, local copies, waits for them, and re-layouts: 13.7 us -> none  [the longest x2 13.7 us: shards(): partial_cov = cross.reshape(d_local * DELAYS, v_cols).astype(jnp.bfloat16)]
    ppermute x1 -> x13, starting transfers between devices: 1.28 us -> 14.9 us  [the longest x12 13.6 us: swapped(): return lax.ppermute(value, ('voxel', 'feature', 'tm'), pairs)]
    dot_general x2 -> x0, matrix products: 9.76 us -> none  [contract_rows(): lax.dot_general(left, right, (((0,), (0,)), ((), ())), preferred_element_...]
    pallas_call x0 -> x2, Pallas kernels: none -> 7.93 us  [call(): pl.pallas_call(kernel, out_shape=out_shape, in_specs=[smem] + [vmem] * (l...]
    and x2 -> x1, other arithmetic: 5.18 us -> 0.01 us  [exchanged(): sort = (row % DELAYS * LANES + row // DELAYS == col).astype(BF16)]
  transfers between devices with their start and end apart: 3 -> 13, of which waited for: 2 -> 8; matrix products, arithmetic and copies ran while one was open for 16% -> 13% of each run, Pallas kernels for 0% -> 8%
where the time goes in v1:
time: 48.1 us; the launch traced here: 47.8 us
  waiting for transfers between devices  15.9 us (33%)
  starting transfers between devices  14.9 us (31%)
  Pallas kernels  7.93 us (16%)
  local copies, waits for them, and re-layouts  4.6 us (10%)
  other arithmetic  4.3 us (9%)
    ppermute x12, starting transfers between devices, swapped(): return lax.ppermute(value, ('voxel', 'feature', 'tm'), pairs)  13.6 us
    ppermute x12, waiting for transfers between devices, swapped(): return lax.ppermute(value, ('voxel', 'feature', 'tm'), pairs)  7.98 us
    pallas_call x2, Pallas kernels, call(): pl.pallas_call(kernel, out_shape=out_shape, in_specs=[smem] + [vmem] * (l...  7.93 us
    ppermute x1, waiting for transfers between devices, exchanged(): head = lax.ppermute(head, 'tm', [(t, t - 2) for t in range(2, tm_count)])  7.93 us
    dynamic_slice x1, local copies, waits for them, and re-layouts, columns(): return lax.dynamic_slice_in_dim(hidden, block * width, width, 1)  3.34 us
    convert_element_type x1, other arithmetic, exchanged(): sort = (row % DELAYS * LANES + row // DELAYS == col).astype(BF16)  1.41 us
    convert_element_type x1, other arithmetic, scaled_by(): return scaled.astype(jnp.bfloat16)  1.36 us
    ppermute x1, starting transfers between devices, exchanged(): head = lax.ppermute(head, 'tm', [(t, t - 2) for t in range(2, tm_count)])  1.28 us
  transfers between devices with their start and end apart: 13, of which 8 were waited for; matrix products, arithmetic and copies ran while one was open for 13% of the time, Pallas kernels for 8%

profile of v1, /device:TPU:0, one launch (start us, length us, event | category | flops | bytes accessed | tf_op | source)
XLA Modules:
  0.0 47.8 jit_solution(234155931334653849)
XLA Ops:
  0.0 2.9 %collective-permute-start.4 = (bf16[768,128]{1,0:T(8,128)(2,1)}, bf16[768,128]{1,0:T(8,128)(2,1)}, u32[]{:S(2)}, u32[]{:S(2)}) collective-permute-start(bf16[768,128]{1,0:T(8,128)(2,1)} %bold_own.1), channel_id=1, source_target_pairs={{0,16},{1,17},{2,18},{3,19},{4,20},{5,21},{6,22},{7,23},{8,24},{9,... | collective-permute-start | bytes 589832 | tf_op jit(solution)/shard_map/ppermute | solution.py:76
  2.9 3.3 %constant_dynamic-slice_fusion = (bf16[768,512]{1,0:T(8,128)(2,1)}, bf16[768,512]{1,0:T(8,128)(2,1)}, bf16[768,512]{1,0:T(8,128)(2,1)S(1)}, bf16[768,512]{1,0:T(8,128)(2,1)}) fusion(bf16[768,2048]{1,0:T(8,128)(2,1)} %param.7, s32[]{:T(128)S(6)} %select_n.70, s32[]{:T(128)S(6)} %select_n.64, s32[]{:T(128)S(6)} %select_n.63, s32[]{:T(128)S(6)} %select_n.69), kind=kLoop, calls=%fused_computation.28 | loop fusion | bytes 6291472 | tf_op jit(solution)/shard_map/dynamic_slice | solution.py:181
  6.3 0.5 %collective-permute-start.2 = (bf16[768,512]{1,0:T(8,128)(2,1)}, bf16[768,512]{1,0:T(8,128)(2,1)}, u32[]{:S(2)}, u32[]{:S(2)}) collective-permute-start(bf16[768,512]{1,0:T(8,128)(2,1)} %get-tuple-element.5), channel_id=1, source_target_pairs={{0,1},{1,0},{2,3},{3,2},{4,5},{5,4},{6,7},{7,6},{8,9},{9,8},{10,11... | collective-permute-start | bytes 2359304 | tf_op jit(solution)/shard_map/ppermute | solution.py:76
  6.8 1.5 %collective-permute-start = (bf16[64,4096]{1,0:T(8,128)(2,1)}, bf16[64,4096]{1,0:T(8,128)(2,1)S(1)}, u32[]{:S(2)}, u32[]{:S(2)}) collective-permute-start(bf16[64,4096]{1,0:T(8,128)(2,1)} %bitcast.panel_t), channel_id=1, source_target_pairs={{0,2},{1,3},{2,0},{3,1},{4,6},{5,7},{6,4},{7,5},{8,10},{9,11},{10,... | collective-permute-start | bytes 1572872 | tf_op jit(solution)/shard_map/ppermute | solution.py:76
  8.3 1.4 %fusion.sort = bf16[1024,1024]{1,0:T(8,128)(2,1)S(1)} fusion(s32[1024]{0:T(1024)S(1)} %get-tuple-element.11, s32[1024]{0:T(1024)S(1)} %get-tuple-element.14, s32[1024]{0:T(1024)S(1)} %get-tuple-element.12, s32[1024]{0:T(1024)S(1)} %get-tuple-element.13, pred[1024]{0:T(1024)(128)(4,1)S(1)} %get-tuple-element.15, pred[1024]{0:T(1024)(128)(4,1)S(1)} %get-tuple-element.16), kind=kLoop, calls=%fused_computation.1 | loop fusion | flops 6291456 | bytes 2115584 | tf_op jit(solution)/shard_map/convert_element_type | solution.py:203
  9.8 0.0 copy-start.1
  9.8 0.3 collective-permute-start.5
  10.1 0.7 %slice_select_fusion.1 = bf16[16,128]{1,0:T(8,128)(2,1)S(1)} fusion(bf16[768,128]{1,0:T(8,128)(2,1)} %collective-permute-done.3.bold_core, bf16[768,128]{1,0:T(8,128)(2,1)} %bold_own.1, pred[]{:T(512)S(6)} %eq.18), kind=kLoop, calls=%fused_computation.26 | loop fusion | flops 2048 | bytes 12289 | tf_op jit(solution)/shard_map/jit(_where)/select_n | solution.py:189
  10.8 0.7 %collective-permute-done.5.bold_xcore = bf16[768,128]{1,0:T(8,128)(2,1)S(1)} collective-permute-done((bf16[768,128]{1,0:T(8,128)(2,1)}, bf16[768,128]{1,0:T(8,128)(2,1)S(1)}, u32[]{:S(2)}, u32[]{:S(2)}) %collective-permute-start.5) | collective-permute-done | bytes 196640 | tf_op jit(solution)/shard_map/ppermute | solution.py:76
  11.5 0.7 %slice_select_fusion = bf16[16,128]{1,0:T(8,128)(2,1)S(1)} fusion(bf16[768,128]{1,0:T(8,128)(2,1)S(1)} %collective-permute-done.5.bold_xcore, bf16[768,128]{1,0:T(8,128)(2,1)} %collective-permute-done.4.bold_x, pred[]{:T(512)S(6)} %eq.18), kind=kLoop, calls=%fused_computation.25 | loop fusion | flops 2048 | bytes 12289 | tf_op jit(solution)/shard_map/jit(_where)/select_n | solution.py:190
  12.2 1.3 %collective-permute-start.6 = (bf16[16,256]{1,0:T(8,128)(2,1)S(1)}, bf16[16,256]{1,0:T(8,128)(2,1)S(1)}, u32[]{:S(2)}, u32[]{:S(2)}) collective-permute-start(bf16[16,256]{1,0:T(8,128)(2,1)S(1)} %pad_maximum_fusion), channel_id=1, source_target_pairs={{2,0},{3,1},{6,4},{7,5},{10,8},{11,9},{14,12},{15,13},{18,16},{19,... | collective-permute-start | bytes 24584 | tf_op jit(solution)/shard_map/ppermute | solution.py:192
  13.5 0.1 pad_dynamic-slice_fusion
  13.6 7.9 %collective-permute-done.6 = bf16[16,256]{1,0:T(8,128)(2,1)S(1)} collective-permute-done((bf16[16,256]{1,0:T(8,128)(2,1)S(1)}, bf16[16,256]{1,0:T(8,128)(2,1)S(1)}, u32[]{:S(2)}, u32[]{:S(2)}) %collective-permute-start.6) | collective-permute-done | bytes 8224 | tf_op jit(solution)/shard_map/ppermute | solution.py:192
  21.6 1.1 %copy-done = bf16[768,512]{1,0:T(8,128)(2,1)S(1)} copy-done((bf16[768,512]{1,0:T(8,128)(2,1)S(1)}, bf16[768,512]{1,0:T(8,128)(2,1)}, u32[]{:S(2)}) %copy-start) | copy-done | bytes 786456
  22.7 3.8 %shard_map.73.earlier = f32[64,1664]{1,0:T(8,128)S(1)} custom-call(s32[16]{0:T(128)S(1)} %concatenate.18.scalars, bf16[64,4096]{1,0:T(8,128)(2,1)} %bitcast.panel_t, bf16[768,512]{1,0:T(8,128)(2,1)S(1)} %copy-done, bf16[768,512]{1,0:T(8,128)(2,1)} %collective-permute-done.2.other, s32[8,1664]{1,0:T(8,128)S(1)} %broadcast_in_dim.2.runs, ...), custom_call_target="tpu_custom_call" | custom-call | flops 805306368 | bytes 8388608 | tf_op jit(solution)/shard_map/pallas_call | solution.py:155
  26.5 0.0 copy-start.5
  26.6 0.0 copy-start.3
  26.6 4.1 %shard_map.74 = f32[64,256]{1,0:T(8,128)S(1)} custom-call(s32[16]{0:T(128)S(1)} %concatenate.18.scalars, bf16[64,4096]{1,0:T(8,128)(2,1)S(1)} %collective-permute-done.panel_t, bf16[768,512]{1,0:T(8,128)(2,1)S(1)} %get-tuple-element.7.own, bf16[768,512]{1,0:T(8,128)(2,1)} %collective-permute-done.1.other, s32[8,1664]{1,0:T(8,128)S(1)} %broadcast_in_dim.2.runs, ...), custom_call_target="tpu_custom_call" | custom-call | flops 805306368 | bytes 8388608 | tf_op jit(solution)/shard_map/pallas_call | solution.py:155
  30.7 0.1 collective-permute-start.7
  30.8 1.2 %collective-permute-done.7 = bf16[64,256]{1,0:T(8,128)(2,1)S(1)} collective-permute-done((bf16[64,256]{1,0:T(8,128)(2,1)S(1)}, bf16[64,256]{1,0:T(8,128)(2,1)S(1)}, u32[]{:S(2)}, u32[]{:S(2)}) %collective-permute-start.7) | collective-permute-done | bytes 32800 | tf_op jit(solution)/shard_map/ppermute | solution.py:76
  32.0 0.1 collective-permute-start.8
  32.1 1.8 %collective-permute-start.10 = (bf16[64,128]{1,0:T(8,128)(2,1)S(1)}, bf16[64,128]{1,0:T(8,128)(2,1)S(1)}, u32[]{:S(2)}, u32[]{:S(2)}) collective-permute-start(bf16[64,128]{1,0:T(8,128)(2,1)S(1)} %get-tuple-element.9), channel_id=1, source_target_pairs={{0,18},{1,19},{2,16},{3,17},{4,22},{5,23},{6,20},{7,21},{8,26},{9,... | collective-permute-start | bytes 49160 | tf_op jit(solution)/shard_map/ppermute | solution.py:76
  33.8 1.7 %collective-permute-start.9 = (bf16[64,128]{1,0:T(8,128)(2,1)S(1)}, bf16[64,128]{1,0:T(8,128)(2,1)S(1)}, u32[]{:S(2)}, u32[]{:S(2)}) collective-permute-start(bf16[64,128]{1,0:T(8,128)(2,1)S(1)} %get-tuple-element.9), channel_id=1, source_target_pairs={{0,16},{1,17},{2,18},{3,19},{4,20},{5,21},{6,22},{7,23},{8,24},{9,... | collective-permute-start | bytes 49160 | tf_op jit(solution)/shard_map/ppermute | solution.py:76
  35.5 0.3 collective-permute-done.8
  35.8 1.0 %collective-permute-done.10 = bf16[64,128]{1,0:T(8,128)(2,1)S(1)} collective-permute-done((bf16[64,128]{1,0:T(8,128)(2,1)S(1)}, bf16[64,128]{1,0:T(8,128)(2,1)S(1)}, u32[]{:S(2)}, u32[]{:S(2)}) %collective-permute-start.10) | collective-permute-done | bytes 16416 | tf_op jit(solution)/shard_map/ppermute | solution.py:76
  36.8 0.8 %collective-permute-done.9 = bf16[64,128]{1,0:T(8,128)(2,1)S(1)} collective-permute-done((bf16[64,128]{1,0:T(8,128)(2,1)S(1)}, bf16[64,128]{1,0:T(8,128)(2,1)S(1)}, u32[]{:S(2)}, u32[]{:S(2)}) %collective-permute-start.9) | collective-permute-done | bytes 16416 | tf_op jit(solution)/shard_map/ppermute | solution.py:76
  37.6 1.9 %collective-permute-start.11 = (bf16[128,128]{1,0:T(8,128)(2,1)S(1)}, bf16[128,128]{1,0:T(8,128)(2,1)S(1)}, u32[]{:S(2)}, u32[]{:S(2)}) collective-permute-start(bf16[128,128]{1,0:T(8,128)(2,1)S(1)} %fusion.2), channel_id=1, source_target_pairs={{0,4},{1,5},{2,6},{3,7},{4,0},{5,1},{6,2},{7,3},{8,12},{9,13},{10,... | collective-permute-start | bytes 98312 | tf_op jit(solution)/shard_map/ppermute | solution.py:76
  39.5 2.1 %collective-permute-done.11 = bf16[128,128]{1,0:T(8,128)(2,1)S(1)} collective-permute-done((bf16[128,128]{1,0:T(8,128)(2,1)S(1)}, bf16[128,128]{1,0:T(8,128)(2,1)S(1)}, u32[]{:S(2)}, u32[]{:S(2)}) %collective-permute-start.11) | collective-permute-done | bytes 32800 | tf_op jit(solution)/shard_map/ppermute | solution.py:76
  41.6 2.9 %collective-permute-start.12 = (bf16[128,128]{1,0:T(8,128)(2,1)S(1)}, bf16[128,128]{1,0:T(8,128)(2,1)S(1)}, u32[]{:S(2)}, u32[]{:S(2)}) collective-permute-start(bf16[128,128]{1,0:T(8,128)(2,1)S(1)} %fusion.1), channel_id=1, source_target_pairs={{0,8},{1,9},{2,10},{3,11},{4,12},{5,13},{6,14},{7,15},{8,0},{9,1},... | collective-permute-start | bytes 98312 | tf_op jit(solution)/shard_map/ppermute | solution.py:76
  44.5 0.1 add_multiply_fusion
  44.5 1.9 %collective-permute-done.12 = bf16[128,128]{1,0:T(8,128)(2,1)S(1)} collective-permute-done((bf16[128,128]{1,0:T(8,128)(2,1)S(1)}, bf16[128,128]{1,0:T(8,128)(2,1)S(1)}, u32[]{:S(2)}, u32[]{:S(2)}) %collective-permute-start.12) | collective-permute-done | bytes 32800 | tf_op jit(solution)/shard_map/ppermute | solution.py:76
  46.5 1.4 %divide_convert_fusion = bf16[24,128,128]{2,1,0:T(8,128)(2,1)} fusion(f32[24,128]{1,0:T(8,128)S(1)} %add_multiply_fusion, f32[128,128]{1,0:T(8,128)S(1)} %convert_add_fusion), kind=kLoop, calls=%fused_computation.2 | loop fusion | flops 786432 | bytes 864256 | tf_op jit(solution)/shard_map/convert_element_type | solution.py:35
  (31 shorter events, 0.1 us)
Async XLA Ops:
  0.0 9.8 %collective-permute-start.4 = (bf16[768,128]{1,0:T(8,128)(2,1)}, bf16[768,128]{1,0:T(8,128)(2,1)}, u32[]{:S(2)}, u32[]{:S(2)}) collective-permute-start(bf16[768,128]{1,0:T(8,128)(2,1)} %bold_own.1), channel_id=1, source_target_pairs={{0,16},{1,17},{2,18},{3,19},{4,20},{5,21},{6,22},{7,23},{8,24},{9,... | collective-permute-start | bytes 589832 | tf_op jit(solution)/shard_map/ppermute | solution.py:76
  2.9 7.2 %collective-permute-start.3 = (bf16[768,128]{1,0:T(8,128)(2,1)}, bf16[768,128]{1,0:T(8,128)(2,1)}, u32[]{:S(2)}, u32[]{:S(2)}) collective-permute-start(bf16[768,128]{1,0:T(8,128)(2,1)} %bold_own.1), channel_id=1, source_target_pairs={{0,1},{1,0},{2,3},{3,2},{4,5},{5,4},{6,7},{7,6},{8,9},{9,8},{10,11... | collective-permute-start | bytes 589832 | tf_op jit(solution)/shard_map/ppermute | solution.py:76
  2.9 10.5 %copy-start.2 = (s32[3072]{0:T(1024)S(1)}, s32[3072]{0:T(1024)}, u32[]{:S(2)}) copy-start(s32[3072]{0:T(1024)} %param.13) | copy-start | bytes 36868
  2.9 10.6 %copy-start.4 = (s32[8]{0:T(128)S(1)}, s32[8]{0:T(128)}, u32[]{:S(2)}) copy-start(s32[8]{0:T(128)} %param.12) | copy-start | bytes 100
  6.3 15.2 %collective-permute-start.2 = (bf16[768,512]{1,0:T(8,128)(2,1)}, bf16[768,512]{1,0:T(8,128)(2,1)}, u32[]{:S(2)}, u32[]{:S(2)}) collective-permute-start(bf16[768,512]{1,0:T(8,128)(2,1)} %get-tuple-element.5), channel_id=1, source_target_pairs={{0,1},{1,0},{2,3},{3,2},{4,5},{5,4},{6,7},{7,6},{8,9},{9,8},{10,11... | collective-permute-start | bytes 2359304 | tf_op jit(solution)/shard_map/ppermute | solution.py:76
  6.8 19.7 %collective-permute-start.1 = (bf16[768,512]{1,0:T(8,128)(2,1)}, bf16[768,512]{1,0:T(8,128)(2,1)}, u32[]{:S(2)}, u32[]{:S(2)}) collective-permute-start(bf16[768,512]{1,0:T(8,128)(2,1)} %get-tuple-element.6), channel_id=1, source_target_pairs={{0,1},{1,0},{2,3},{3,2},{4,5},{5,4},{6,7},{7,6},{8,9},{9,8},{10,11... | collective-permute-start | bytes 2359304 | tf_op jit(solution)/shard_map/ppermute | solution.py:76
  6.8 19.7 %collective-permute-start = (bf16[64,4096]{1,0:T(8,128)(2,1)}, bf16[64,4096]{1,0:T(8,128)(2,1)S(1)}, u32[]{:S(2)}, u32[]{:S(2)}) collective-permute-start(bf16[64,4096]{1,0:T(8,128)(2,1)} %bitcast.panel_t), channel_id=1, source_target_pairs={{0,2},{1,3},{2,0},{3,1},{4,6},{5,7},{6,4},{7,5},{8,10},{9,11},{10,... | collective-permute-start | bytes 1572872 | tf_op jit(solution)/shard_map/ppermute | solution.py:76
  9.8 16.8 %copy-start.1 = (bf16[768,128]{1,0:T(8,128)(2,1)S(1)}, bf16[768,128]{1,0:T(8,128)(2,1)}, u32[]{:S(2)}) copy-start(bf16[768,128]{1,0:T(8,128)(2,1)} %bold_own.1) | copy-start | bytes 589828
  9.8 1.7 %collective-permute-start.5 = (bf16[768,128]{1,0:T(8,128)(2,1)}, bf16[768,128]{1,0:T(8,128)(2,1)S(1)}, u32[]{:S(2)}, u32[]{:S(2)}) collective-permute-start(bf16[768,128]{1,0:T(8,128)(2,1)} %collective-permute-done.4.bold_x), channel_id=1, source_target_pairs={{0,1},{1,0},{2,3},{3,2},{4,5},{5,4},{6,7},{7,6},{8,9},{9,8},{10,11... | collective-permute-start | bytes 589832 | tf_op jit(solution)/shard_map/ppermute | solution.py:76
  12.2 9.3 %collective-permute-start.6 = (bf16[16,256]{1,0:T(8,128)(2,1)S(1)}, bf16[16,256]{1,0:T(8,128)(2,1)S(1)}, u32[]{:S(2)}, u32[]{:S(2)}) collective-permute-start(bf16[16,256]{1,0:T(8,128)(2,1)S(1)} %pad_maximum_fusion), channel_id=1, source_target_pairs={{2,0},{3,1},{6,4},{7,5},{10,8},{11,9},{14,12},{15,13},{18,16},{19,... | collective-permute-start | bytes 24584 | tf_op jit(solution)/shard_map/ppermute | solution.py:192
  21.5 1.1 %copy-start = (bf16[768,512]{1,0:T(8,128)(2,1)S(1)}, bf16[768,512]{1,0:T(8,128)(2,1)}, u32[]{:S(2)}) copy-start(bf16[768,512]{1,0:T(8,128)(2,1)} %get-tuple-element.8.own) | copy-start | bytes 2359300
  26.5 12.9 %copy-start.5 = (s32[24]{0:T(128)S(1)}, s32[24]{0:T(128)}, u32[]{:S(2)}) copy-start(s32[24]{0:T(128)} %param.11) | copy-start | bytes 292
  26.6 17.9 %copy-start.3 = (f32[128]{0:T(128)S(1)}, f32[128]{0:T(128)}, u32[]{:S(2)}) copy-start(f32[128]{0:T(128)} %param.10) | copy-start | bytes 1540
  30.7 1.3 %collective-permute-start.7 = (bf16[64,256]{1,0:T(8,128)(2,1)S(1)}, bf16[64,256]{1,0:T(8,128)(2,1)S(1)}, u32[]{:S(2)}, u32[]{:S(2)}) collective-permute-start(bf16[64,256]{1,0:T(8,128)(2,1)S(1)} %convert_element_type.43), channel_id=1, source_target_pairs={{0,1},{1,0},{2,3},{3,2},{4,5},{5,4},{6,7},{7,6},{8,9},{9,8},{10,11... | collective-permute-start | bytes 98312 | tf_op jit(solution)/shard_map/ppermute | solution.py:76
  32.0 3.8 %collective-permute-start.8 = (bf16[64,128]{1,0:T(8,128)(2,1)S(1)}, bf16[64,128]{1,0:T(8,128)(2,1)S(1)}, u32[]{:S(2)}, u32[]{:S(2)}) collective-permute-start(bf16[64,128]{1,0:T(8,128)(2,1)S(1)} %get-tuple-element.10), channel_id=1, source_target_pairs={{0,2},{1,3},{2,0},{3,1},{4,6},{5,7},{6,4},{7,5},{8,10},{9,11},{10,... | collective-permute-start | bytes 49160 | tf_op jit(solution)/shard_map/ppermute | solution.py:76
  32.1 4.7 %collective-permute-start.10 = (bf16[64,128]{1,0:T(8,128)(2,1)S(1)}, bf16[64,128]{1,0:T(8,128)(2,1)S(1)}, u32[]{:S(2)}, u32[]{:S(2)}) collective-permute-start(bf16[64,128]{1,0:T(8,128)(2,1)S(1)} %get-tuple-element.9), channel_id=1, source_target_pairs={{0,18},{1,19},{2,16},{3,17},{4,22},{5,23},{6,20},{7,21},{8,26},{9,... | collective-permute-start | bytes 49160 | tf_op jit(solution)/shard_map/ppermute | solution.py:76
  33.8 3.7 %collective-permute-start.9 = (bf16[64,128]{1,0:T(8,128)(2,1)S(1)}, bf16[64,128]{1,0:T(8,128)(2,1)S(1)}, u32[]{:S(2)}, u32[]{:S(2)}) collective-permute-start(bf16[64,128]{1,0:T(8,128)(2,1)S(1)} %get-tuple-element.9), channel_id=1, source_target_pairs={{0,16},{1,17},{2,18},{3,19},{4,20},{5,21},{6,22},{7,23},{8,24},{9,... | collective-permute-start | bytes 49160 | tf_op jit(solution)/shard_map/ppermute | solution.py:76
  37.6 4.0 %collective-permute-start.11 = (bf16[128,128]{1,0:T(8,128)(2,1)S(1)}, bf16[128,128]{1,0:T(8,128)(2,1)S(1)}, u32[]{:S(2)}, u32[]{:S(2)}) collective-permute-start(bf16[128,128]{1,0:T(8,128)(2,1)S(1)} %fusion.2), channel_id=1, source_target_pairs={{0,4},{1,5},{2,6},{3,7},{4,0},{5,1},{6,2},{7,3},{8,12},{9,13},{10,... | collective-permute-start | bytes 98312 | tf_op jit(solution)/shard_map/ppermute | solution.py:76
  41.6 4.9 %collective-permute-start.12 = (bf16[128,128]{1,0:T(8,128)(2,1)S(1)}, bf16[128,128]{1,0:T(8,128)(2,1)S(1)}, u32[]{:S(2)}, u32[]{:S(2)}) collective-permute-start(bf16[128,128]{1,0:T(8,128)(2,1)S(1)} %fusion.1), channel_id=1, source_target_pairs={{0,8},{1,9},{2,10},{3,11},{4,12},{5,13},{6,14},{7,15},{8,0},{9,1},... | collective-permute-start | bytes 98312 | tf_op jit(solution)/shard_map/ppermute | solution.py:76

commit v2 on v0

--- a/solution.py
+++ b/solution.py
@@ -3,10 +3,15 @@
 import jax
 import jax.numpy as jnp
 from jax import lax
+from jax.experimental import pallas as pl
+from jax.experimental.pallas import tpu as pltpu
 from jax.sharding import PartitionSpec as P
 
 DELAYS = 8
 MAXD = 12
+LANES = 128
+F32 = jnp.float32
+BF16 = jnp.bfloat16
 
 
 def passed_along(value, axis, steps):
@@ -21,7 +26,15 @@
     )
 
 
-def shards(hidden, bold, panel, eigvals, ridge_grid, delays, runs):
+def scaled_by(rotated, eigvals, ridge_grid, total_rows):
+    penalty = 2.0 ** ((ridge_grid.astype(jnp.float32) - 8.0) * 0.5)
+    scaled = rotated[None] / (
+        math.sqrt(total_rows) * (eigvals[None, :, None] + penalty[:, None, None])
+    )
+    return scaled.astype(jnp.bfloat16)
+
+
+def gathered(hidden, bold, panel, eigvals, ridge_grid, delays, runs):
     t_rows = hidden.shape[0]
     d_local = hidden.shape[1]
     v_cols = bold.shape[1]
@@ -47,14 +60,236 @@
         lax.all_gather(panel_rows, "voxel", axis=1, tiled=True), partial_cov
     )
     rotated = lax.psum(rotated_part.astype(jnp.bfloat16), ("feature", "tm")).astype(jnp.float32)
-    penalty = 2.0 ** ((ridge_grid.astype(jnp.float32) - 8.0) * 0.5)
-    scaled = rotated[None] / (
-        math.sqrt(total_rows) * (eigvals[None, :, None] + penalty[:, None, None])
-    )
-    return scaled.astype(jnp.bfloat16)
+    return scaled_by(rotated, eigvals, ridge_grid, total_rows)
+
+
+def swapped(value, voxel, feature, tm):
+    sizes = (lax.axis_size("voxel"), lax.axis_size("feature"), lax.axis_size("tm"))
+    pairs = []
+    for v in range(sizes[0]):
+        for f in range(sizes[1]):
+            for t in range(sizes[2]):
+                source = (v * sizes[1] + f) * sizes[2] + t
+                target = ((v ^ voxel) * sizes[1] + (f ^ feature)) * sizes[2] + (t ^ tm)
+                pairs.append((source, target))
+    return lax.ppermute(value, ("voxel", "feature", "tm"), pairs)
+
+
+def sorted_by_slot(panel_t, sort, groups):
+    rows = panel_t.shape[0]
+    block = DELAYS * LANES
+    stacked = jnp.concatenate([panel_t[:, g * block:(g + 1) * block] for g in range(groups)], 0)
+    mixed = jnp.dot(stacked, sort[...], preferred_element_type=F32).astype(BF16)
+    return [
+        (k, g, mixed[g * rows:(g + 1) * rows, k * LANES:(k + 1) * LANES])
+        for g in range(groups) for k in range(DELAYS)
+    ]
+
+
+def lag_sums(scalars, runs, products, total):
+    p_cols = total.shape[0]
+    tiles = products.shape[1] // LANES
+    lane = lax.broadcasted_iota(jnp.int32, (8, LANES), 1)
+    here = runs[...]
+    kept = [(pltpu.roll(here, scalars[k], 1) == here).astype(F32) for k in range(DELAYS)]
+    for row in range(0, p_cols, 8):
+        sums = [total[row:row + 8, j * LANES:(j + 1) * LANES] for j in range(tiles)]
+        for k in range(DELAYS):
+            low = lane < scalars[k]
+            before = jnp.zeros((8, LANES), F32)
+            at = k * p_cols + row
+            for j in range(tiles):
+                if j < tiles - 1:
+                    now = pltpu.roll(
+                        products[at:at + 8, j * LANES:(j + 1) * LANES], scalars[k], 1
+                    )
+                    moved = jnp.where(low, before, now)
+                    before = now
+                else:
+                    moved = jnp.where(low, before, 0.0)
+                sums[j] = sums[j] + moved * kept[k][:, j * LANES:(j + 1) * LANES]
+        for j in range(tiles):
+            total[row:row + 8, j * LANES:(j + 1) * LANES] = sums[j]
+
+
+def sort_into(ordered, panel_t, sort):
+    rows = panel_t.shape[0]
+    for k, g, tile in sorted_by_slot(panel_t, sort, ordered.shape[1] // LANES):
+        ordered[k * rows:(k + 1) * rows, g * LANES:(g + 1) * LANES] = tile
+
+
+def product(ordered, hidden):
+    return lax.dot_general(
+        ordered[...], hidden[...], (((1,), (1,)), ((), ())), preferred_element_type=F32
+    )
+
+
+def feature_copy(hidden, block, target, sem):
+    width = target.shape[1]
+    return pltpu.make_async_copy(
+        hidden.at[:, pl.ds(pl.multiple_of(block * width, width), width)], target, sem
+    )
+
+
+def early_kernel(
+    scalars, panel_t, panel_core, hidden, runs, total, sort, products, ordered, loaded, hidden_own, hidden_core, sems,
+):
+    rows = hidden.shape[0]
+    tm = scalars[DELAYS]
+    copies = [
+        pltpu.make_async_copy(panel_t, loaded, sems.at[0]),
+        feature_copy(hidden, tm, hidden_own, sems.at[1]),
+        feature_copy(hidden, tm ^ 1, hidden_core, sems.at[2]),
+    ]
+    for copy in copies:
+        copy.start()
+    block = DELAYS * LANES
+    gap = lax.broadcasted_iota(jnp.int32, (block, LANES), 0) - DELAYS * lax.broadcasted_iota(
+        jnp.int32, (block, LANES), 1
+    )
+    for k in range(DELAYS):
+        sort[:, k * LANES:(k + 1) * LANES] = (gap == k).astype(F32).astype(BF16)
+    total[...] = jnp.zeros_like(total)
+    copies[0].wait()
+    sort_into(ordered, loaded[...], sort)
+    copies[1].wait()
+    products[:, :rows] = product(ordered, hidden_own)
+    sort_into(ordered, panel_core[...], sort)
+    copies[2].wait()
+    products[:, :rows] += product(ordered, hidden_core)
+    lag_sums(scalars, runs, products, total)
+
+
+def own_kernel(panel_t, sort, hidden_own, products, ordered):
+    sort_into(ordered, panel_t[...], sort)
+    products[...] = product(ordered, hidden_own)
+
+
+def late_kernel(
+    scalars, panel_t, sort, hidden_core, own, runs, earlier, bold, bold_x, ahead, out, ordered, products, total,
+):
+    rows = hidden_core.shape[0]
+    v_cols = bold.shape[1]
+    total[...] = earlier[...]
+    sort_into(ordered, panel_t[...], sort)
+    products[:, :rows] = own[...] + product(ordered, hidden_core)
+    lag_sums(scalars, runs, products, total)
+    mine = total[:, :rows].astype(BF16)
+    beyond = total[:, rows:].astype(BF16)
+    blank = jnp.zeros((LANES - ahead.shape[0], v_cols), BF16)
+    for place, part in enumerate((bold, bold_x)):
+        out[:, place * v_cols:(place + 1) * v_cols] = jnp.dot(
+            mine, part[...], preferred_element_type=F32
+        ) + jnp.dot(
+            beyond,
+            jnp.concatenate([ahead[:, place * v_cols:(place + 1) * v_cols], blank], 0),
+            preferred_element_type=F32,
+        )
+
+
+def head_kernel(bold, bold_x, head):
+    v_cols = bold.shape[1]
+    head[:, :v_cols] = bold[:16, :]
+    head[:, v_cols:] = bold_x[:16, :]
+
+
+def call(kernel, operands, out_shape, scratch, outside=()):
+    hbm = pl.BlockSpec(memory_space=pltpu.HBM)
+    operands = [
+        pltpu.with_memory_space_constraint(operand, pltpu.HBM) if n in outside else operand
+        for n, operand in enumerate(operands)
+    ]
+    vmem = pl.BlockSpec(memory_space=pltpu.VMEM)
+    smem = pl.BlockSpec(memory_space=pltpu.SMEM)
+    return pl.pallas_call(
+        kernel,
+        out_shape=out_shape,
+        in_specs=[
+            smem if operand.ndim == 1 else hbm if n in outside else vmem
+            for n, operand in enumerate(operands)
+        ],
+        out_specs=jax.tree.map(lambda _: vmem, out_shape),
+        scratch_shapes=scratch,
+        compiler_params=pltpu.CompilerParams(vmem_limit_bytes=12 * 1024 * 1024),
+        cost_estimate=pl.CostEstimate(flops=1024, bytes_accessed=1024, transcendentals=0),
+    )(*operands)
+
+
+def after(value, done):
+    return lax.optimization_barrier((value, done))[0]
+
+
+def exchanged(hidden, bold, panel, eigvals, ridge_grid, delays, runs):
+    t_rows, d_local = hidden.shape
+    v_cols = bold.shape[1]
+    p_cols = panel.shape[1]
+    tm_count = lax.axis_size("tm")
+    total_rows = t_rows * tm_count
+    width = d_local // tm_count
+    block = DELAYS * LANES
+    tm = lax.axis_index("tm")
+    voxel = lax.axis_index("voxel")
+    reach = t_rows + LANES
+    dma = pltpu.SemaphoreType.DMA
+    scalars = jnp.concatenate([delays, jnp.full((8,), tm, jnp.int32)])
+
+    panel_t = panel.T
+    late_t = swapped(panel_t, 0, 0, 2)
+
+    bold_x = swapped(bold, 1, 0, 0)
+
+    runs_pad = jnp.concatenate([runs, jnp.full((LANES,), -1, jnp.int32)])
+    own_runs = lax.dynamic_slice_in_dim(runs_pad, tm * t_rows, reach)
+    own_runs = jnp.broadcast_to(own_runs[None], (8, reach))
+    panel_core = swapped(panel_t, 0, 0, 1)
+    features = pltpu.VMEM((t_rows, width), BF16)
+    ordered = pltpu.VMEM((DELAYS * p_cols, width), BF16)
+    products = pltpu.VMEM((DELAYS * p_cols, reach), F32)
+    earlier, sort = call(
+        early_kernel, (scalars, panel_t, panel_core, hidden, own_runs),
+        (jax.ShapeDtypeStruct((p_cols, reach), F32), jax.ShapeDtypeStruct((block, block), BF16)),
+        [products, ordered, pltpu.VMEM(panel_t.shape, BF16), features, features, dma((3,))], (1, 3),
+    )
+    head = call(
+        head_kernel, (bold, after(bold_x, earlier)),
+        jax.ShapeDtypeStruct((16, 2 * v_cols), BF16), [],
+    )
+    ahead = passed_along(head, "tm", -1)
+    hidden_late = after(hidden, head)
+    hidden_own = lax.dynamic_slice_in_dim(hidden_late, (tm ^ 2) * width, width, 1)
+    hidden_core = lax.dynamic_slice_in_dim(hidden_late, (tm ^ 3) * width, width, 1)
+    late_t = after(late_t, (ahead, hidden_own, hidden_core))
+    late_core = swapped(late_t, 0, 0, 1)
+    own = call(
+        own_kernel, (late_t, sort, hidden_own),
+        jax.ShapeDtypeStruct((DELAYS * p_cols, t_rows), F32), [ordered],
+    )
+    part = call(
+        late_kernel,
+        (scalars, after(late_core, own), sort, hidden_core, own, own_runs, earlier, bold, bold_x, ahead),
+        jax.ShapeDtypeStruct((p_cols, 2 * v_cols), F32),
+        [ordered, products, pltpu.VMEM((p_cols, reach), F32)],
+    )
+
+    part = part + swapped(part.astype(BF16), 0, 0, 1).astype(F32)
+    mine, theirs = part[:, :v_cols], part[:, v_cols:]
+    mine_b, theirs_b = mine.astype(BF16), theirs.astype(BF16)
+    from_y = swapped(mine_b, 0, 0, 2)
+    from_x = swapped(theirs_b, 1, 0, 0)
+    from_xy = swapped(theirs_b, 1, 0, 2)
+    near = mine + from_y.astype(F32)
+    far = from_x.astype(F32) + from_xy.astype(F32)
+    rotated = jnp.where(
+        voxel == 0, jnp.concatenate([near, far], 0), jnp.concatenate([far, near], 0)
+    )
+    rotated = rotated + swapped(rotated.astype(BF16), 0, 1, 0).astype(F32)
+    rotated = rotated + swapped(rotated.astype(BF16), 0, 2, 0).astype(F32)
+    return scaled_by(rotated, eigvals, ridge_grid, total_rows)
 
 
 def solution(mesh):
+    sizes = (mesh.shape["voxel"], mesh.shape["feature"], mesh.shape["tm"])
+    shards = exchanged if sizes == (2, 4, 4) else gathered
     return jax.shard_map(
         shards,
         mesh=mesh,

time: 168 us -> 39.6 us (0.24)
  blocking collectives: 61.2 us -> 0 us
  between operations: 33.5 us -> 0.14 us
  waiting for transfers between devices: 37.1 us -> 14 us
  local copies, waits for them, and re-layouts: 15.7 us -> 1.64 us
  starting transfers between devices: 1.36 us -> 14 us
  matrix products: 9.76 us -> 0 us
  Pallas kernels: 0 us -> 8.15 us
  other arithmetic: 8.25 us -> 1.5 us
    psum x1 -> x0, blocking collectives: 61.2 us -> none  [shards(): lax.psum(rotated_part.astype(jnp.bfloat16), ('feature', 'tm'))]
    all_gather x2 -> x0, waiting for transfers between devices: 36.4 us -> none  [the longest x1 26.9 us: shards(): panel_rows = lax.all_gather(panel, 'tm', axis=0, tiled=True)]
    ppermute x0 -> x10, waiting for transfers between devices: none -> 13.9 us  [swapped(): return lax.ppermute(value, ('voxel', 'feature', 'tm'), pairs)]
    convert_element_type x3 -> x0, local copies, waits for them, and re-layouts: 13.7 us -> none  [the longest x2 13.7 us: shards(): partial_cov = cross.reshape(d_local * DELAYS, v_cols).astype(jnp.bfloat16)]
    ppermute x0 -> x10, starting transfers between devices: none -> 12.7 us  [swapped(): return lax.ppermute(value, ('voxel', 'feature', 'tm'), pairs)]
    dot_general x2 -> x0, matrix products: 9.76 us -> none  [contract_rows(): lax.dot_general(left, right, (((0,), (0,)), ((), ())), preferred_element_...]
    pallas_call x0 -> x4, Pallas kernels: none -> 8.15 us  [call(): pl.pallas_call(kernel, out_shape=out_shape, in_specs=[smem if operand.ndi...]
    and x2 -> x0, other arithmetic: 5.18 us -> none  [shards(): valid = (positions + offset < total_rows) & (target_runs == own_runs)]
  transfers between devices with their start and end apart: 3 -> 11, of which waited for: 2 -> 8; matrix products, arithmetic and copies ran while one was open for 16% -> 4% of each run, Pallas kernels for 0% -> 15%
where the time goes in v2:
time: 39.6 us; the launch traced here: 39.4 us
  starting transfers between devices  14 us (35%)
  waiting for transfers between devices  14 us (35%)
  Pallas kernels  8.15 us (21%)
  local copies, waits for them, and re-layouts  1.64 us (4%)
  other arithmetic  1.5 us (4%)
    ppermute x10, waiting for transfers between devices, swapped(): return lax.ppermute(value, ('voxel', 'feature', 'tm'), pairs)  13.9 us
    ppermute x10, starting transfers between devices, swapped(): return lax.ppermute(value, ('voxel', 'feature', 'tm'), pairs)  12.7 us
    pallas_call x4, Pallas kernels, call(): pl.pallas_call(kernel, out_shape=out_shape, in_specs=[smem if operand.ndi...  8.15 us
    convert_element_type x1, other arithmetic, scaled_by(): return scaled.astype(jnp.bfloat16)  1.36 us
    ppermute x1, starting transfers between devices, passed_along(): lax.ppermute(value, axis, [(source, source + steps) for source in range(f...  1.29 us
  transfers between devices with their start and end apart: 11, of which 8 were waited for; matrix products, arithmetic and copies ran while one was open for 4% of the time, Pallas kernels for 15%

profile of v2, /device:TPU:0, one launch (start us, length us, event | category | flops | bytes accessed | tf_op | source)
XLA Modules:
  0.0 39.4 jit_solution(17895611558993654202)
XLA Ops:
  0.0 0.5 %collective-permute-start.2 = (bf16[64,4096]{1,0:T(8,128)(2,1)}, bf16[64,4096]{1,0:T(8,128)(2,1)S(1)}, u32[]{:S(2)}, u32[]{:S(2)}) collective-permute-start(bf16[64,4096]{1,0:T(8,128)(2,1)} %bitcast.1), channel_id=1, source_target_pairs={{0,1},{1,0},{2,3},{3,2},{4,5},{5,4},{6,7},{7,6},{8,9},{9,8},{10,11... | collective-permute-start | bytes 1572872 | tf_op jit(solution)/shard_map/ppermute | solution.py:75
  0.5 2.5 %collective-permute-start = (bf16[64,4096]{1,0:T(8,128)(2,1)}, bf16[64,4096]{1,0:T(8,128)(2,1)S(1)}, u32[]{:S(2)}, u32[]{:S(2)}) collective-permute-start(bf16[64,4096]{1,0:T(8,128)(2,1)} %bitcast.2), channel_id=1, source_target_pairs={{0,2},{1,3},{2,0},{3,1},{4,6},{5,7},{6,4},{7,5},{8,10},{9,11},{10,... | collective-permute-start | bytes 1572872 | tf_op jit(solution)/shard_map/ppermute | solution.py:75
  3.0 1.5 %collective-permute-start.1 = (bf16[768,128]{1,0:T(8,128)(2,1)}, bf16[768,128]{1,0:T(8,128)(2,1)S(1)}, u32[]{:S(2)}, u32[]{:S(2)}) collective-permute-start(bf16[768,128]{1,0:T(8,128)(2,1)} %bold.3), channel_id=1, source_target_pairs={{0,16},{1,17},{2,18},{3,19},{4,20},{5,21},{6,22},{7,23},{8,24},{9,... | collective-permute-start | bytes 589832 | tf_op jit(solution)/shard_map/ppermute | solution.py:75
  4.5 0.7 %concatenate.12.scalars = s32[16]{0:T(128)S(1)} pad(s32[8]{0:T(128)} %param.12, s32[]{:T(128)S(6)} %axis_index.25), padding=0_8 | pad | bytes 100 | tf_op jit(solution)/shard_map/concatenate | solution.py:234
  5.1 0.8 %pad_dynamic-slice_fusion = s32[896]{0:T(1024)S(1)} fusion(s32[]{:T(128)S(6)} %select_n.18, s32[3072]{0:T(1024)} %param.13), kind=kLoop, calls=%fused_computation.10 | loop fusion | bytes 15876 | tf_op jit(solution)/shard_map/dynamic_slice | solution.py:242
  5.9 0.0 collective-permute-done.2.panel_core
  5.9 0.0 copy-start.1
  5.9 4.8 %shard_map.73 = (f32[64,896]{1,0:T(8,128)S(1)}, bf16[1024,1024]{1,0:T(8,128)(2,1)S(1)}) custom-call(s32[16]{0:T(128)S(1)} %concatenate.12.scalars, bf16[64,4096]{1,0:T(8,128)(2,1)} %bitcast.3, bf16[64,4096]{1,0:T(8,128)(2,1)S(1)} %collective-permute-done.2.panel_core, bf16[768,2048]{1,0:T(8,128)(2,1)} %hidden.1, s32[8,896]{1,0:T(8,128)S(1)} %broadcast_in_dim.2.runs), custom_call_target="tpu_custom_call" | custom-call | flops 1024 | bytes 1024 | tf_op jit(solution)/shard_map/pallas_call | solution.py:204
  10.7 0.0 collective-permute-done.1.bold_x
  10.7 1.3 %collective-permute-start.3 = (bf16[16,256]{1,0:T(8,128)(2,1)S(1)}, bf16[16,256]{1,0:T(8,128)(2,1)S(1)}, u32[]{:S(2)}, u32[]{:S(2)}) collective-permute-start(bf16[16,256]{1,0:T(8,128)(2,1)S(1)} %shard_map.74), channel_id=1, source_target_pairs={{1,0},{2,1},{3,2},{5,4},{6,5},{7,6},{9,8},{10,9},{11,10},{13,12},{... | collective-permute-start | bytes 24584 | tf_op jit(solution)/shard_map/ppermute | solution.py:20
  12.0 0.2 constant_dynamic-slice_fusion
  12.2 3.5 %collective-permute-done.panel_t = bf16[64,4096]{1,0:T(8,128)(2,1)S(1)} collective-permute-done((bf16[64,4096]{1,0:T(8,128)(2,1)}, bf16[64,4096]{1,0:T(8,128)(2,1)S(1)}, u32[]{:S(2)}, u32[]{:S(2)}) %collective-permute-start) | collective-permute-done | bytes 524320 | tf_op jit(solution)/shard_map/ppermute | solution.py:75
  15.8 0.1 collective-permute-start.4
  15.9 1.2 %shard_map.75.own = f32[512,768]{1,0:T(8,128)S(1)} custom-call(bf16[64,4096]{1,0:T(8,128)(2,1)S(1)} %collective-permute-done.panel_t, bf16[1024,1024]{1,0:T(8,128)(2,1)S(1)} %get-tuple-element.15.sort, bf16[768,512]{1,0:T(8,128)(2,1)S(1)} %get-tuple-element.18.hidden_own), custom_call_target="tpu_custom_call" | custom-call | flops 1024 | bytes 1024 | tf_op jit(solution)/shard_map/pallas_call | solution.py:204
  17.1 0.0 copy-start.3
  17.1 0.0 copy-start.2
  17.1 0.6 %collective-permute-done.4.panel_t = bf16[64,4096]{1,0:T(8,128)(2,1)S(1)} collective-permute-done((bf16[64,4096]{1,0:T(8,128)(2,1)S(1)}, bf16[64,4096]{1,0:T(8,128)(2,1)S(1)}, u32[]{:S(2)}, u32[]{:S(2)}) %collective-permute-start.4) | collective-permute-done | bytes 524320 | tf_op jit(solution)/shard_map/ppermute | solution.py:75
  17.7 2.2 %shard_map.76 = f32[64,256]{1,0:T(8,128)S(1)} custom-call(s32[16]{0:T(128)S(1)} %concatenate.12.scalars, bf16[64,4096]{1,0:T(8,128)(2,1)S(1)} %collective-permute-done.4.panel_t, bf16[1024,1024]{1,0:T(8,128)(2,1)S(1)} %get-tuple-element.15.sort, bf16[768,512]{1,0:T(8,128)(2,1)S(1)} %get-tuple-element.17.hidden_core, f32[512,768]{1,0:T(8,128)S(1)} %shard_map.75.own, ...), custom_call_target="tpu_custom_call" | custom-call | flops 1024 | bytes 1024 | tf_op jit(solution)/shard_map/pallas_call | solution.py:204
  19.9 0.2 collective-permute-start.5
  20.1 1.1 %collective-permute-done.5 = bf16[64,256]{1,0:T(8,128)(2,1)S(1)} collective-permute-done((bf16[64,256]{1,0:T(8,128)(2,1)S(1)}, bf16[64,256]{1,0:T(8,128)(2,1)S(1)}, u32[]{:S(2)}, u32[]{:S(2)}) %collective-permute-start.5) | collective-permute-done | bytes 32800 | tf_op jit(solution)/shard_map/ppermute | solution.py:75
  21.2 1.8 %collective-permute-start.6 = (bf16[64,128]{1,0:T(8,128)(2,1)S(1)}, bf16[64,128]{1,0:T(8,128)(2,1)S(1)}, u32[]{:S(2)}, u32[]{:S(2)}) collective-permute-start(bf16[64,128]{1,0:T(8,128)(2,1)S(1)} %get-tuple-element.20), channel_id=1, source_target_pairs={{0,2},{1,3},{2,0},{3,1},{4,6},{5,7},{6,4},{7,5},{8,10},{9,11},{10,... | collective-permute-start | bytes 49160 | tf_op jit(solution)/shard_map/ppermute | solution.py:75
  23.0 1.5 %collective-permute-start.7 = (bf16[64,128]{1,0:T(8,128)(2,1)S(1)}, bf16[64,128]{1,0:T(8,128)(2,1)S(1)}, u32[]{:S(2)}, u32[]{:S(2)}) collective-permute-start(bf16[64,128]{1,0:T(8,128)(2,1)S(1)} %get-tuple-element.19), channel_id=1, source_target_pairs={{0,16},{1,17},{2,18},{3,19},{4,20},{5,21},{6,22},{7,23},{8,24},{9,... | collective-permute-start | bytes 49160 | tf_op jit(solution)/shard_map/ppermute | solution.py:75
  24.5 0.3 collective-permute-start.8
  24.8 0.2 collective-permute-done.6
  25.0 1.8 %collective-permute-done.7 = bf16[64,128]{1,0:T(8,128)(2,1)S(1)} collective-permute-done((bf16[64,128]{1,0:T(8,128)(2,1)S(1)}, bf16[64,128]{1,0:T(8,128)(2,1)S(1)}, u32[]{:S(2)}, u32[]{:S(2)}) %collective-permute-start.7) | collective-permute-done | bytes 16416 | tf_op jit(solution)/shard_map/ppermute | solution.py:75
  26.9 2.3 %collective-permute-done.8 = bf16[64,128]{1,0:T(8,128)(2,1)S(1)} collective-permute-done((bf16[64,128]{1,0:T(8,128)(2,1)S(1)}, bf16[64,128]{1,0:T(8,128)(2,1)S(1)}, u32[]{:S(2)}, u32[]{:S(2)}) %collective-permute-start.8) | collective-permute-done | bytes 16416 | tf_op jit(solution)/shard_map/ppermute | solution.py:75
  29.2 1.6 %collective-permute-start.9 = (bf16[128,128]{1,0:T(8,128)(2,1)S(1)}, bf16[128,128]{1,0:T(8,128)(2,1)S(1)}, u32[]{:S(2)}, u32[]{:S(2)}) collective-permute-start(bf16[128,128]{1,0:T(8,128)(2,1)S(1)} %fusion.1), channel_id=1, source_target_pairs={{0,4},{1,5},{2,6},{3,7},{4,0},{5,1},{6,2},{7,3},{8,12},{9,13},{10,... | collective-permute-start | bytes 98312 | tf_op jit(solution)/shard_map/ppermute | solution.py:75
  30.8 2.3 %collective-permute-done.9 = bf16[128,128]{1,0:T(8,128)(2,1)S(1)} collective-permute-done((bf16[128,128]{1,0:T(8,128)(2,1)S(1)}, bf16[128,128]{1,0:T(8,128)(2,1)S(1)}, u32[]{:S(2)}, u32[]{:S(2)}) %collective-permute-start.9) | collective-permute-done | bytes 32800 | tf_op jit(solution)/shard_map/ppermute | solution.py:75
  33.2 2.8 %collective-permute-start.10 = (bf16[128,128]{1,0:T(8,128)(2,1)S(1)}, bf16[128,128]{1,0:T(8,128)(2,1)S(1)}, u32[]{:S(2)}, u32[]{:S(2)}) collective-permute-start(bf16[128,128]{1,0:T(8,128)(2,1)S(1)} %fusion), channel_id=1, source_target_pairs={{0,8},{1,9},{2,10},{3,11},{4,12},{5,13},{6,14},{7,15},{8,0},{9,1},... | collective-permute-start | bytes 98312 | tf_op jit(solution)/shard_map/ppermute | solution.py:75
  35.9 0.1 add_multiply_fusion
  36.0 2.0 %collective-permute-done.10 = bf16[128,128]{1,0:T(8,128)(2,1)S(1)} collective-permute-done((bf16[128,128]{1,0:T(8,128)(2,1)S(1)}, bf16[128,128]{1,0:T(8,128)(2,1)S(1)}, u32[]{:S(2)}, u32[]{:S(2)}) %collective-permute-start.10) | collective-permute-done | bytes 32800 | tf_op jit(solution)/shard_map/ppermute | solution.py:75
  38.1 1.4 %divide_convert_fusion = bf16[24,128,128]{2,1,0:T(8,128)(2,1)} fusion(f32[24,128]{1,0:T(8,128)S(1)} %add_multiply_fusion, f32[128,128]{1,0:T(8,128)S(1)} %convert_add_fusion), kind=kLoop, calls=%fused_computation | loop fusion | flops 786432 | bytes 864256 | tf_op jit(solution)/shard_map/convert_element_type | solution.py:34
  (17 shorter events, 0.1 us)
Async XLA Ops:
  0.0 5.9 %collective-permute-start.2 = (bf16[64,4096]{1,0:T(8,128)(2,1)}, bf16[64,4096]{1,0:T(8,128)(2,1)S(1)}, u32[]{:S(2)}, u32[]{:S(2)}) collective-permute-start(bf16[64,4096]{1,0:T(8,128)(2,1)} %bitcast.1), channel_id=1, source_target_pairs={{0,1},{1,0},{2,3},{3,2},{4,5},{5,4},{6,7},{7,6},{8,9},{9,8},{10,11... | collective-permute-start | bytes 1572872 | tf_op jit(solution)/shard_map/ppermute | solution.py:75
  0.5 15.3 %collective-permute-start = (bf16[64,4096]{1,0:T(8,128)(2,1)}, bf16[64,4096]{1,0:T(8,128)(2,1)S(1)}, u32[]{:S(2)}, u32[]{:S(2)}) collective-permute-start(bf16[64,4096]{1,0:T(8,128)(2,1)} %bitcast.2), channel_id=1, source_target_pairs={{0,2},{1,3},{2,0},{3,1},{4,6},{5,7},{6,4},{7,5},{8,10},{9,11},{10,... | collective-permute-start | bytes 1572872 | tf_op jit(solution)/shard_map/ppermute | solution.py:75
  3.0 7.7 %collective-permute-start.1 = (bf16[768,128]{1,0:T(8,128)(2,1)}, bf16[768,128]{1,0:T(8,128)(2,1)S(1)}, u32[]{:S(2)}, u32[]{:S(2)}) collective-permute-start(bf16[768,128]{1,0:T(8,128)(2,1)} %bold.3), channel_id=1, source_target_pairs={{0,16},{1,17},{2,18},{3,19},{4,20},{5,21},{6,22},{7,23},{8,24},{9,... | collective-permute-start | bytes 589832 | tf_op jit(solution)/shard_map/ppermute | solution.py:75
  5.9 4.8 %copy-start = (bf16[768,128]{1,0:T(8,128)(2,1)S(1)}, bf16[768,128]{1,0:T(8,128)(2,1)}, u32[]{:S(2)}) copy-start(bf16[768,128]{1,0:T(8,128)(2,1)} %bold.3) | copy-start | bytes 589828
  5.9 6.1 %copy-start.1 = (bf16[768,2048]{1,0:T(8,128)(2,1)S(1)}, bf16[768,2048]{1,0:T(8,128)(2,1)}, u32[]{:S(2)}) copy-start(bf16[768,2048]{1,0:T(8,128)(2,1)} %hidden.1) | copy-start | bytes 9437188
  10.7 5.0 %collective-permute-start.3 = (bf16[16,256]{1,0:T(8,128)(2,1)S(1)}, bf16[16,256]{1,0:T(8,128)(2,1)S(1)}, u32[]{:S(2)}, u32[]{:S(2)}) collective-permute-start(bf16[16,256]{1,0:T(8,128)(2,1)S(1)} %shard_map.74), channel_id=1, source_target_pairs={{1,0},{2,1},{3,2},{5,4},{6,5},{7,6},{9,8},{10,9},{11,10},{13,12},{... | collective-permute-start | bytes 24584 | tf_op jit(solution)/shard_map/ppermute | solution.py:20
  15.8 1.9 %collective-permute-start.4 = (bf16[64,4096]{1,0:T(8,128)(2,1)S(1)}, bf16[64,4096]{1,0:T(8,128)(2,1)S(1)}, u32[]{:S(2)}, u32[]{:S(2)}) collective-permute-start(bf16[64,4096]{1,0:T(8,128)(2,1)S(1)} %collective-permute-done.panel_t), channel_id=1, source_target_pairs={{0,1},{1,0},{2,3},{3,2},{4,5},{5,4},{6,7},{7,6},{8,9},{9,8},{10,11... | collective-permute-start | bytes 1572872 | tf_op jit(solution)/shard_map/ppermute | solution.py:75
  17.1 13.7 %copy-start.3 = (s32[24]{0:T(128)S(1)}, s32[24]{0:T(128)}, u32[]{:S(2)}) copy-start(s32[24]{0:T(128)} %param.11) | copy-start | bytes 292
  17.1 18.9 %copy-start.2 = (f32[128]{0:T(128)S(1)}, f32[128]{0:T(128)}, u32[]{:S(2)}) copy-start(f32[128]{0:T(128)} %param.10) | copy-start | bytes 1540
  19.9 1.3 %collective-permute-start.5 = (bf16[64,256]{1,0:T(8,128)(2,1)S(1)}, bf16[64,256]{1,0:T(8,128)(2,1)S(1)}, u32[]{:S(2)}, u32[]{:S(2)}) collective-permute-start(bf16[64,256]{1,0:T(8,128)(2,1)S(1)} %convert_element_type.37), channel_id=1, source_target_pairs={{0,1},{1,0},{2,3},{3,2},{4,5},{5,4},{6,7},{7,6},{8,9},{9,8},{10,11... | collective-permute-start | bytes 98312 | tf_op jit(solution)/shard_map/ppermute | solution.py:75
  21.2 3.8 %collective-permute-start.6 = (bf16[64,128]{1,0:T(8,128)(2,1)S(1)}, bf16[64,128]{1,0:T(8,128)(2,1)S(1)}, u32[]{:S(2)}, u32[]{:S(2)}) collective-permute-start(bf16[64,128]{1,0:T(8,128)(2,1)S(1)} %get-tuple-element.20), channel_id=1, source_target_pairs={{0,2},{1,3},{2,0},{3,1},{4,6},{5,7},{6,4},{7,5},{8,10},{9,11},{10,... | collective-permute-start | bytes 49160 | tf_op jit(solution)/shard_map/ppermute | solution.py:75
  23.0 3.8 %collective-permute-start.7 = (bf16[64,128]{1,0:T(8,128)(2,1)S(1)}, bf16[64,128]{1,0:T(8,128)(2,1)S(1)}, u32[]{:S(2)}, u32[]{:S(2)}) collective-permute-start(bf16[64,128]{1,0:T(8,128)(2,1)S(1)} %get-tuple-element.19), channel_id=1, source_target_pairs={{0,16},{1,17},{2,18},{3,19},{4,20},{5,21},{6,22},{7,23},{8,24},{9,... | collective-permute-start | bytes 49160 | tf_op jit(solution)/shard_map/ppermute | solution.py:75
  24.5 4.6 %collective-permute-start.8 = (bf16[64,128]{1,0:T(8,128)(2,1)S(1)}, bf16[64,128]{1,0:T(8,128)(2,1)S(1)}, u32[]{:S(2)}, u32[]{:S(2)}) collective-permute-start(bf16[64,128]{1,0:T(8,128)(2,1)S(1)} %get-tuple-element.19), channel_id=1, source_target_pairs={{0,18},{1,19},{2,16},{3,17},{4,22},{5,23},{6,20},{7,21},{8,26},{9,... | collective-permute-start | bytes 49160 | tf_op jit(solution)/shard_map/ppermute | solution.py:75
  29.2 4.0 %collective-permute-start.9 = (bf16[128,128]{1,0:T(8,128)(2,1)S(1)}, bf16[128,128]{1,0:T(8,128)(2,1)S(1)}, u32[]{:S(2)}, u32[]{:S(2)}) collective-permute-start(bf16[128,128]{1,0:T(8,128)(2,1)S(1)} %fusion.1), channel_id=1, source_target_pairs={{0,4},{1,5},{2,6},{3,7},{4,0},{5,1},{6,2},{7,3},{8,12},{9,13},{10,... | collective-permute-start | bytes 98312 | tf_op jit(solution)/shard_map/ppermute | solution.py:75
  33.2 4.9 %collective-permute-start.10 = (bf16[128,128]{1,0:T(8,128)(2,1)S(1)}, bf16[128,128]{1,0:T(8,128)(2,1)S(1)}, u32[]{:S(2)}, u32[]{:S(2)}) collective-permute-start(bf16[128,128]{1,0:T(8,128)(2,1)S(1)} %fusion), channel_id=1, source_target_pairs={{0,8},{1,9},{2,10},{3,11},{4,12},{5,13},{6,14},{7,15},{8,0},{9,1},... | collective-permute-start | bytes 98312 | tf_op jit(solution)/shard_map/ppermute | solution.py:75

commit v3 on v2

v3 whole, which is shorter than its diff:
```python
import math

import jax
import jax.numpy as jnp
from jax import lax
from jax.experimental import pallas as pl
from jax.experimental.pallas import tpu as pltpu
from jax.sharding import PartitionSpec as P

DELAYS = 8
MAXD = 12
LANES = 128
F32 = jnp.float32
BF16 = jnp.bfloat16


def passed_along(value, axis, steps):
    count = lax.axis_size(axis)
    first, last = (max(0, -steps), min(count, count - steps))
    return lax.ppermute(value, axis, [(source, source + steps) for source in range(first, last)])


def contract_rows(left, right):
    return lax.dot_general(
        left, right, (((0,), (0,)), ((), ())), preferred_element_type=jnp.float32
    )


def scaled_by(rotated, eigvals, ridge_grid, total_rows):
    penalty = 2.0 ** ((ridge_grid.astype(jnp.float32) - 8.0) * 0.5)
    scaled = rotated[None] / (
        math.sqrt(total_rows) * (eigvals[None, :, None] + penalty[:, None, None])
    )
    return scaled.astype(jnp.bfloat16)


def gathered(hidden, bold, panel, eigvals, ridge_grid, delays, runs):
    t_rows = hidden.shape[0]
    d_local = hidden.shape[1]
    v_cols = bold.shape[1]
    total_rows = t_rows * lax.axis_size("tm")
    first = lax.axis_index("tm") * t_rows
    ahead = passed_along(bold[:MAXD], "tm", -1)
    extended = jnp.concatenate([bold, ahead], 0)
    runs_pad = jnp.concatenate([runs, jnp.full((MAXD,), -1, jnp.int32)])
    own_runs = lax.dynamic_slice_in_dim(runs, first, t_rows)
    positions = first + jnp.arange(t_rows, dtype=jnp.int32)
    lagged_list = []
    for slot in range(DELAYS):
        offset = delays[slot]
        target_runs = lax.dynamic_slice_in_dim(runs_pad, first + offset, t_rows)
        valid = (positions + offset < total_rows) & (target_runs == own_runs)
        moved = lax.dynamic_slice_in_dim(extended, offset, t_rows, 0)
        lagged_list.append(jnp.where(valid[:, None], moved, jnp.zeros_like(moved)))
    stacked = jnp.stack(lagged_list, 1).reshape(t_rows, DELAYS * v_cols)
    cross = contract_rows(hidden, stacked)
    partial_cov = cross.reshape(d_local * DELAYS, v_cols).astype(jnp.bfloat16)
    panel_rows = lax.all_gather(panel, "tm", axis=0, tiled=True)
    rotated_part = contract_rows(
        lax.all_gather(panel_rows, "voxel", axis=1, tiled=True), partial_cov
    )
    rotated = lax.psum(rotated_part.astype(jnp.bfloat16), ("feature", "tm")).astype(jnp.float32)
    return scaled_by(rotated, eigvals, ridge_grid, total_rows)


def swapped(value, voxel, feature, tm):
    sizes = (lax.axis_size("voxel"), lax.axis_size("feature"), lax.axis_size("tm"))
    pairs = []
    for v in range(sizes[0]):
        for f in range(sizes[1]):
            for t in range(sizes[2]):
                source = (v * sizes[1] + f) * sizes[2] + t
                target = ((v ^ voxel) * sizes[1] + (f ^ feature)) * sizes[2] + (t ^ tm)
                pairs.append((source, target))
    return lax.ppermute(value, ("voxel", "feature", "tm"), pairs)


def sort_matrices(sort):
    block = sort.shape[1]
    half = LANES // 2
    row = lax.broadcasted_iota(jnp.int32, (block, LANES), 0)
    lane = lax.broadcasted_iota(jnp.int32, (block, LANES), 1)
    upper = lane // half
    gap = row - DELAYS * (lane % half)
    for n, slot in enumerate((upper, 1 - upper)):
        for t in range(DELAYS // 2):
            sort[n, :, t * LANES:(t + 1) * LANES] = (gap - slot == 2 * t).astype(F32).astype(BF16)


def sort_into(ordered, panel_t, sort):
    rows = panel_t.shape[0]
    block = sort.shape[1]
    pairs = panel_t.shape[1] // (2 * block)
    mixed = [
        jnp.dot(
            jnp.concatenate(
                [panel_t[:, (2 * m + n) * block:(2 * m + n + 1) * block] for m in range(pairs)], 0
            ),
            sort[n], preferred_element_type=F32,
        )
        for n in range(2)
    ]
    low = lax.broadcasted_iota(jnp.int32, (rows, LANES), 1) < LANES // 2
    for m in range(pairs):
        for t in range(DELAYS // 2):
            first, second = (
                part[m * rows:(m + 1) * rows, t * LANES:(t + 1) * LANES] for part in mixed
            )
            for k, tile in (
                (2 * t, jnp.where(low, first, second)),
                (2 * t + 1, pltpu.roll(jnp.where(low, second, first), LANES // 2, 1)),
            ):
                ordered[k * rows:(k + 1) * rows, m * LANES:(m + 1) * LANES] = tile.astype(BF16)


def lag_sums(products, valid, first, shift, total, start):
    p_cols = total.shape[0]
    tiles = products.shape[1] // LANES
    places = valid.shape[0] // DELAYS
    stacked = []
    for j in range(tiles):
        parts = []
        for k in range(DELAYS):
            mask = jnp.broadcast_to(valid[pl.ds(k * places + first + j, 1), :], (p_cols, LANES))
            part = products[k * p_cols:(k + 1) * p_cols, j * LANES:(j + 1) * LANES]
            parts.append((part * mask).astype(BF16))
        stacked.append(jnp.concatenate(parts, 1))
    moved = jnp.dot(jnp.concatenate(stacked, 0), shift[...], preferred_element_type=F32)
    for j in range(tiles + 1):
        at = pl.ds(pl.multiple_of(start + j * LANES, LANES), LANES)
        add = total[:, at]
        if j < tiles:
            add = add + moved[j * p_cols:(j + 1) * p_cols, :LANES]
        if j > 0:
            add = add + moved[(j - 1) * p_cols:j * p_cols, LANES:]
        total[:, at] = add


def product(ordered, hidden):
    return lax.dot_general(
        ordered[...], hidden[...], (((1,), (1,)), ((), ())), preferred_element_type=F32
    )


def feature_copy(hidden, block, target, sem):
    width = target.shape[1]
    return pltpu.make_async_copy(
        hidden.at[:, pl.ds(pl.multiple_of(block * width, width), width)], target, sem
    )


def early_kernel(
    delays_in, panel_t, panel_core, hidden, runs, total, sort, valid, shift,
    delays, here, products, ordered, loaded, hidden_own, hidden_core, sems,
):
    rows = hidden.shape[0]
    tm = lax.axis_index("tm")
    copies = [
        pltpu.make_async_copy(delays_in, delays, sems.at[0]),
        pltpu.make_async_copy(runs, here, sems.at[1]),
        pltpu.make_async_copy(panel_t, loaded, sems.at[2]),
        feature_copy(hidden, tm, hidden_own, sems.at[3]),
        feature_copy(hidden, tm ^ 1, hidden_core, sems.at[4]),
    ]
    for copy in copies:
        copy.start()
    sort_matrices(sort)
    total[...] = jnp.zeros_like(total)
    copies[2].wait()
    sort_into(ordered, loaded[...], sort)
    copies[3].wait()
    products[...] = product(ordered, hidden_own)
    sort_into(ordered, panel_core[...], sort)
    copies[0].wait()
    copies[1].wait()
    places = here.shape[0]
    now = here[...]
    place = lax.broadcasted_iota(jnp.int32, now.shape, 0)
    lane = lax.broadcasted_iota(jnp.int32, now.shape, 1)
    later = jnp.where(place == places - 1, -1, pltpu.roll(now, places - 1, 0))
    row = lax.broadcasted_iota(jnp.int32, (LANES, 2 * LANES), 0)
    col = lax.broadcasted_iota(jnp.int32, (LANES, 2 * LANES), 1)
    for k in range(DELAYS):
        back = LANES - delays[k]
        target = jnp.where(lane < back, pltpu.roll(now, back, 1), pltpu.roll(later, back, 1))
        valid[k * places:(k + 1) * places, :] = (target == now).astype(F32)
        shift[k * LANES:(k + 1) * LANES, :] = (col - row == delays[k]).astype(F32).astype(BF16)
    copies[4].wait()
    products[...] += product(ordered, hidden_core)
    lag_sums(products, valid, tm * (rows // LANES), shift, total, 0)


def add_part(panel_t, sort, hidden, valid, shift, total, ordered, products):
    sort_into(ordered, panel_t[...], sort)
    products[...] = product(ordered, hidden)
    lag_sums(products, valid, lax.axis_index("tm") * (hidden.shape[0] // LANES), shift, total, 0)


def own_kernel(panel_t, sort, hidden, valid, shift, earlier, total, ordered, products):
    total[...] = earlier[...]
    add_part(panel_t, sort, hidden, valid, shift, total, ordered, products)


def late_kernel(
    panel_t, sort, hidden, valid, shift, earlier, bold, bold_x, ahead, out, ordered, products, total,
):
    rows, v_cols = bold.shape
    total[...] = earlier[...]
    add_part(panel_t, sort, hidden, valid, shift, total, ordered, products)
    mine = total[:, :rows].astype(BF16)
    beyond = total[:, rows:].astype(BF16)
    blank = jnp.zeros((LANES - ahead.shape[0], v_cols), BF16)
    for place, part in enumerate((bold, bold_x)):
        cols = slice(place * v_cols, (place + 1) * v_cols)
        out[:, cols] = jnp.dot(mine, part[...], preferred_element_type=F32) + jnp.dot(
            beyond, jnp.concatenate([ahead[:, cols], blank], 0), preferred_element_type=F32
        )


def head_kernel(bold, bold_x, head):
    v_cols = bold.shape[1]
    for place, part in enumerate((bold, bold_x)):
        head[:, place * v_cols:(place + 1) * v_cols] = part[:16, :]


def call(kernel, operands, out_shape, scratch, outside=()):
    hbm = pl.BlockSpec(memory_space=pltpu.HBM)
    operands = [
        pltpu.with_memory_space_constraint(operand, pltpu.HBM) if n in outside else operand
        for n, operand in enumerate(operands)
    ]
    vmem = pl.BlockSpec(memory_space=pltpu.VMEM)
    return pl.pallas_call(
        kernel,
        out_shape=out_shape,
        in_specs=[
            hbm if n in outside else vmem
            for n, operand in enumerate(operands)
        ],
        out_specs=jax.tree.map(lambda _: vmem, out_shape),
        scratch_shapes=scratch,
        compiler_params=pltpu.CompilerParams(vmem_limit_bytes=12 * 1024 * 1024),
        cost_estimate=pl.CostEstimate(flops=1024, bytes_accessed=1024, transcendentals=0),
    )(*operands)


def after(value, done):
    return lax.optimization_barrier((value, done))[0]


def exchanged(hidden, bold, panel, eigvals, ridge_grid, delays, runs):
    t_rows, d_local = hidden.shape
    v_cols = bold.shape[1]
    p_cols = panel.shape[1]
    tm_count = lax.axis_size("tm")
    total_rows = t_rows * tm_count
    width = d_local // tm_count
    block = DELAYS * LANES
    tm = lax.axis_index("tm")
    voxel = lax.axis_index("voxel")
    reach = t_rows + LANES
    dma = pltpu.SemaphoreType.DMA

    panel_t = panel.T
    late_t = swapped(panel_t, 0, 0, 2)
    panel_core = swapped(panel_t, 0, 0, 1)
    bold_x = swapped(bold, 1, 0, 0)

    places = runs.shape[0] // LANES
    features = pltpu.VMEM((t_rows, width), BF16)
    ordered = pltpu.VMEM((DELAYS * p_cols, width), BF16)
    products = pltpu.VMEM((DELAYS * p_cols, t_rows), F32)
    total = jax.ShapeDtypeStruct((p_cols, reach), F32)
    earlier, sort, valid, shift = call(
        early_kernel, (delays, panel_t, panel_core, hidden, runs.reshape(places, LANES)),
        (total, jax.ShapeDtypeStruct((2, block // 2, block // 2), BF16),
         jax.ShapeDtypeStruct((DELAYS * places, LANES), F32), jax.ShapeDtypeStruct((block, 2 * LANES), BF16)),
        [pltpu.SMEM(delays.shape, jnp.int32), pltpu.VMEM((places, LANES), jnp.int32),
         products, ordered, pltpu.VMEM(panel_t.shape, BF16), features, features, dma((5,))], (0, 1, 3, 4),
    )
    head = call(
        head_kernel, (bold, after(bold_x, earlier)), jax.ShapeDtypeStruct((16, 2 * v_cols), BF16), []
    )
    ahead = passed_along(head, "tm", -1)
    hidden_late = after(hidden, head)
    hidden_own = lax.dynamic_slice_in_dim(hidden_late, (tm ^ 2) * width, width, 1)
    hidden_core = lax.dynamic_slice_in_dim(hidden_late, (tm ^ 3) * width, width, 1)
    late_t = after(late_t, (ahead, hidden_own, hidden_core))
    late_core = swapped(late_t, 0, 0, 1)
    earlier = call(
        own_kernel, (late_t, sort, hidden_own, valid, shift, earlier), total, [ordered, products]
    )
    part = call(
        late_kernel,
        (after(late_core, earlier), sort, hidden_core, valid, shift, earlier, bold, bold_x, ahead),
        jax.ShapeDtypeStruct((p_cols, 2 * v_cols), F32),
        [ordered, products, pltpu.VMEM((p_cols, reach), F32)],
    )

    part = part + swapped(part.astype(BF16), 0, 0, 1).astype(F32)
    mine, theirs = part[:, :v_cols], part[:, v_cols:]
    mine_b, theirs_b = mine.astype(BF16), theirs.astype(BF16)
    from_y = swapped(mine_b, 0, 0, 2)
    from_x = swapped(theirs_b, 1, 0, 0)
    from_xy = swapped(theirs_b, 1, 0, 2)
    near = mine + from_y.astype(F32)
    far = from_x.astype(F32) + from_xy.astype(F32)
    rotated = jnp.where(
        voxel == 0, jnp.concatenate([near, far], 0), jnp.concatenate([far, near], 0)
    )
    rounded = rotated.astype(BF16)
    others = [swapped(rounded, 0, step, 0) for step in (1, 3, 2)]
    rotated = rotated + sum(other.astype(F32) for other in others)
    penalty = 2.0 ** ((ridge_grid.astype(F32) - 8.0) * 0.5)
    scale = 1.0 / (math.sqrt(total_rows) * (eigvals[None, :] + penalty[:, None]))
    return (rotated[None] * scale[:, :, None]).astype(BF16)


def solution(mesh):
    sizes = (mesh.shape["voxel"], mesh.shape["feature"], mesh.shape["tm"])
    shards = exchanged if sizes == (2, 4, 4) else gathered
    return jax.shard_map(
        shards,
        mesh=mesh,
        in_specs=(
            P("tm", "feature"),
            P("tm", "voxel"),
            P(("feature", "tm"), "voxel"),
            P(),
            P(),
            P(),
            P(),
        ),
        out_specs=P(None, None, "voxel"),
        check_vma=False,
    )
```

time: 39.6 us -> 38.7 us (0.977)
  local copies, waits for them, and re-layouts: 1.64 us -> 0.21 us
  waiting for transfers between devices: 14 us -> 15.2 us
  Pallas kernels: 8.15 us -> 7.45 us
    ppermute x10 -> x11, waiting for transfers between devices: 13.9 us -> 15.2 us  [swapped(): return lax.ppermute(value, ('voxel', 'feature', 'tm'), pairs)]
    dynamic_slice x1 -> x0, local copies, waits for them, and re-layouts: 0.77 us -> none  [exchanged(): own_runs = lax.dynamic_slice_in_dim(runs_pad, tm * t_rows, reach)]
    pallas_call x4, Pallas kernels: 8.15 us -> 7.45 us  [call(): pl.pallas_call(kernel, out_shape=out_shape, in_specs=[hbm if n in outside...]
    concatenate x1 -> x0, local copies, waits for them, and re-layouts: 0.66 us -> none  [exchanged(): scalars = jnp.concatenate([delays, jnp.full((8,), tm, jnp.int32)])]
    ppermute x10 -> x11, starting transfers between devices: 12.7 us -> 12.9 us  [swapped(): return lax.ppermute(value, ('voxel', 'feature', 'tm'), pairs)]
    convert_element_type x3 -> x2, other arithmetic: 1.38 us -> 1.36 us  [the longest x1 1.35 us: exchanged(): return (rotated[None] * scale[:, :, None]).astype(BF16)]
  transfers between devices with their start and end apart: 11 -> 12, of which waited for: 8 -> 9; matrix products, arithmetic and copies ran while one was open for 4% -> 1% of each run, Pallas kernels for 15% -> 15%
where the time goes in v3:
time: 38.7 us; the launch traced here: 38.6 us
  waiting for transfers between devices  15.2 us (39%)
  starting transfers between devices  14.2 us (37%)
  Pallas kernels  7.45 us (19%)
  other arithmetic  1.49 us (4%)
    ppermute x11, waiting for transfers between devices, swapped(): return lax.ppermute(value, ('voxel', 'feature', 'tm'), pairs)  15.2 us
    ppermute x11, starting transfers between devices, swapped(): return lax.ppermute(value, ('voxel', 'feature', 'tm'), pairs)  12.9 us
    pallas_call x4, Pallas kernels, call(): pl.pallas_call(kernel, out_shape=out_shape, in_specs=[hbm if n in outside...  7.45 us
    convert_element_type x1, other arithmetic, exchanged(): return (rotated[None] * scale[:, :, None]).astype(BF16)  1.35 us
    ppermute x1, starting transfers between devices, passed_along(): lax.ppermute(value, axis, [(source, source + steps) for source in range(f...  1.28 us
  transfers between devices with their start and end apart: 12, of which 9 were waited for; matrix products, arithmetic and copies ran while one was open for 1% of the time, Pallas kernels for 15%

profile of v3, /device:TPU:0, one launch (start us, length us, event | category | flops | bytes accessed | tf_op | source)
XLA Modules:
  0.0 38.6 jit_solution(14658616793819272168)
XLA Ops:
  0.0 0.5 %collective-permute-start.2 = (bf16[64,4096]{1,0:T(8,128)(2,1)}, bf16[64,4096]{1,0:T(8,128)(2,1)S(1)}, u32[]{:S(2)}, u32[]{:S(2)}) collective-permute-start(bf16[64,4096]{1,0:T(8,128)(2,1)} %bitcast.2), channel_id=1, source_target_pairs={{0,1},{1,0},{2,3},{3,2},{4,5},{5,4},{6,7},{7,6},{8,9},{9,8},{10,11... | collective-permute-start | bytes 1572872 | tf_op jit(solution)/shard_map/ppermute | solution.py:75
  0.5 2.5 %collective-permute-start = (bf16[64,4096]{1,0:T(8,128)(2,1)}, bf16[64,4096]{1,0:T(8,128)(2,1)S(1)}, u32[]{:S(2)}, u32[]{:S(2)}) collective-permute-start(bf16[64,4096]{1,0:T(8,128)(2,1)} %bitcast.3), channel_id=1, source_target_pairs={{0,2},{1,3},{2,0},{3,1},{4,6},{5,7},{6,4},{7,5},{8,10},{9,11},{10,... | collective-permute-start | bytes 1572872 | tf_op jit(solution)/shard_map/ppermute | solution.py:75
  3.0 1.5 %collective-permute-start.1 = (bf16[768,128]{1,0:T(8,128)(2,1)}, bf16[768,128]{1,0:T(8,128)(2,1)S(1)}, u32[]{:S(2)}, u32[]{:S(2)}) collective-permute-start(bf16[768,128]{1,0:T(8,128)(2,1)} %bold.3), channel_id=1, source_target_pairs={{0,16},{1,17},{2,18},{3,19},{4,20},{5,21},{6,22},{7,23},{8,24},{9,... | collective-permute-start | bytes 589832 | tf_op jit(solution)/shard_map/ppermute | solution.py:75
  4.5 0.0 collective-permute-done.2.panel_core
  4.5 4.1 %shard_map.73 = (f32[64,896]{1,0:T(8,128)S(1)}, bf16[2,512,512]{2,1,0:T(8,128)(2,1)S(1)}, f32[192,128]{1,0:T(8,128)S(1)}, bf16[1024,256]{1,0:T(8,128)(2,1)S(1)}) custom-call(s32[8]{0:T(128)} %delays_in.1, bf16[64,4096]{1,0:T(8,128)(2,1)} %bitcast.4, bf16[64,4096]{1,0:T(8,128)(2,1)S(1)} %collective-permute-done.2.panel_core, bf16[768,2048]{1,0:T(8,128)(2,1)} %hidden.1, ...), custom_call_target="tpu_custom_call" | custom-call | flops 1024 | bytes 1024 | tf_op jit(solution)/shard_map/pallas_call | solution.py:233
  8.6 1.6 %collective-permute-done.1.bold_x = bf16[768,128]{1,0:T(8,128)(2,1)S(1)} collective-permute-done((bf16[768,128]{1,0:T(8,128)(2,1)}, bf16[768,128]{1,0:T(8,128)(2,1)S(1)}, u32[]{:S(2)}, u32[]{:S(2)}) %collective-permute-start.1) | collective-permute-done | bytes 196640 | tf_op jit(solution)/shard_map/ppermute | solution.py:75
  10.2 1.3 %collective-permute-start.3 = (bf16[16,256]{1,0:T(8,128)(2,1)S(1)}, bf16[16,256]{1,0:T(8,128)(2,1)S(1)}, u32[]{:S(2)}, u32[]{:S(2)}) collective-permute-start(bf16[16,256]{1,0:T(8,128)(2,1)S(1)} %shard_map.74), channel_id=1, source_target_pairs={{1,0},{2,1},{3,2},{5,4},{6,5},{7,6},{9,8},{10,9},{11,10},{13,12},{... | collective-permute-start | bytes 24584 | tf_op jit(solution)/shard_map/ppermute | solution.py:20
  11.5 0.2 constant_dynamic-slice_fusion
  11.7 4.1 %collective-permute-done.panel_t = bf16[64,4096]{1,0:T(8,128)(2,1)S(1)} collective-permute-done((bf16[64,4096]{1,0:T(8,128)(2,1)}, bf16[64,4096]{1,0:T(8,128)(2,1)S(1)}, u32[]{:S(2)}, u32[]{:S(2)}) %collective-permute-start) | collective-permute-done | bytes 524320 | tf_op jit(solution)/shard_map/ppermute | solution.py:75
  15.8 0.0 collective-permute-done.3.ahead
  15.8 0.1 collective-permute-start.4
  15.9 1.6 %shard_map.75.earlier = f32[64,896]{1,0:T(8,128)S(1)} custom-call(bf16[64,4096]{1,0:T(8,128)(2,1)S(1)} %collective-permute-done.panel_t, bf16[2,512,512]{2,1,0:T(8,128)(2,1)S(1)} %get-tuple-element.17.sort, bf16[768,512]{1,0:T(8,128)(2,1)S(1)} %get-tuple-element.22.hidden, f32[192,128]{1,0:T(8,128)S(1)} %get-tuple-element.18.valid, ...), custom_call_target="tpu_custom_call" | custom-call | flops 1024 | bytes 1024 | tf_op jit(solution)/shard_map/pallas_call | solution.py:233
  17.5 0.0 copy-start.3
  17.5 0.0 copy-start.2
  17.5 0.2 collective-permute-done.4.panel_t
  17.7 1.7 %shard_map.76 = f32[64,256]{1,0:T(8,128)S(1)} custom-call(bf16[64,4096]{1,0:T(8,128)(2,1)S(1)} %collective-permute-done.4.panel_t, bf16[2,512,512]{2,1,0:T(8,128)(2,1)S(1)} %get-tuple-element.17.sort, bf16[768,512]{1,0:T(8,128)(2,1)S(1)} %get-tuple-element.21.hidden, f32[192,128]{1,0:T(8,128)S(1)} %get-tuple-element.18.valid, ...), custom_call_target="tpu_custom_call" | custom-call | flops 1024 | bytes 1024 | tf_op jit(solution)/shard_map/pallas_call | solution.py:233
  19.5 0.3 collective-permute-start.5
  19.8 1.0 %collective-permute-done.5 = bf16[64,256]{1,0:T(8,128)(2,1)S(1)} collective-permute-done((bf16[64,256]{1,0:T(8,128)(2,1)S(1)}, bf16[64,256]{1,0:T(8,128)(2,1)S(1)}, u32[]{:S(2)}, u32[]{:S(2)}) %collective-permute-start.5) | collective-permute-done | bytes 32800 | tf_op jit(solution)/shard_map/ppermute | solution.py:75
  20.8 1.8 %collective-permute-start.6 = (bf16[64,128]{1,0:T(8,128)(2,1)S(1)}, bf16[64,128]{1,0:T(8,128)(2,1)S(1)}, u32[]{:S(2)}, u32[]{:S(2)}) collective-permute-start(bf16[64,128]{1,0:T(8,128)(2,1)S(1)} %get-tuple-element.24), channel_id=1, source_target_pairs={{0,2},{1,3},{2,0},{3,1},{4,6},{5,7},{6,4},{7,5},{8,10},{9,11},{10,... | collective-permute-start | bytes 49160 | tf_op jit(solution)/shard_map/ppermute | solution.py:75
  22.6 1.5 %collective-permute-start.7 = (bf16[64,128]{1,0:T(8,128)(2,1)S(1)}, bf16[64,128]{1,0:T(8,128)(2,1)S(1)}, u32[]{:S(2)}, u32[]{:S(2)}) collective-permute-start(bf16[64,128]{1,0:T(8,128)(2,1)S(1)} %get-tuple-element.23), channel_id=1, source_target_pairs={{0,16},{1,17},{2,18},{3,19},{4,20},{5,21},{6,22},{7,23},{8,24},{9,... | collective-permute-start | bytes 49160 | tf_op jit(solution)/shard_map/ppermute | solution.py:75
  24.1 0.3 collective-permute-start.8
  24.3 0.2 collective-permute-done.6
  24.6 1.8 %collective-permute-done.7 = bf16[64,128]{1,0:T(8,128)(2,1)S(1)} collective-permute-done((bf16[64,128]{1,0:T(8,128)(2,1)S(1)}, bf16[64,128]{1,0:T(8,128)(2,1)S(1)}, u32[]{:S(2)}, u32[]{:S(2)}) %collective-permute-start.7) | collective-permute-done | bytes 16416 | tf_op jit(solution)/shard_map/ppermute | solution.py:75
  26.4 2.3 %collective-permute-done.8 = bf16[64,128]{1,0:T(8,128)(2,1)S(1)} collective-permute-done((bf16[64,128]{1,0:T(8,128)(2,1)S(1)}, bf16[64,128]{1,0:T(8,128)(2,1)S(1)}, u32[]{:S(2)}, u32[]{:S(2)}) %collective-permute-start.8) | collective-permute-done | bytes 16416 | tf_op jit(solution)/shard_map/ppermute | solution.py:75
  28.7 3.7 %collective-permute-start.10 = (bf16[128,128]{1,0:T(8,128)(2,1)S(1)}, bf16[128,128]{1,0:T(8,128)(2,1)S(1)}, u32[]{:S(2)}, u32[]{:S(2)}) collective-permute-start(bf16[128,128]{1,0:T(8,128)(2,1)S(1)} %fusion), channel_id=1, source_target_pairs={{0,12},{1,13},{2,14},{3,15},{4,8},{5,9},{6,10},{7,11},{8,4},{9,5},... | collective-permute-start | bytes 98312 | tf_op jit(solution)/shard_map/ppermute | solution.py:75
  32.4 0.0 collective-permute-start.11
  32.4 0.8 %collective-permute-start.9 = (bf16[128,128]{1,0:T(8,128)(2,1)S(1)}, bf16[128,128]{1,0:T(8,128)(2,1)S(1)}, u32[]{:S(2)}, u32[]{:S(2)}) collective-permute-start(bf16[128,128]{1,0:T(8,128)(2,1)S(1)} %fusion), channel_id=1, source_target_pairs={{0,4},{1,5},{2,6},{3,7},{4,0},{5,1},{6,2},{7,3},{8,12},{9,13},{10,... | collective-permute-start | bytes 98312 | tf_op jit(solution)/shard_map/ppermute | solution.py:75
  33.2 0.1 multiply_divide_fusion
  33.3 1.3 %collective-permute-done.10 = bf16[128,128]{1,0:T(8,128)(2,1)S(1)} collective-permute-done((bf16[128,128]{1,0:T(8,128)(2,1)S(1)}, bf16[128,128]{1,0:T(8,128)(2,1)S(1)}, u32[]{:S(2)}, u32[]{:S(2)}) %collective-permute-start.10) | collective-permute-done | bytes 32800 | tf_op jit(solution)/shard_map/ppermute | solution.py:75
  34.6 2.6 %collective-permute-done.11 = bf16[128,128]{1,0:T(8,128)(2,1)S(1)} collective-permute-done((bf16[128,128]{1,0:T(8,128)(2,1)S(1)}, bf16[128,128]{1,0:T(8,128)(2,1)S(1)}, u32[]{:S(2)}, u32[]{:S(2)}) %collective-permute-start.11) | collective-permute-done | bytes 32800 | tf_op jit(solution)/shard_map/ppermute | solution.py:75
  37.2 0.0 collective-permute-done.9
  37.2 1.4 %multiply_convert_fusion = bf16[24,128,128]{2,1,0:T(8,128)(2,1)} fusion(f32[24,128]{1,0:T(8,128)S(1)} %multiply_divide_fusion, f32[128,128]{1,0:T(8,128)S(1)} %add_add_fusion), kind=kLoop, calls=%fused_computation | loop fusion | flops 786432 | bytes 864256 | tf_op jit(solution)/shard_map/convert_element_type | solution.py:316
  (15 shorter events, 0.1 us)
Async XLA Ops:
  0.0 4.5 %collective-permute-start.2 = (bf16[64,4096]{1,0:T(8,128)(2,1)}, bf16[64,4096]{1,0:T(8,128)(2,1)S(1)}, u32[]{:S(2)}, u32[]{:S(2)}) collective-permute-start(bf16[64,4096]{1,0:T(8,128)(2,1)} %bitcast.2), channel_id=1, source_target_pairs={{0,1},{1,0},{2,3},{3,2},{4,5},{5,4},{6,7},{7,6},{8,9},{9,8},{10,11... | collective-permute-start | bytes 1572872 | tf_op jit(solution)/shard_map/ppermute | solution.py:75
  0.5 15.3 %collective-permute-start = (bf16[64,4096]{1,0:T(8,128)(2,1)}, bf16[64,4096]{1,0:T(8,128)(2,1)S(1)}, u32[]{:S(2)}, u32[]{:S(2)}) collective-permute-start(bf16[64,4096]{1,0:T(8,128)(2,1)} %bitcast.3), channel_id=1, source_target_pairs={{0,2},{1,3},{2,0},{3,1},{4,6},{5,7},{6,4},{7,5},{8,10},{9,11},{10,... | collective-permute-start | bytes 1572872 | tf_op jit(solution)/shard_map/ppermute | solution.py:75
  3.0 7.2 %collective-permute-start.1 = (bf16[768,128]{1,0:T(8,128)(2,1)}, bf16[768,128]{1,0:T(8,128)(2,1)S(1)}, u32[]{:S(2)}, u32[]{:S(2)}) collective-permute-start(bf16[768,128]{1,0:T(8,128)(2,1)} %bold.3), channel_id=1, source_target_pairs={{0,16},{1,17},{2,18},{3,19},{4,20},{5,21},{6,22},{7,23},{8,24},{9,... | collective-permute-start | bytes 589832 | tf_op jit(solution)/shard_map/ppermute | solution.py:75
  4.5 5.8 %copy-start = (bf16[768,128]{1,0:T(8,128)(2,1)S(1)}, bf16[768,128]{1,0:T(8,128)(2,1)}, u32[]{:S(2)}) copy-start(bf16[768,128]{1,0:T(8,128)(2,1)} %bold.3) | copy-start | bytes 589828
  4.5 7.0 %copy-start.1 = (bf16[768,2048]{1,0:T(8,128)(2,1)S(1)}, bf16[768,2048]{1,0:T(8,128)(2,1)}, u32[]{:S(2)}) copy-start(bf16[768,2048]{1,0:T(8,128)(2,1)} %hidden.1) | copy-start | bytes 9437188
  10.2 5.6 %collective-permute-start.3 = (bf16[16,256]{1,0:T(8,128)(2,1)S(1)}, bf16[16,256]{1,0:T(8,128)(2,1)S(1)}, u32[]{:S(2)}, u32[]{:S(2)}) collective-permute-start(bf16[16,256]{1,0:T(8,128)(2,1)S(1)} %shard_map.74), channel_id=1, source_target_pairs={{1,0},{2,1},{3,2},{5,4},{6,5},{7,6},{9,8},{10,9},{11,10},{13,12},{... | collective-permute-start | bytes 24584 | tf_op jit(solution)/shard_map/ppermute | solution.py:20
  15.8 1.9 %collective-permute-start.4 = (bf16[64,4096]{1,0:T(8,128)(2,1)S(1)}, bf16[64,4096]{1,0:T(8,128)(2,1)S(1)}, u32[]{:S(2)}, u32[]{:S(2)}) collective-permute-start(bf16[64,4096]{1,0:T(8,128)(2,1)S(1)} %collective-permute-done.panel_t), channel_id=1, source_target_pairs={{0,1},{1,0},{2,3},{3,2},{4,5},{5,4},{6,7},{7,6},{8,9},{9,8},{10,11... | collective-permute-start | bytes 1572872 | tf_op jit(solution)/shard_map/ppermute | solution.py:75
  17.5 5.1 %copy-start.3 = (s32[24]{0:T(128)S(1)}, s32[24]{0:T(128)}, u32[]{:S(2)}) copy-start(s32[24]{0:T(128)} %param.11) | copy-start | bytes 292
  17.5 15.7 %copy-start.2 = (f32[128]{0:T(128)S(1)}, f32[128]{0:T(128)}, u32[]{:S(2)}) copy-start(f32[128]{0:T(128)} %param.10) | copy-start | bytes 1540
  19.5 1.3 %collective-permute-start.5 = (bf16[64,256]{1,0:T(8,128)(2,1)S(1)}, bf16[64,256]{1,0:T(8,128)(2,1)S(1)}, u32[]{:S(2)}, u32[]{:S(2)}) collective-permute-start(bf16[64,256]{1,0:T(8,128)(2,1)S(1)} %convert_element_type.37), channel_id=1, source_target_pairs={{0,1},{1,0},{2,3},{3,2},{4,5},{5,4},{6,7},{7,6},{8,9},{9,8},{10,11... | collective-permute-start | bytes 98312 | tf_op jit(solution)/shard_map/ppermute | solution.py:75
  20.8 3.8 %collective-permute-start.6 = (bf16[64,128]{1,0:T(8,128)(2,1)S(1)}, bf16[64,128]{1,0:T(8,128)(2,1)S(1)}, u32[]{:S(2)}, u32[]{:S(2)}) collective-permute-start(bf16[64,128]{1,0:T(8,128)(2,1)S(1)} %get-tuple-element.24), channel_id=1, source_target_pairs={{0,2},{1,3},{2,0},{3,1},{4,6},{5,7},{6,4},{7,5},{8,10},{9,11},{10,... | collective-permute-start | bytes 49160 | tf_op jit(solution)/shard_map/ppermute | solution.py:75
  22.6 3.8 %collective-permute-start.7 = (bf16[64,128]{1,0:T(8,128)(2,1)S(1)}, bf16[64,128]{1,0:T(8,128)(2,1)S(1)}, u32[]{:S(2)}, u32[]{:S(2)}) collective-permute-start(bf16[64,128]{1,0:T(8,128)(2,1)S(1)} %get-tuple-element.23), channel_id=1, source_target_pairs={{0,16},{1,17},{2,18},{3,19},{4,20},{5,21},{6,22},{7,23},{8,24},{9,... | collective-permute-start | bytes 49160 | tf_op jit(solution)/shard_map/ppermute | solution.py:75
  24.1 4.6 %collective-permute-start.8 = (bf16[64,128]{1,0:T(8,128)(2,1)S(1)}, bf16[64,128]{1,0:T(8,128)(2,1)S(1)}, u32[]{:S(2)}, u32[]{:S(2)}) collective-permute-start(bf16[64,128]{1,0:T(8,128)(2,1)S(1)} %get-tuple-element.23), channel_id=1, source_target_pairs={{0,18},{1,19},{2,16},{3,17},{4,22},{5,23},{6,20},{7,21},{8,26},{9,... | collective-permute-start | bytes 49160 | tf_op jit(solution)/shard_map/ppermute | solution.py:75
  28.7 5.9 %collective-permute-start.10 = (bf16[128,128]{1,0:T(8,128)(2,1)S(1)}, bf16[128,128]{1,0:T(8,128)(2,1)S(1)}, u32[]{:S(2)}, u32[]{:S(2)}) collective-permute-start(bf16[128,128]{1,0:T(8,128)(2,1)S(1)} %fusion), channel_id=1, source_target_pairs={{0,12},{1,13},{2,14},{3,15},{4,8},{5,9},{6,10},{7,11},{8,4},{9,5},... | collective-permute-start | bytes 98312 | tf_op jit(solution)/shard_map/ppermute | solution.py:75
  32.4 4.8 %collective-permute-start.11 = (bf16[128,128]{1,0:T(8,128)(2,1)S(1)}, bf16[128,128]{1,0:T(8,128)(2,1)S(1)}, u32[]{:S(2)}, u32[]{:S(2)}) collective-permute-start(bf16[128,128]{1,0:T(8,128)(2,1)S(1)} %fusion), channel_id=1, source_target_pairs={{0,8},{1,9},{2,10},{3,11},{4,12},{5,13},{6,14},{7,15},{8,0},{9,1},... | collective-permute-start | bytes 98312 | tf_op jit(solution)/shard_map/ppermute | solution.py:75
  32.4 4.8 %collective-permute-start.9 = (bf16[128,128]{1,0:T(8,128)(2,1)S(1)}, bf16[128,128]{1,0:T(8,128)(2,1)S(1)}, u32[]{:S(2)}, u32[]{:S(2)}) collective-permute-start(bf16[128,128]{1,0:T(8,128)(2,1)S(1)} %fusion), channel_id=1, source_target_pairs={{0,4},{1,5},{2,6},{3,7},{4,0},{5,1},{6,2},{7,3},{8,12},{9,13},{10,... | collective-permute-start | bytes 98312 | tf_op jit(solution)/shard_map/ppermute | solution.py:75

commit v4 on v3

--- a/solution.py
+++ b/solution.py
@@ -75,45 +75,49 @@
     return lax.ppermute(value, ("voxel", "feature", "tm"), pairs)
 
 
+GROUPS = 4
+
+
 def sort_matrices(sort):
-    block = sort.shape[1]
-    half = LANES // 2
-    row = lax.broadcasted_iota(jnp.int32, (block, LANES), 0)
-    lane = lax.broadcasted_iota(jnp.int32, (block, LANES), 1)
-    upper = lane // half
-    gap = row - DELAYS * (lane % half)
-    for n, slot in enumerate((upper, 1 - upper)):
-        for t in range(DELAYS // 2):
-            sort[n, :, t * LANES:(t + 1) * LANES] = (gap - slot == 2 * t).astype(F32).astype(BF16)
+    width = LANES // GROUPS
+    row = lax.broadcasted_iota(jnp.int32, (sort.shape[1], LANES), 0)
+    lane = lax.broadcasted_iota(jnp.int32, (sort.shape[1], LANES), 1)
+    gap = row - DELAYS * (lane % width)
+    for n in range(GROUPS):
+        slot = (lane // width - n) % GROUPS
+        for t in range(DELAYS // GROUPS):
+            sort[n, :, t * LANES:(t + 1) * LANES] = (gap - slot == GROUPS * t).astype(F32).astype(BF16)
 
 
 def sort_into(ordered, panel_t, sort):
     rows = panel_t.shape[0]
     block = sort.shape[1]
-    pairs = panel_t.shape[1] // (2 * block)
+    width = LANES // GROUPS
+    tiles = panel_t.shape[1] // (GROUPS * block)
     mixed = [
         jnp.dot(
             jnp.concatenate(
-                [panel_t[:, (2 * m + n) * block:(2 * m + n + 1) * block] for m in range(pairs)], 0
+                [panel_t[:, (GROUPS * m + n) * block:(GROUPS * m + n + 1) * block] for m in range(tiles)], 0
             ),
             sort[n], preferred_element_type=F32,
         )
-        for n in range(2)
+        for n in range(GROUPS)
     ]
-    low = lax.broadcasted_iota(jnp.int32, (rows, LANES), 1) < LANES // 2
-    for m in range(pairs):
-        for t in range(DELAYS // 2):
-            first, second = (
-                part[m * rows:(m + 1) * rows, t * LANES:(t + 1) * LANES] for part in mixed
-            )
-            for k, tile in (
-                (2 * t, jnp.where(low, first, second)),
-                (2 * t + 1, pltpu.roll(jnp.where(low, second, first), LANES // 2, 1)),
-            ):
+    lane = lax.broadcasted_iota(jnp.int32, (rows, LANES), 1)
+    for m in range(tiles):
+        for t in range(DELAYS // GROUPS):
+            parts = [part[m * rows:(m + 1) * rows, t * LANES:(t + 1) * LANES] for part in mixed]
+            for r in range(GROUPS):
+                tile = parts[(GROUPS - 1 - r) % GROUPS]
+                for place in range(GROUPS - 2, -1, -1):
+                    tile = jnp.where(lane < (place + 1) * width, parts[(place - r) % GROUPS], tile)
+                if r:
+                    tile = pltpu.roll(tile, LANES - r * width, 1)
+                k = t * GROUPS + r
                 ordered[k * rows:(k + 1) * rows, m * LANES:(m + 1) * LANES] = tile.astype(BF16)
 
 
-def lag_sums(products, valid, first, shift, total, start):
+def lag_sums(products, valid, shift, total):
     p_cols = total.shape[0]
     tiles = products.shape[1] // LANES
     places = valid.shape[0] // DELAYS
@@ -121,13 +125,13 @@
     for j in range(tiles):
         parts = []
         for k in range(DELAYS):
-            mask = jnp.broadcast_to(valid[pl.ds(k * places + first + j, 1), :], (p_cols, LANES))
+            mask = valid[k * places + j:k * places + j + 1, :]
             part = products[k * p_cols:(k + 1) * p_cols, j * LANES:(j + 1) * LANES]
             parts.append((part * mask).astype(BF16))
         stacked.append(jnp.concatenate(parts, 1))
     moved = jnp.dot(jnp.concatenate(stacked, 0), shift[...], preferred_element_type=F32)
     for j in range(tiles + 1):
-        at = pl.ds(pl.multiple_of(start + j * LANES, LANES), LANES)
+        at = slice(j * LANES, (j + 1) * LANES)
         add = total[:, at]
         if j < tiles:
             add = add + moved[j * p_cols:(j + 1) * p_cols, :LANES]
@@ -151,9 +155,10 @@
 
 def early_kernel(
     delays_in, panel_t, panel_core, hidden, runs, total, sort, valid, shift,
-    delays, here, products, ordered, loaded, hidden_own, hidden_core, sems,
+    delays, here, all_valid, products, ordered, loaded, hidden_own, hidden_core, sems,
 ):
     rows = hidden.shape[0]
+    tiles, kept = rows // LANES, valid.shape[0] // DELAYS
     tm = lax.axis_index("tm")
     copies = [
         pltpu.make_async_copy(delays_in, delays, sems.at[0]),
@@ -183,17 +188,18 @@
     for k in range(DELAYS):
         back = LANES - delays[k]
         target = jnp.where(lane < back, pltpu.roll(now, back, 1), pltpu.roll(later, back, 1))
-        valid[k * places:(k + 1) * places, :] = (target == now).astype(F32)
+        all_valid[k * places:(k + 1) * places, :] = (target == now).astype(F32)
+        valid[k * kept:k * kept + tiles, :] = all_valid[pl.ds(k * places + tm * tiles, tiles), :]
         shift[k * LANES:(k + 1) * LANES, :] = (col - row == delays[k]).astype(F32).astype(BF16)
     copies[4].wait()
     products[...] += product(ordered, hidden_core)
-    lag_sums(products, valid, tm * (rows // LANES), shift, total, 0)
+    lag_sums(products, valid, shift, total)
 
 
 def add_part(panel_t, sort, hidden, valid, shift, total, ordered, products):
     sort_into(ordered, panel_t[...], sort)
     products[...] = product(ordered, hidden)
-    lag_sums(products, valid, lax.axis_index("tm") * (hidden.shape[0] // LANES), shift, total, 0)
+    lag_sums(products, valid, shift, total)
 
 
 def own_kernel(panel_t, sort, hidden, valid, shift, earlier, total, ordered, products):
@@ -221,6 +227,23 @@
     v_cols = bold.shape[1]
     for place, part in enumerate((bold, bold_x)):
         head[:, place * v_cols:(place + 1) * v_cols] = part[:16, :]
+
+
+PARTS = 8
+
+
+def scale_kernel(rotated, scale, out, scaled, sems):
+    step = scaled.shape[0] // PARTS
+    total = rotated[...]
+    copies = []
+    for part in range(PARTS):
+        for r in range(part * step, (part + 1) * step):
+            scaled[r] = (total * scale[r]).astype(BF16)
+        rows = pl.ds(part * step, step)
+        copies.append(pltpu.make_async_copy(scaled.at[rows], out.at[rows], sems.at[part]))
+        copies[-1].start()
+    for copy in copies:
+        copy.wait()
 
 
 def call(kernel, operands, out_shape, scratch, outside=()):
@@ -273,13 +296,17 @@
     total = jax.ShapeDtypeStruct((p_cols, reach), F32)
     earlier, sort, valid, shift = call(
         early_kernel, (delays, panel_t, panel_core, hidden, runs.reshape(places, LANES)),
-        (total, jax.ShapeDtypeStruct((2, block // 2, block // 2), BF16),
-         jax.ShapeDtypeStruct((DELAYS * places, LANES), F32), jax.ShapeDtypeStruct((block, 2 * LANES), BF16)),
+        (total, jax.ShapeDtypeStruct((GROUPS, block // GROUPS, block // GROUPS), BF16),
+         jax.ShapeDtypeStruct((DELAYS * -(-t_rows // (8 * LANES)) * 8, LANES), F32), jax.ShapeDtypeStruct((block, 2 * LANES), BF16)),
         [pltpu.SMEM(delays.shape, jnp.int32), pltpu.VMEM((places, LANES), jnp.int32),
+         pltpu.VMEM((DELAYS * places, LANES), F32),
          products, ordered, pltpu.VMEM(panel_t.shape, BF16), features, features, dma((5,))], (0, 1, 3, 4),
     )
+    penalty = 2.0 ** ((ridge_grid.astype(F32) - 8.0) * 0.5)
+    scale = 1.0 / (math.sqrt(total_rows) * (eigvals[None, :] + penalty[:, None]))
+    scale = jnp.broadcast_to(scale[:, :, None], (*scale.shape, v_cols))
     head = call(
-        head_kernel, (bold, after(bold_x, earlier)), jax.ShapeDtypeStruct((16, 2 * v_cols), BF16), []
+        head_kernel, (bold, after(bold_x, (earlier, scale))), jax.ShapeDtypeStruct((16, 2 * v_cols), BF16), []
     )
     ahead = passed_along(head, "tm", -1)
     hidden_late = after(hidden, head)
@@ -311,9 +338,15 @@
     rounded = rotated.astype(BF16)
     others = [swapped(rounded, 0, step, 0) for step in (1, 3, 2)]
     rotated = rotated + sum(other.astype(F32) for other in others)
-    penalty = 2.0 ** ((ridge_grid.astype(F32) - 8.0) * 0.5)
-    scale = 1.0 / (math.sqrt(total_rows) * (eigvals[None, :] + penalty[:, None]))
-    return (rotated[None] * scale[:, :, None]).astype(BF16)
+    shape = (ridge_grid.shape[0], 2 * p_cols, v_cols)
+    return pl.pallas_call(
+        scale_kernel,
+        out_shape=jax.ShapeDtypeStruct(shape, BF16),
+        in_specs=2 * [pl.BlockSpec(memory_space=pltpu.VMEM)],
+        out_specs=pl.BlockSpec(memory_space=pl.ANY),
+        scratch_shapes=[pltpu.VMEM(shape, BF16), dma((PARTS,))],
+        compiler_params=pltpu.CompilerParams(vmem_limit_bytes=4 * 1024 * 1024),
+    )(rotated, scale)
 
 
 def solution(mesh):

time: 38.7 us -> 38.1 us (0.984)
  waiting for transfers between devices: 15.2 us -> 13.7 us
  local copies, waits for them, and re-layouts: 0.21 us -> 0.66 us
    ppermute x11, waiting for transfers between devices: 15.2 us -> 13.7 us  [swapped(): return lax.ppermute(value, ('voxel', 'feature', 'tm'), pairs)]
    convert_element_type x1 -> x0, other arithmetic: 1.35 us -> none  [exchanged(): return (rotated[None] * scale[:, :, None]).astype(BF16)]
    pallas_call x0 -> x1, Pallas kernels: none -> 0.95 us  [exchanged(): pl.pallas_call(scale_kernel, out_shape=jax.ShapeDtypeStruct(shape, BF16),...]
    pow x1, other arithmetic: 0.01 us -> 0.81 us  [exchanged(): penalty = 2.0 ** ((ridge_grid.astype(F32) - 8.0) * 0.5)]
    div x1, other arithmetic: 0.07 us -> 0.88 us  [exchanged(): 1.0 / (math.sqrt(total_rows) * (eigvals[None, :] + penalty[:, None]))]
    pallas_call x4, Pallas kernels: 7.45 us -> 6.87 us  [call(): pl.pallas_call(kernel, out_shape=out_shape, in_specs=[hbm if n in outside...]
    broadcast_in_dim x0 -> x1, local copies, waits for them, and re-layouts: none -> 0.46 us  [exchanged(): scale = jnp.broadcast_to(scale[:, :, None], (*scale.shape, v_cols))]
  transfers between devices with their start and end apart: 12 -> 12, of which waited for: 9 -> 9; matrix products, arithmetic and copies ran while one was open for 1% -> 6% of each run, Pallas kernels for 15% -> 14%
where the time goes in v4:
time: 38.1 us; the launch traced here: 38 us
  starting transfers between devices  13.9 us (36%)
  waiting for transfers between devices  13.7 us (36%)
  Pallas kernels  7.82 us (21%)
  other arithmetic  1.75 us (5%)
  local copies, waits for them, and re-layouts  0.66 us (2%)
    ppermute x11, waiting for transfers between devices, swapped(): return lax.ppermute(value, ('voxel', 'feature', 'tm'), pairs)  13.7 us
    ppermute x11, starting transfers between devices, swapped(): return lax.ppermute(value, ('voxel', 'feature', 'tm'), pairs)  12.6 us
    pallas_call x4, Pallas kernels, call(): pl.pallas_call(kernel, out_shape=out_shape, in_specs=[hbm if n in outside...  6.87 us
    ppermute x1, starting transfers between devices, passed_along(): lax.ppermute(value, axis, [(source, source + steps) for source in range(f...  1.29 us
    pallas_call x1, Pallas kernels, exchanged(): pl.pallas_call(scale_kernel, out_shape=jax.ShapeDtypeStruct(shape, BF16),...  0.95 us
    div x1, other arithmetic, exchanged(): 1.0 / (math.sqrt(total_rows) * (eigvals[None, :] + penalty[:, None]))  0.88 us
    pow x1, other arithmetic, exchanged(): penalty = 2.0 ** ((ridge_grid.astype(F32) - 8.0) * 0.5)  0.81 us
  transfers between devices with their start and end apart: 12, of which 9 were waited for; matrix products, arithmetic and copies ran while one was open for 6% of the time, Pallas kernels for 14%

profile of v4, /device:TPU:0, one launch (start us, length us, event | category | flops | bytes accessed | tf_op | source)
XLA Modules:
  0.0 38.0 jit_solution(17381801511793360901)
XLA Ops:
  0.0 0.5 %collective-permute-start.2 = (bf16[64,4096]{1,0:T(8,128)(2,1)}, bf16[64,4096]{1,0:T(8,128)(2,1)S(1)}, u32[]{:S(2)}, u32[]{:S(2)}) collective-permute-start(bf16[64,4096]{1,0:T(8,128)(2,1)} %bitcast.2), channel_id=1, source_target_pairs={{0,1},{1,0},{2,3},{3,2},{4,5},{5,4},{6,7},{7,6},{8,9},{9,8},{10,11... | collective-permute-start | bytes 1572872 | tf_op jit(solution)/shard_map/ppermute | solution.py:75
  0.5 2.6 %collective-permute-start = (bf16[64,4096]{1,0:T(8,128)(2,1)}, bf16[64,4096]{1,0:T(8,128)(2,1)S(1)}, u32[]{:S(2)}, u32[]{:S(2)}) collective-permute-start(bf16[64,4096]{1,0:T(8,128)(2,1)} %bitcast.3), channel_id=1, source_target_pairs={{0,2},{1,3},{2,0},{3,1},{4,6},{5,7},{6,4},{7,5},{8,10},{9,11},{10,... | collective-permute-start | bytes 1572872 | tf_op jit(solution)/shard_map/ppermute | solution.py:75
  3.0 1.5 %collective-permute-start.1 = (bf16[768,128]{1,0:T(8,128)(2,1)}, bf16[768,128]{1,0:T(8,128)(2,1)S(1)}, u32[]{:S(2)}, u32[]{:S(2)}) collective-permute-start(bf16[768,128]{1,0:T(8,128)(2,1)} %bold.3), channel_id=1, source_target_pairs={{0,16},{1,17},{2,18},{3,19},{4,20},{5,21},{6,22},{7,23},{8,24},{9,... | collective-permute-start | bytes 589832 | tf_op jit(solution)/shard_map/ppermute | solution.py:75
  4.5 0.8 %multiply_power_fusion = f32[24]{0:T(128)S(1)} fusion(s32[24]{0:T(128)} %param.11), kind=kLoop, calls=%fused_computation.9 | loop fusion | flops 72 | bytes 192 | tf_op jit(solution)/shard_map/pow | solution.py:305
  5.3 0.9 %multiply_divide_fusion = f32[24,128]{1,0:T(8,128)S(1)} fusion(f32[24]{0:T(128)S(1)} %multiply_power_fusion, f32[128]{0:T(128)} %param.10), kind=kLoop, calls=%fused_computation.8 | loop fusion | flops 9216 | bytes 12896 | tf_op jit(solution)/shard_map/div | solution.py:306
  6.2 0.0 collective-permute-done.2.panel_core
  6.2 3.8 %shard_map.73 = (f32[64,896]{1,0:T(8,128)S(1)}, bf16[4,256,256]{2,1,0:T(8,128)(2,1)S(1)}, f32[64,128]{1,0:T(8,128)S(1)}, bf16[1024,256]{1,0:T(8,128)(2,1)S(1)}) custom-call(s32[8]{0:T(128)} %delays_in.1, bf16[64,4096]{1,0:T(8,128)(2,1)} %bitcast.4, bf16[64,4096]{1,0:T(8,128)(2,1)S(1)} %collective-permute-done.2.panel_core, bf16[768,2048]{1,0:T(8,128)(2,1)} %hidden.1, ...), custom_call_target="tpu_custom_call" | custom-call | flops 1024 | bytes 1024 | tf_op jit(solution)/shard_map/pallas_call | solution.py:256
  10.0 0.2 collective-permute-done.1.bold_x
  10.2 0.5 %broadcast_in_dim.2.scale = f32[24,128,128]{2,1,0:T(8,128)S(1)} broadcast(f32[24,128]{1,0:T(8,128)S(1)} %multiply_divide_fusion), dimensions={0,1} | broadcast | bytes 1585152 | tf_op jit(solution)/shard_map/broadcast_in_dim | solution.py:307
  10.7 1.3 %collective-permute-start.3 = (bf16[16,256]{1,0:T(8,128)(2,1)S(1)}, bf16[16,256]{1,0:T(8,128)(2,1)S(1)}, u32[]{:S(2)}, u32[]{:S(2)}) collective-permute-start(bf16[16,256]{1,0:T(8,128)(2,1)S(1)} %shard_map.74), channel_id=1, source_target_pairs={{1,0},{2,1},{3,2},{5,4},{6,5},{7,6},{9,8},{10,9},{11,10},{13,12},{... | collective-permute-start | bytes 24584 | tf_op jit(solution)/shard_map/ppermute | solution.py:20
  12.0 0.2 constant_dynamic-slice_fusion
  12.2 3.6 %collective-permute-done.panel_t = bf16[64,4096]{1,0:T(8,128)(2,1)S(1)} collective-permute-done((bf16[64,4096]{1,0:T(8,128)(2,1)}, bf16[64,4096]{1,0:T(8,128)(2,1)S(1)}, u32[]{:S(2)}, u32[]{:S(2)}) %collective-permute-start) | collective-permute-done | bytes 524320 | tf_op jit(solution)/shard_map/ppermute | solution.py:75
  15.8 0.0 collective-permute-done.3.ahead
  15.8 0.1 collective-permute-start.4
  15.9 1.4 %shard_map.75.earlier = f32[64,896]{1,0:T(8,128)S(1)} custom-call(bf16[64,4096]{1,0:T(8,128)(2,1)S(1)} %collective-permute-done.panel_t, bf16[4,256,256]{2,1,0:T(8,128)(2,1)S(1)} %get-tuple-element.17.sort, bf16[768,512]{1,0:T(8,128)(2,1)S(1)} %get-tuple-element.22.hidden, f32[64,128]{1,0:T(8,128)S(1)} %get-tuple-element.18.valid, ...), custom_call_target="tpu_custom_call" | custom-call | flops 1024 | bytes 1024 | tf_op jit(solution)/shard_map/pallas_call | solution.py:256
  17.4 0.3 collective-permute-done.4.panel_t
  17.7 1.6 %shard_map.76 = f32[64,256]{1,0:T(8,128)S(1)} custom-call(bf16[64,4096]{1,0:T(8,128)(2,1)S(1)} %collective-permute-done.4.panel_t, bf16[4,256,256]{2,1,0:T(8,128)(2,1)S(1)} %get-tuple-element.17.sort, bf16[768,512]{1,0:T(8,128)(2,1)S(1)} %get-tuple-element.21.hidden, f32[64,128]{1,0:T(8,128)S(1)} %get-tuple-element.18.valid, ...), custom_call_target="tpu_custom_call" | custom-call | flops 1024 | bytes 1024 | tf_op jit(solution)/shard_map/pallas_call | solution.py:256
  19.3 0.2 collective-permute-start.5
  19.5 1.1 %collective-permute-done.5 = bf16[64,256]{1,0:T(8,128)(2,1)S(1)} collective-permute-done((bf16[64,256]{1,0:T(8,128)(2,1)S(1)}, bf16[64,256]{1,0:T(8,128)(2,1)S(1)}, u32[]{:S(2)}, u32[]{:S(2)}) %collective-permute-start.5) | collective-permute-done | bytes 32800 | tf_op jit(solution)/shard_map/ppermute | solution.py:75
  20.6 1.8 %collective-permute-start.6 = (bf16[64,128]{1,0:T(8,128)(2,1)S(1)}, bf16[64,128]{1,0:T(8,128)(2,1)S(1)}, u32[]{:S(2)}, u32[]{:S(2)}) collective-permute-start(bf16[64,128]{1,0:T(8,128)(2,1)S(1)} %get-tuple-element.24), channel_id=1, source_target_pairs={{0,2},{1,3},{2,0},{3,1},{4,6},{5,7},{6,4},{7,5},{8,10},{9,11},{10,... | collective-permute-start | bytes 49160 | tf_op jit(solution)/shard_map/ppermute | solution.py:75
  22.5 1.5 %collective-permute-start.7 = (bf16[64,128]{1,0:T(8,128)(2,1)S(1)}, bf16[64,128]{1,0:T(8,128)(2,1)S(1)}, u32[]{:S(2)}, u32[]{:S(2)}) collective-permute-start(bf16[64,128]{1,0:T(8,128)(2,1)S(1)} %get-tuple-element.23), channel_id=1, source_target_pairs={{0,16},{1,17},{2,18},{3,19},{4,20},{5,21},{6,22},{7,23},{8,24},{9,... | collective-permute-start | bytes 49160 | tf_op jit(solution)/shard_map/ppermute | solution.py:75
  23.9 0.3 collective-permute-start.8
  24.2 0.2 collective-permute-done.6
  24.5 1.8 %collective-permute-done.7 = bf16[64,128]{1,0:T(8,128)(2,1)S(1)} collective-permute-done((bf16[64,128]{1,0:T(8,128)(2,1)S(1)}, bf16[64,128]{1,0:T(8,128)(2,1)S(1)}, u32[]{:S(2)}, u32[]{:S(2)}) %collective-permute-start.7) | collective-permute-done | bytes 16416 | tf_op jit(solution)/shard_map/ppermute | solution.py:75
  26.3 2.3 %collective-permute-done.8 = bf16[64,128]{1,0:T(8,128)(2,1)S(1)} collective-permute-done((bf16[64,128]{1,0:T(8,128)(2,1)S(1)}, bf16[64,128]{1,0:T(8,128)(2,1)S(1)}, u32[]{:S(2)}, u32[]{:S(2)}) %collective-permute-start.8) | collective-permute-done | bytes 16416 | tf_op jit(solution)/shard_map/ppermute | solution.py:75
  28.6 2.7 %collective-permute-start.11 = (bf16[128,128]{1,0:T(8,128)(2,1)S(1)}, bf16[128,128]{1,0:T(8,128)(2,1)S(1)}, u32[]{:S(2)}, u32[]{:S(2)}) collective-permute-start(bf16[128,128]{1,0:T(8,128)(2,1)S(1)} %fusion), channel_id=1, source_target_pairs={{0,8},{1,9},{2,10},{3,11},{4,12},{5,13},{6,14},{7,15},{8,0},{9,1},... | collective-permute-start | bytes 98312 | tf_op jit(solution)/shard_map/ppermute | solution.py:75
  31.3 1.3 %collective-permute-start.10 = (bf16[128,128]{1,0:T(8,128)(2,1)S(1)}, bf16[128,128]{1,0:T(8,128)(2,1)S(1)}, u32[]{:S(2)}, u32[]{:S(2)}) collective-permute-start(bf16[128,128]{1,0:T(8,128)(2,1)S(1)} %fusion), channel_id=1, source_target_pairs={{0,12},{1,13},{2,14},{3,15},{4,8},{5,9},{6,10},{7,11},{8,4},{9,5},... | collective-permute-start | bytes 98312 | tf_op jit(solution)/shard_map/ppermute | solution.py:75
  32.6 0.2 collective-permute-start.9
  32.8 1.0 %collective-permute-done.11 = bf16[128,128]{1,0:T(8,128)(2,1)S(1)} collective-permute-done((bf16[128,128]{1,0:T(8,128)(2,1)S(1)}, bf16[128,128]{1,0:T(8,128)(2,1)S(1)}, u32[]{:S(2)}, u32[]{:S(2)}) %collective-permute-start.11) | collective-permute-done | bytes 32800 | tf_op jit(solution)/shard_map/ppermute | solution.py:75
  33.8 3.2 %collective-permute-done.10 = bf16[128,128]{1,0:T(8,128)(2,1)S(1)} collective-permute-done((bf16[128,128]{1,0:T(8,128)(2,1)S(1)}, bf16[128,128]{1,0:T(8,128)(2,1)S(1)}, u32[]{:S(2)}, u32[]{:S(2)}) %collective-permute-start.10) | collective-permute-done | bytes 32800 | tf_op jit(solution)/shard_map/ppermute | solution.py:75
  37.0 0.0 collective-permute-done.9
  37.0 1.0 %shard_map.77 = bf16[24,128,128]{2,1,0:T(8,128)(2,1)} custom-call(f32[128,128]{1,0:T(8,128)S(1)} %add_add_fusion.rotated, f32[24,128,128]{2,1,0:T(8,128)S(1)} %broadcast_in_dim.2.scale), custom_call_target="tpu_custom_call" | custom-call | tf_op jit(solution)/shard_map/pallas_call | solution.py:342
  (12 shorter events, 0.1 us)
Async XLA Ops:
  0.0 10.7 %copy-start = (bf16[768,128]{1,0:T(8,128)(2,1)S(1)}, bf16[768,128]{1,0:T(8,128)(2,1)}, u32[]{:S(2)}) copy-start(bf16[768,128]{1,0:T(8,128)(2,1)} %bold.3) | copy-start | bytes 589828
  0.0 6.2 %collective-permute-start.2 = (bf16[64,4096]{1,0:T(8,128)(2,1)}, bf16[64,4096]{1,0:T(8,128)(2,1)S(1)}, u32[]{:S(2)}, u32[]{:S(2)}) collective-permute-start(bf16[64,4096]{1,0:T(8,128)(2,1)} %bitcast.2), channel_id=1, source_target_pairs={{0,1},{1,0},{2,3},{3,2},{4,5},{5,4},{6,7},{7,6},{8,9},{9,8},{10,11... | collective-permute-start | bytes 1572872 | tf_op jit(solution)/shard_map/ppermute | solution.py:75
  0.5 15.3 %collective-permute-start = (bf16[64,4096]{1,0:T(8,128)(2,1)}, bf16[64,4096]{1,0:T(8,128)(2,1)S(1)}, u32[]{:S(2)}, u32[]{:S(2)}) collective-permute-start(bf16[64,4096]{1,0:T(8,128)(2,1)} %bitcast.3), channel_id=1, source_target_pairs={{0,2},{1,3},{2,0},{3,1},{4,6},{5,7},{6,4},{7,5},{8,10},{9,11},{10,... | collective-permute-start | bytes 1572872 | tf_op jit(solution)/shard_map/ppermute | solution.py:75
  3.0 7.2 %collective-permute-start.1 = (bf16[768,128]{1,0:T(8,128)(2,1)}, bf16[768,128]{1,0:T(8,128)(2,1)S(1)}, u32[]{:S(2)}, u32[]{:S(2)}) collective-permute-start(bf16[768,128]{1,0:T(8,128)(2,1)} %bold.3), channel_id=1, source_target_pairs={{0,16},{1,17},{2,18},{3,19},{4,20},{5,21},{6,22},{7,23},{8,24},{9,... | collective-permute-start | bytes 589832 | tf_op jit(solution)/shard_map/ppermute | solution.py:75
  4.5 7.5 %copy-start.1 = (bf16[768,2048]{1,0:T(8,128)(2,1)S(1)}, bf16[768,2048]{1,0:T(8,128)(2,1)}, u32[]{:S(2)}) copy-start(bf16[768,2048]{1,0:T(8,128)(2,1)} %hidden.1) | copy-start | bytes 9437188
  10.7 5.1 %collective-permute-start.3 = (bf16[16,256]{1,0:T(8,128)(2,1)S(1)}, bf16[16,256]{1,0:T(8,128)(2,1)S(1)}, u32[]{:S(2)}, u32[]{:S(2)}) collective-permute-start(bf16[16,256]{1,0:T(8,128)(2,1)S(1)} %shard_map.74), channel_id=1, source_target_pairs={{1,0},{2,1},{3,2},{5,4},{6,5},{7,6},{9,8},{10,9},{11,10},{13,12},{... | collective-permute-start | bytes 24584 | tf_op jit(solution)/shard_map/ppermute | solution.py:20
  15.8 1.9 %collective-permute-start.4 = (bf16[64,4096]{1,0:T(8,128)(2,1)S(1)}, bf16[64,4096]{1,0:T(8,128)(2,1)S(1)}, u32[]{:S(2)}, u32[]{:S(2)}) collective-permute-start(bf16[64,4096]{1,0:T(8,128)(2,1)S(1)} %collective-permute-done.panel_t), channel_id=1, source_target_pairs={{0,1},{1,0},{2,3},{3,2},{4,5},{5,4},{6,7},{7,6},{8,9},{9,8},{10,11... | collective-permute-start | bytes 1572872 | tf_op jit(solution)/shard_map/ppermute | solution.py:75
  19.3 1.3 %collective-permute-start.5 = (bf16[64,256]{1,0:T(8,128)(2,1)S(1)}, bf16[64,256]{1,0:T(8,128)(2,1)S(1)}, u32[]{:S(2)}, u32[]{:S(2)}) collective-permute-start(bf16[64,256]{1,0:T(8,128)(2,1)S(1)} %convert_element_type.35), channel_id=1, source_target_pairs={{0,1},{1,0},{2,3},{3,2},{4,5},{5,4},{6,7},{7,6},{8,9},{9,8},{10,11... | collective-permute-start | bytes 98312 | tf_op jit(solution)/shard_map/ppermute | solution.py:75
  20.6 3.8 %collective-permute-start.6 = (bf16[64,128]{1,0:T(8,128)(2,1)S(1)}, bf16[64,128]{1,0:T(8,128)(2,1)S(1)}, u32[]{:S(2)}, u32[]{:S(2)}) collective-permute-start(bf16[64,128]{1,0:T(8,128)(2,1)S(1)} %get-tuple-element.24), channel_id=1, source_target_pairs={{0,2},{1,3},{2,0},{3,1},{4,6},{5,7},{6,4},{7,5},{8,10},{9,11},{10,... | collective-permute-start | bytes 49160 | tf_op jit(solution)/shard_map/ppermute | solution.py:75
  22.5 3.8 %collective-permute-start.7 = (bf16[64,128]{1,0:T(8,128)(2,1)S(1)}, bf16[64,128]{1,0:T(8,128)(2,1)S(1)}, u32[]{:S(2)}, u32[]{:S(2)}) collective-permute-start(bf16[64,128]{1,0:T(8,128)(2,1)S(1)} %get-tuple-element.23), channel_id=1, source_target_pairs={{0,16},{1,17},{2,18},{3,19},{4,20},{5,21},{6,22},{7,23},{8,24},{9,... | collective-permute-start | bytes 49160 | tf_op jit(solution)/shard_map/ppermute | solution.py:75
  23.9 4.6 %collective-permute-start.8 = (bf16[64,128]{1,0:T(8,128)(2,1)S(1)}, bf16[64,128]{1,0:T(8,128)(2,1)S(1)}, u32[]{:S(2)}, u32[]{:S(2)}) collective-permute-start(bf16[64,128]{1,0:T(8,128)(2,1)S(1)} %get-tuple-element.23), channel_id=1, source_target_pairs={{0,18},{1,19},{2,16},{3,17},{4,22},{5,23},{6,20},{7,21},{8,26},{9,... | collective-permute-start | bytes 49160 | tf_op jit(solution)/shard_map/ppermute | solution.py:75
  28.6 5.2 %collective-permute-start.11 = (bf16[128,128]{1,0:T(8,128)(2,1)S(1)}, bf16[128,128]{1,0:T(8,128)(2,1)S(1)}, u32[]{:S(2)}, u32[]{:S(2)}) collective-permute-start(bf16[128,128]{1,0:T(8,128)(2,1)S(1)} %fusion), channel_id=1, source_target_pairs={{0,8},{1,9},{2,10},{3,11},{4,12},{5,13},{6,14},{7,15},{8,0},{9,1},... | collective-permute-start | bytes 98312 | tf_op jit(solution)/shard_map/ppermute | solution.py:75
  31.3 5.7 %collective-permute-start.10 = (bf16[128,128]{1,0:T(8,128)(2,1)S(1)}, bf16[128,128]{1,0:T(8,128)(2,1)S(1)}, u32[]{:S(2)}, u32[]{:S(2)}) collective-permute-start(bf16[128,128]{1,0:T(8,128)(2,1)S(1)} %fusion), channel_id=1, source_target_pairs={{0,12},{1,13},{2,14},{3,15},{4,8},{5,9},{6,10},{7,11},{8,4},{9,5},... | collective-permute-start | bytes 98312 | tf_op jit(solution)/shard_map/ppermute | solution.py:75
  32.6 4.4 %collective-permute-start.9 = (bf16[128,128]{1,0:T(8,128)(2,1)S(1)}, bf16[128,128]{1,0:T(8,128)(2,1)S(1)}, u32[]{:S(2)}, u32[]{:S(2)}) collective-permute-start(bf16[128,128]{1,0:T(8,128)(2,1)S(1)} %fusion), channel_id=1, source_target_pairs={{0,4},{1,5},{2,6},{3,7},{4,0},{5,1},{6,2},{7,3},{8,12},{9,13},{10,... | collective-permute-start | bytes 98312 | tf_op jit(solution)/shard_map/ppermute | solution.py:75

commit v5 on v4

--- a/solution.py
+++ b/solution.py
@@ -324,20 +324,20 @@
         [ordered, products, pltpu.VMEM((p_cols, reach), F32)],
     )
 
-    part = part + swapped(part.astype(BF16), 0, 0, 1).astype(F32)
-    mine, theirs = part[:, :v_cols], part[:, v_cols:]
-    mine_b, theirs_b = mine.astype(BF16), theirs.astype(BF16)
-    from_y = swapped(mine_b, 0, 0, 2)
-    from_x = swapped(theirs_b, 1, 0, 0)
-    from_xy = swapped(theirs_b, 1, 0, 2)
-    near = mine + from_y.astype(F32)
+    part = part.astype(BF16)
+    part = part.astype(F32) + swapped(part, 0, 0, 1).astype(F32)
+    mine, theirs = part[:, :v_cols].astype(BF16), part[:, v_cols:].astype(BF16)
+    from_y = swapped(mine, 0, 0, 3)
+    from_x = swapped(theirs, 1, 0, 1)
+    from_xy = swapped(theirs, 1, 0, 3)
+    near = mine.astype(F32) + from_y.astype(F32)
     far = from_x.astype(F32) + from_xy.astype(F32)
     rotated = jnp.where(
         voxel == 0, jnp.concatenate([near, far], 0), jnp.concatenate([far, near], 0)
     )
-    rounded = rotated.astype(BF16)
-    others = [swapped(rounded, 0, step, 0) for step in (1, 3, 2)]
-    rotated = rotated + sum(other.astype(F32) for other in others)
+    for step in (1, 2):
+        rounded = rotated.astype(BF16)
+        rotated = rounded.astype(F32) + swapped(rounded, 0, step, 1).astype(F32)
     shape = (ridge_grid.shape[0], 2 * p_cols, v_cols)
     return pl.pallas_call(
         scale_kernel,

time: 38.1 us -> 38.4 us (level)
  starting transfers between devices: 13.9 us -> 14.9 us
  waiting for transfers between devices: 13.7 us -> 13 us
    ppermute x11 -> x10, starting transfers between devices: 12.6 us -> 13.6 us  [swapped(): return lax.ppermute(value, ('voxel', 'feature', 'tm'), pairs)]
    ppermute x11 -> x10, waiting for transfers between devices: 13.7 us -> 13 us  [swapped(): return lax.ppermute(value, ('voxel', 'feature', 'tm'), pairs)]
  transfers between devices with their start and end apart: 12 -> 11, of which waited for: 9 -> 9; matrix products, arithmetic and copies ran while one was open for 6% -> 6% of each run, Pallas kernels for 14% -> 14%
where the time goes in v5:
time: 38.4 us; the launch traced here: 38.3 us
  starting transfers between devices  14.9 us (39%)
  waiting for transfers between devices  13 us (34%)
  Pallas kernels  7.82 us (20%)
  other arithmetic  1.76 us (5%)
  local copies, waits for them, and re-layouts  0.65 us (2%)
    ppermute x10, starting transfers between devices, swapped(): return lax.ppermute(value, ('voxel', 'feature', 'tm'), pairs)  13.6 us
    ppermute x10, waiting for transfers between devices, swapped(): return lax.ppermute(value, ('voxel', 'feature', 'tm'), pairs)  13 us
    pallas_call x4, Pallas kernels, call(): pl.pallas_call(kernel, out_shape=out_shape, in_specs=[hbm if n in outside...  6.87 us
    ppermute x1, starting transfers between devices, passed_along(): lax.ppermute(value, axis, [(source, source + steps) for source in range(f...  1.29 us
    pallas_call x1, Pallas kernels, exchanged(): pl.pallas_call(scale_kernel, out_shape=jax.ShapeDtypeStruct(shape, BF16),...  0.95 us
    div x1, other arithmetic, exchanged(): 1.0 / (math.sqrt(total_rows) * (eigvals[None, :] + penalty[:, None]))  0.88 us
    pow x1, other arithmetic, exchanged(): penalty = 2.0 ** ((ridge_grid.astype(F32) - 8.0) * 0.5)  0.81 us
  transfers between devices with their start and end apart: 11, of which 9 were waited for; matrix products, arithmetic and copies ran while one was open for 6% of the time, Pallas kernels for 14%

profile of v5, /device:TPU:0, one launch (start us, length us, event | category | flops | bytes accessed | tf_op | source)
XLA Modules:
  0.0 38.3 jit_solution(10819949882314169203)
XLA Ops:
  0.0 0.5 %collective-permute-start.2 = (bf16[64,4096]{1,0:T(8,128)(2,1)}, bf16[64,4096]{1,0:T(8,128)(2,1)S(1)}, u32[]{:S(2)}, u32[]{:S(2)}) collective-permute-start(bf16[64,4096]{1,0:T(8,128)(2,1)} %bitcast.2), channel_id=1, source_target_pairs={{0,1},{1,0},{2,3},{3,2},{4,5},{5,4},{6,7},{7,6},{8,9},{9,8},{10,11... | collective-permute-start | bytes 1572872 | tf_op jit(solution)/shard_map/ppermute | solution.py:75
  0.5 2.6 %collective-permute-start = (bf16[64,4096]{1,0:T(8,128)(2,1)}, bf16[64,4096]{1,0:T(8,128)(2,1)S(1)}, u32[]{:S(2)}, u32[]{:S(2)}) collective-permute-start(bf16[64,4096]{1,0:T(8,128)(2,1)} %bitcast.3), channel_id=1, source_target_pairs={{0,2},{1,3},{2,0},{3,1},{4,6},{5,7},{6,4},{7,5},{8,10},{9,11},{10,... | collective-permute-start | bytes 1572872 | tf_op jit(solution)/shard_map/ppermute | solution.py:75
  3.0 1.5 %collective-permute-start.1 = (bf16[768,128]{1,0:T(8,128)(2,1)}, bf16[768,128]{1,0:T(8,128)(2,1)S(1)}, u32[]{:S(2)}, u32[]{:S(2)}) collective-permute-start(bf16[768,128]{1,0:T(8,128)(2,1)} %bold.3), channel_id=1, source_target_pairs={{0,16},{1,17},{2,18},{3,19},{4,20},{5,21},{6,22},{7,23},{8,24},{9,... | collective-permute-start | bytes 589832 | tf_op jit(solution)/shard_map/ppermute | solution.py:75
  4.5 0.8 %multiply_power_fusion = f32[24]{0:T(128)S(1)} fusion(s32[24]{0:T(128)} %param.11), kind=kLoop, calls=%fused_computation.8 | loop fusion | flops 72 | bytes 192 | tf_op jit(solution)/shard_map/pow | solution.py:305
  5.3 0.9 %multiply_divide_fusion = f32[24,128]{1,0:T(8,128)S(1)} fusion(f32[24]{0:T(128)S(1)} %multiply_power_fusion, f32[128]{0:T(128)} %param.10), kind=kLoop, calls=%fused_computation.7 | loop fusion | flops 9216 | bytes 12896 | tf_op jit(solution)/shard_map/div | solution.py:306
  6.2 0.0 collective-permute-done.2.panel_core
  6.2 3.8 %shard_map.73 = (f32[64,896]{1,0:T(8,128)S(1)}, bf16[4,256,256]{2,1,0:T(8,128)(2,1)S(1)}, f32[64,128]{1,0:T(8,128)S(1)}, bf16[1024,256]{1,0:T(8,128)(2,1)S(1)}) custom-call(s32[8]{0:T(128)} %delays_in.1, bf16[64,4096]{1,0:T(8,128)(2,1)} %bitcast.4, bf16[64,4096]{1,0:T(8,128)(2,1)S(1)} %collective-permute-done.2.panel_core, bf16[768,2048]{1,0:T(8,128)(2,1)} %hidden.1, ...), custom_call_target="tpu_custom_call" | custom-call | flops 1024 | bytes 1024 | tf_op jit(solution)/shard_map/pallas_call | solution.py:256
  10.0 0.2 collective-permute-done.1.bold_x
  10.2 0.5 %broadcast_in_dim.2.scale = f32[24,128,128]{2,1,0:T(8,128)S(1)} broadcast(f32[24,128]{1,0:T(8,128)S(1)} %multiply_divide_fusion), dimensions={0,1} | broadcast | bytes 1585152 | tf_op jit(solution)/shard_map/broadcast_in_dim | solution.py:307
  10.7 0.0 copy-done
  10.7 1.3 %collective-permute-start.3 = (bf16[16,256]{1,0:T(8,128)(2,1)S(1)}, bf16[16,256]{1,0:T(8,128)(2,1)S(1)}, u32[]{:S(2)}, u32[]{:S(2)}) collective-permute-start(bf16[16,256]{1,0:T(8,128)(2,1)S(1)} %shard_map.74), channel_id=1, source_target_pairs={{1,0},{2,1},{3,2},{5,4},{6,5},{7,6},{9,8},{10,9},{11,10},{13,12},{... | collective-permute-start | bytes 24584 | tf_op jit(solution)/shard_map/ppermute | solution.py:20
  12.0 0.0 copy-done.1
  12.0 0.2 constant_dynamic-slice_fusion
  12.2 3.6 %collective-permute-done.panel_t = bf16[64,4096]{1,0:T(8,128)(2,1)S(1)} collective-permute-done((bf16[64,4096]{1,0:T(8,128)(2,1)}, bf16[64,4096]{1,0:T(8,128)(2,1)S(1)}, u32[]{:S(2)}, u32[]{:S(2)}) %collective-permute-start) | collective-permute-done | bytes 524320 | tf_op jit(solution)/shard_map/ppermute | solution.py:75
  15.8 0.0 collective-permute-done.3.ahead
  15.8 0.1 collective-permute-start.4
  15.9 1.4 %shard_map.75.earlier = f32[64,896]{1,0:T(8,128)S(1)} custom-call(bf16[64,4096]{1,0:T(8,128)(2,1)S(1)} %collective-permute-done.panel_t, bf16[4,256,256]{2,1,0:T(8,128)(2,1)S(1)} %get-tuple-element.17.sort, bf16[768,512]{1,0:T(8,128)(2,1)S(1)} %get-tuple-element.22.hidden, f32[64,128]{1,0:T(8,128)S(1)} %get-tuple-element.18.valid, ...), custom_call_target="tpu_custom_call" | custom-call | flops 1024 | bytes 1024 | tf_op jit(solution)/shard_map/pallas_call | solution.py:256
  17.4 0.3 collective-permute-done.4.panel_t
  17.7 1.6 %shard_map.76 = f32[64,256]{1,0:T(8,128)S(1)} custom-call(bf16[64,4096]{1,0:T(8,128)(2,1)S(1)} %collective-permute-done.4.panel_t, bf16[4,256,256]{2,1,0:T(8,128)(2,1)S(1)} %get-tuple-element.17.sort, bf16[768,512]{1,0:T(8,128)(2,1)S(1)} %get-tuple-element.21.hidden, f32[64,128]{1,0:T(8,128)S(1)} %get-tuple-element.18.valid, ...), custom_call_target="tpu_custom_call" | custom-call | flops 1024 | bytes 1024 | tf_op jit(solution)/shard_map/pallas_call | solution.py:256
  19.3 0.2 collective-permute-start.5
  19.5 1.1 %collective-permute-done.5 = bf16[64,256]{1,0:T(8,128)(2,1)S(1)} collective-permute-done((bf16[64,256]{1,0:T(8,128)(2,1)S(1)}, bf16[64,256]{1,0:T(8,128)(2,1)S(1)}, u32[]{:S(2)}, u32[]{:S(2)}) %collective-permute-start.5) | collective-permute-done | bytes 32800 | tf_op jit(solution)/shard_map/ppermute | solution.py:75
  20.6 1.6 %collective-permute-start.6 = (bf16[64,128]{1,0:T(8,128)(2,1)S(1)}, bf16[64,128]{1,0:T(8,128)(2,1)S(1)}, u32[]{:S(2)}, u32[]{:S(2)}) collective-permute-start(bf16[64,128]{1,0:T(8,128)(2,1)S(1)} %slice.10), channel_id=1, source_target_pairs={{0,3},{1,2},{2,1},{3,0},{4,7},{5,6},{6,5},{7,4},{8,11},{9,10},{10,... | collective-permute-start | bytes 49160 | tf_op jit(solution)/shard_map/ppermute | solution.py:75
  22.2 1.7 %collective-permute-done.6 = bf16[64,128]{1,0:T(8,128)(2,1)S(1)} collective-permute-done((bf16[64,128]{1,0:T(8,128)(2,1)S(1)}, bf16[64,128]{1,0:T(8,128)(2,1)S(1)}, u32[]{:S(2)}, u32[]{:S(2)}) %collective-permute-start.6) | collective-permute-done | bytes 16416 | tf_op jit(solution)/shard_map/ppermute | solution.py:75
  23.9 2.5 %collective-permute-start.8 = (bf16[64,128]{1,0:T(8,128)(2,1)S(1)}, bf16[64,128]{1,0:T(8,128)(2,1)S(1)}, u32[]{:S(2)}, u32[]{:S(2)}) collective-permute-start(bf16[64,128]{1,0:T(8,128)(2,1)S(1)} %get-tuple-element.24), channel_id=1, source_target_pairs={{0,19},{1,18},{2,17},{3,16},{4,23},{5,22},{6,21},{7,20},{8,27},{9,... | collective-permute-start | bytes 49160 | tf_op jit(solution)/shard_map/ppermute | solution.py:75
  26.4 0.5 %collective-permute-start.7 = (bf16[64,128]{1,0:T(8,128)(2,1)S(1)}, bf16[64,128]{1,0:T(8,128)(2,1)S(1)}, u32[]{:S(2)}, u32[]{:S(2)}) collective-permute-start(bf16[64,128]{1,0:T(8,128)(2,1)S(1)} %get-tuple-element.24), channel_id=1, source_target_pairs={{0,17},{1,16},{2,19},{3,18},{4,21},{5,20},{6,23},{7,22},{8,25},{9,... | collective-permute-start | bytes 49160 | tf_op jit(solution)/shard_map/ppermute | solution.py:75
  26.9 1.1 %collective-permute-done.8 = bf16[64,128]{1,0:T(8,128)(2,1)S(1)} collective-permute-done((bf16[64,128]{1,0:T(8,128)(2,1)S(1)}, bf16[64,128]{1,0:T(8,128)(2,1)S(1)}, u32[]{:S(2)}, u32[]{:S(2)}) %collective-permute-start.8) | collective-permute-done | bytes 16416 | tf_op jit(solution)/shard_map/ppermute | solution.py:75
  28.0 1.5 %collective-permute-done.7 = bf16[64,128]{1,0:T(8,128)(2,1)S(1)} collective-permute-done((bf16[64,128]{1,0:T(8,128)(2,1)S(1)}, bf16[64,128]{1,0:T(8,128)(2,1)S(1)}, u32[]{:S(2)}, u32[]{:S(2)}) %collective-permute-start.7) | collective-permute-done | bytes 16416 | tf_op jit(solution)/shard_map/ppermute | solution.py:75
  29.6 1.6 %collective-permute-start.9 = (bf16[128,128]{1,0:T(8,128)(2,1)S(1)}, bf16[128,128]{1,0:T(8,128)(2,1)S(1)}, u32[]{:S(2)}, u32[]{:S(2)}) collective-permute-start(bf16[128,128]{1,0:T(8,128)(2,1)S(1)} %fusion), channel_id=1, source_target_pairs={{0,5},{1,4},{2,7},{3,6},{4,1},{5,0},{6,3},{7,2},{8,13},{9,12},{10,... | collective-permute-start | bytes 98312 | tf_op jit(solution)/shard_map/ppermute | solution.py:75
  31.2 1.8 %collective-permute-done.9 = bf16[128,128]{1,0:T(8,128)(2,1)S(1)} collective-permute-done((bf16[128,128]{1,0:T(8,128)(2,1)S(1)}, bf16[128,128]{1,0:T(8,128)(2,1)S(1)}, u32[]{:S(2)}, u32[]{:S(2)}) %collective-permute-start.9) | collective-permute-done | bytes 32800 | tf_op jit(solution)/shard_map/ppermute | solution.py:75
  33.0 2.6 %collective-permute-start.10 = (bf16[128,128]{1,0:T(8,128)(2,1)S(1)}, bf16[128,128]{1,0:T(8,128)(2,1)S(1)}, u32[]{:S(2)}, u32[]{:S(2)}) collective-permute-start(bf16[128,128]{1,0:T(8,128)(2,1)S(1)} %add_convert_fusion), channel_id=1, source_target_pairs={{0,9},{1,8},{2,11},{3,10},{4,13},{5,12},{6,15},{7,14},{8,1},{9,0},... | collective-permute-start | bytes 98312 | tf_op jit(solution)/shard_map/ppermute | solution.py:75
  35.6 1.7 %collective-permute-done.10 = bf16[128,128]{1,0:T(8,128)(2,1)S(1)} collective-permute-done((bf16[128,128]{1,0:T(8,128)(2,1)S(1)}, bf16[128,128]{1,0:T(8,128)(2,1)S(1)}, u32[]{:S(2)}, u32[]{:S(2)}) %collective-permute-start.10) | collective-permute-done | bytes 32800 | tf_op jit(solution)/shard_map/ppermute | solution.py:75
  37.3 1.0 %shard_map.77 = bf16[24,128,128]{2,1,0:T(8,128)(2,1)} custom-call(f32[128,128]{1,0:T(8,128)S(1)} %convert_add_fusion.rotated, f32[24,128,128]{2,1,0:T(8,128)S(1)} %broadcast_in_dim.2.scale), custom_call_target="tpu_custom_call" | custom-call | tf_op jit(solution)/shard_map/pallas_call | solution.py:342
  (11 shorter events, 0.1 us)
Async XLA Ops:
  0.0 10.7 %copy-start = (bf16[768,128]{1,0:T(8,128)(2,1)S(1)}, bf16[768,128]{1,0:T(8,128)(2,1)}, u32[]{:S(2)}) copy-start(bf16[768,128]{1,0:T(8,128)(2,1)} %bold.3) | copy-start | bytes 589828
  0.0 6.2 %collective-permute-start.2 = (bf16[64,4096]{1,0:T(8,128)(2,1)}, bf16[64,4096]{1,0:T(8,128)(2,1)S(1)}, u32[]{:S(2)}, u32[]{:S(2)}) collective-permute-start(bf16[64,4096]{1,0:T(8,128)(2,1)} %bitcast.2), channel_id=1, source_target_pairs={{0,1},{1,0},{2,3},{3,2},{4,5},{5,4},{6,7},{7,6},{8,9},{9,8},{10,11... | collective-permute-start | bytes 1572872 | tf_op jit(solution)/shard_map/ppermute | solution.py:75
  0.5 15.3 %collective-permute-start = (bf16[64,4096]{1,0:T(8,128)(2,1)}, bf16[64,4096]{1,0:T(8,128)(2,1)S(1)}, u32[]{:S(2)}, u32[]{:S(2)}) collective-permute-start(bf16[64,4096]{1,0:T(8,128)(2,1)} %bitcast.3), channel_id=1, source_target_pairs={{0,2},{1,3},{2,0},{3,1},{4,6},{5,7},{6,4},{7,5},{8,10},{9,11},{10,... | collective-permute-start | bytes 1572872 | tf_op jit(solution)/shard_map/ppermute | solution.py:75
  3.0 7.2 %collective-permute-start.1 = (bf16[768,128]{1,0:T(8,128)(2,1)}, bf16[768,128]{1,0:T(8,128)(2,1)S(1)}, u32[]{:S(2)}, u32[]{:S(2)}) collective-permute-start(bf16[768,128]{1,0:T(8,128)(2,1)} %bold.3), channel_id=1, source_target_pairs={{0,16},{1,17},{2,18},{3,19},{4,20},{5,21},{6,22},{7,23},{8,24},{9,... | collective-permute-start | bytes 589832 | tf_op jit(solution)/shard_map/ppermute | solution.py:75
  4.5 7.5 %copy-start.1 = (bf16[768,2048]{1,0:T(8,128)(2,1)S(1)}, bf16[768,2048]{1,0:T(8,128)(2,1)}, u32[]{:S(2)}) copy-start(bf16[768,2048]{1,0:T(8,128)(2,1)} %hidden.1) | copy-start | bytes 9437188
  10.7 5.1 %collective-permute-start.3 = (bf16[16,256]{1,0:T(8,128)(2,1)S(1)}, bf16[16,256]{1,0:T(8,128)(2,1)S(1)}, u32[]{:S(2)}, u32[]{:S(2)}) collective-permute-start(bf16[16,256]{1,0:T(8,128)(2,1)S(1)} %shard_map.74), channel_id=1, source_target_pairs={{1,0},{2,1},{3,2},{5,4},{6,5},{7,6},{9,8},{10,9},{11,10},{13,12},{... | collective-permute-start | bytes 24584 | tf_op jit(solution)/shard_map/ppermute | solution.py:20
  15.8 1.9 %collective-permute-start.4 = (bf16[64,4096]{1,0:T(8,128)(2,1)S(1)}, bf16[64,4096]{1,0:T(8,128)(2,1)S(1)}, u32[]{:S(2)}, u32[]{:S(2)}) collective-permute-start(bf16[64,4096]{1,0:T(8,128)(2,1)S(1)} %collective-permute-done.panel_t), channel_id=1, source_target_pairs={{0,1},{1,0},{2,3},{3,2},{4,5},{5,4},{6,7},{7,6},{8,9},{9,8},{10,11... | collective-permute-start | bytes 1572872 | tf_op jit(solution)/shard_map/ppermute | solution.py:75
  19.3 1.3 %collective-permute-start.5 = (bf16[64,256]{1,0:T(8,128)(2,1)S(1)}, bf16[64,256]{1,0:T(8,128)(2,1)S(1)}, u32[]{:S(2)}, u32[]{:S(2)}) collective-permute-start(bf16[64,256]{1,0:T(8,128)(2,1)S(1)} %convert_element_type.45), channel_id=1, source_target_pairs={{0,1},{1,0},{2,3},{3,2},{4,5},{5,4},{6,7},{7,6},{8,9},{9,8},{10,11... | collective-permute-start | bytes 98312 | tf_op jit(solution)/shard_map/ppermute | solution.py:75
  20.6 3.2 %collective-permute-start.6 = (bf16[64,128]{1,0:T(8,128)(2,1)S(1)}, bf16[64,128]{1,0:T(8,128)(2,1)S(1)}, u32[]{:S(2)}, u32[]{:S(2)}) collective-permute-start(bf16[64,128]{1,0:T(8,128)(2,1)S(1)} %slice.10), channel_id=1, source_target_pairs={{0,3},{1,2},{2,1},{3,0},{4,7},{5,6},{6,5},{7,4},{8,11},{9,10},{10,... | collective-permute-start | bytes 49160 | tf_op jit(solution)/shard_map/ppermute | solution.py:75
  23.9 4.1 %collective-permute-start.8 = (bf16[64,128]{1,0:T(8,128)(2,1)S(1)}, bf16[64,128]{1,0:T(8,128)(2,1)S(1)}, u32[]{:S(2)}, u32[]{:S(2)}) collective-permute-start(bf16[64,128]{1,0:T(8,128)(2,1)S(1)} %get-tuple-element.24), channel_id=1, source_target_pairs={{0,19},{1,18},{2,17},{3,16},{4,23},{5,22},{6,21},{7,20},{8,27},{9,... | collective-permute-start | bytes 49160 | tf_op jit(solution)/shard_map/ppermute | solution.py:75
  26.4 3.2 %collective-permute-start.7 = (bf16[64,128]{1,0:T(8,128)(2,1)S(1)}, bf16[64,128]{1,0:T(8,128)(2,1)S(1)}, u32[]{:S(2)}, u32[]{:S(2)}) collective-permute-start(bf16[64,128]{1,0:T(8,128)(2,1)S(1)} %get-tuple-element.24), channel_id=1, source_target_pairs={{0,17},{1,16},{2,19},{3,18},{4,21},{5,20},{6,23},{7,22},{8,25},{9,... | collective-permute-start | bytes 49160 | tf_op jit(solution)/shard_map/ppermute | solution.py:75
  29.6 3.4 %collective-permute-start.9 = (bf16[128,128]{1,0:T(8,128)(2,1)S(1)}, bf16[128,128]{1,0:T(8,128)(2,1)S(1)}, u32[]{:S(2)}, u32[]{:S(2)}) collective-permute-start(bf16[128,128]{1,0:T(8,128)(2,1)S(1)} %fusion), channel_id=1, source_target_pairs={{0,5},{1,4},{2,7},{3,6},{4,1},{5,0},{6,3},{7,2},{8,13},{9,12},{10,... | collective-permute-start | bytes 98312 | tf_op jit(solution)/shard_map/ppermute | solution.py:75
  33.0 4.3 %collective-permute-start.10 = (bf16[128,128]{1,0:T(8,128)(2,1)S(1)}, bf16[128,128]{1,0:T(8,128)(2,1)S(1)}, u32[]{:S(2)}, u32[]{:S(2)}) collective-permute-start(bf16[128,128]{1,0:T(8,128)(2,1)S(1)} %add_convert_fusion), channel_id=1, source_target_pairs={{0,9},{1,8},{2,11},{3,10},{4,13},{5,12},{6,15},{7,14},{8,1},{9,0},... | collective-permute-start | bytes 98312 | tf_op jit(solution)/shard_map/ppermute | solution.py:75

commit v6 on v5

--- a/solution.py
+++ b/solution.py
@@ -327,9 +327,10 @@
     part = part.astype(BF16)
     part = part.astype(F32) + swapped(part, 0, 0, 1).astype(F32)
     mine, theirs = part[:, :v_cols].astype(BF16), part[:, v_cols:].astype(BF16)
-    from_y = swapped(mine, 0, 0, 3)
     from_x = swapped(theirs, 1, 0, 1)
     from_xy = swapped(theirs, 1, 0, 3)
+    from_y = swapped(mine, 0, 0, 3)
+    from_y, from_x, from_xy = lax.optimization_barrier((from_y, from_x, from_xy))
     near = mine.astype(F32) + from_y.astype(F32)
     far = from_x.astype(F32) + from_xy.astype(F32)
     rotated = jnp.where(

time: 38.4 us -> 35.7 us (0.930)
  starting transfers between devices: 14.9 us -> 13 us
  waiting for transfers between devices: 13 us -> 12.1 us
    ppermute x10, starting transfers between devices: 13.6 us -> 11.7 us  [swapped(): return lax.ppermute(value, ('voxel', 'feature', 'tm'), pairs)]
    ppermute x10, waiting for transfers between devices: 13 us -> 12.1 us  [swapped(): return lax.ppermute(value, ('voxel', 'feature', 'tm'), pairs)]
  transfers between devices with their start and end apart: 11 -> 11, of which waited for: 9 -> 9; matrix products, arithmetic and copies ran while one was open for 6% -> 7% of each run, Pallas kernels for 14% -> 15%
where the time goes in v6:
time: 35.7 us; the launch traced here: 35.5 us
  starting transfers between devices  13 us (36%)
  waiting for transfers between devices  12.1 us (34%)
  Pallas kernels  7.82 us (22%)
  other arithmetic  1.75 us (5%)
  local copies, waits for them, and re-layouts  0.65 us (2%)
    ppermute x10, waiting for transfers between devices, swapped(): return lax.ppermute(value, ('voxel', 'feature', 'tm'), pairs)  12.1 us
    ppermute x10, starting transfers between devices, swapped(): return lax.ppermute(value, ('voxel', 'feature', 'tm'), pairs)  11.7 us
    pallas_call x4, Pallas kernels, call(): pl.pallas_call(kernel, out_shape=out_shape, in_specs=[hbm if n in outside...  6.87 us
    ppermute x1, starting transfers between devices, passed_along(): lax.ppermute(value, axis, [(source, source + steps) for source in range(f...  1.29 us
    pallas_call x1, Pallas kernels, exchanged(): pl.pallas_call(scale_kernel, out_shape=jax.ShapeDtypeStruct(shape, BF16),...  0.95 us
    div x1, other arithmetic, exchanged(): 1.0 / (math.sqrt(total_rows) * (eigvals[None, :] + penalty[:, None]))  0.88 us
    pow x1, other arithmetic, exchanged(): penalty = 2.0 ** ((ridge_grid.astype(F32) - 8.0) * 0.5)  0.81 us
  transfers between devices with their start and end apart: 11, of which 9 were waited for; matrix products, arithmetic and copies ran while one was open for 7% of the time, Pallas kernels for 15%

profile of v6, /device:TPU:0, one launch (start us, length us, event | category | flops | bytes accessed | tf_op | source)
XLA Modules:
  0.0 35.5 jit_solution(14956922210976559784)
XLA Ops:
  0.0 0.5 %collective-permute-start.2 = (bf16[64,4096]{1,0:T(8,128)(2,1)}, bf16[64,4096]{1,0:T(8,128)(2,1)S(1)}, u32[]{:S(2)}, u32[]{:S(2)}) collective-permute-start(bf16[64,4096]{1,0:T(8,128)(2,1)} %bitcast.2), channel_id=1, source_target_pairs={{0,1},{1,0},{2,3},{3,2},{4,5},{5,4},{6,7},{7,6},{8,9},{9,8},{10,11... | collective-permute-start | bytes 1572872 | tf_op jit(solution)/shard_map/ppermute | solution.py:75
  0.5 2.6 %collective-permute-start = (bf16[64,4096]{1,0:T(8,128)(2,1)}, bf16[64,4096]{1,0:T(8,128)(2,1)S(1)}, u32[]{:S(2)}, u32[]{:S(2)}) collective-permute-start(bf16[64,4096]{1,0:T(8,128)(2,1)} %bitcast.3), channel_id=1, source_target_pairs={{0,2},{1,3},{2,0},{3,1},{4,6},{5,7},{6,4},{7,5},{8,10},{9,11},{10,... | collective-permute-start | bytes 1572872 | tf_op jit(solution)/shard_map/ppermute | solution.py:75
  3.0 1.5 %collective-permute-start.1 = (bf16[768,128]{1,0:T(8,128)(2,1)}, bf16[768,128]{1,0:T(8,128)(2,1)S(1)}, u32[]{:S(2)}, u32[]{:S(2)}) collective-permute-start(bf16[768,128]{1,0:T(8,128)(2,1)} %bold.3), channel_id=1, source_target_pairs={{0,16},{1,17},{2,18},{3,19},{4,20},{5,21},{6,22},{7,23},{8,24},{9,... | collective-permute-start | bytes 589832 | tf_op jit(solution)/shard_map/ppermute | solution.py:75
  4.5 0.8 %multiply_power_fusion = f32[24]{0:T(128)S(1)} fusion(s32[24]{0:T(128)} %param.11), kind=kLoop, calls=%fused_computation.8 | loop fusion | flops 72 | bytes 192 | tf_op jit(solution)/shard_map/pow | solution.py:305
  5.3 0.9 %multiply_divide_fusion = f32[24,128]{1,0:T(8,128)S(1)} fusion(f32[24]{0:T(128)S(1)} %multiply_power_fusion, f32[128]{0:T(128)} %param.10), kind=kLoop, calls=%fused_computation.7 | loop fusion | flops 9216 | bytes 12896 | tf_op jit(solution)/shard_map/div | solution.py:306
  6.2 0.0 collective-permute-done.2.panel_core
  6.2 3.8 %shard_map.73 = (f32[64,896]{1,0:T(8,128)S(1)}, bf16[4,256,256]{2,1,0:T(8,128)(2,1)S(1)}, f32[64,128]{1,0:T(8,128)S(1)}, bf16[1024,256]{1,0:T(8,128)(2,1)S(1)}) custom-call(s32[8]{0:T(128)} %delays_in.1, bf16[64,4096]{1,0:T(8,128)(2,1)} %bitcast.4, bf16[64,4096]{1,0:T(8,128)(2,1)S(1)} %collective-permute-done.2.panel_core, bf16[768,2048]{1,0:T(8,128)(2,1)} %hidden.1, ...), custom_call_target="tpu_custom_call" | custom-call | flops 1024 | bytes 1024 | tf_op jit(solution)/shard_map/pallas_call | solution.py:256
  10.0 0.2 collective-permute-done.1.bold_x
  10.2 0.5 %broadcast_in_dim.2.scale = f32[24,128,128]{2,1,0:T(8,128)S(1)} broadcast(f32[24,128]{1,0:T(8,128)S(1)} %multiply_divide_fusion), dimensions={0,1} | broadcast | bytes 1585152 | tf_op jit(solution)/shard_map/broadcast_in_dim | solution.py:307
  10.7 0.0 copy-done
  10.7 1.3 %collective-permute-start.3 = (bf16[16,256]{1,0:T(8,128)(2,1)S(1)}, bf16[16,256]{1,0:T(8,128)(2,1)S(1)}, u32[]{:S(2)}, u32[]{:S(2)}) collective-permute-start(bf16[16,256]{1,0:T(8,128)(2,1)S(1)} %shard_map.74), channel_id=1, source_target_pairs={{1,0},{2,1},{3,2},{5,4},{6,5},{7,6},{9,8},{10,9},{11,10},{13,12},{... | collective-permute-start | bytes 24584 | tf_op jit(solution)/shard_map/ppermute | solution.py:20
  12.0 0.0 copy-done.1
  12.0 0.2 constant_dynamic-slice_fusion
  12.2 3.6 %collective-permute-done.panel_t = bf16[64,4096]{1,0:T(8,128)(2,1)S(1)} collective-permute-done((bf16[64,4096]{1,0:T(8,128)(2,1)}, bf16[64,4096]{1,0:T(8,128)(2,1)S(1)}, u32[]{:S(2)}, u32[]{:S(2)}) %collective-permute-start) | collective-permute-done | bytes 524320 | tf_op jit(solution)/shard_map/ppermute | solution.py:75
  15.8 0.0 collective-permute-done.3.ahead
  15.8 0.1 collective-permute-start.4
  15.9 1.4 %shard_map.75.earlier = f32[64,896]{1,0:T(8,128)S(1)} custom-call(bf16[64,4096]{1,0:T(8,128)(2,1)S(1)} %collective-permute-done.panel_t, bf16[4,256,256]{2,1,0:T(8,128)(2,1)S(1)} %get-tuple-element.20.sort, bf16[768,512]{1,0:T(8,128)(2,1)S(1)} %get-tuple-element.28.hidden, f32[64,128]{1,0:T(8,128)S(1)} %get-tuple-element.21.valid, ...), custom_call_target="tpu_custom_call" | custom-call | flops 1024 | bytes 1024 | tf_op jit(solution)/shard_map/pallas_call | solution.py:256
  17.4 0.3 collective-permute-done.4.panel_t
  17.7 1.6 %shard_map.76 = f32[64,256]{1,0:T(8,128)S(1)} custom-call(bf16[64,4096]{1,0:T(8,128)(2,1)S(1)} %collective-permute-done.4.panel_t, bf16[4,256,256]{2,1,0:T(8,128)(2,1)S(1)} %get-tuple-element.20.sort, bf16[768,512]{1,0:T(8,128)(2,1)S(1)} %get-tuple-element.27.hidden, f32[64,128]{1,0:T(8,128)S(1)} %get-tuple-element.21.valid, ...), custom_call_target="tpu_custom_call" | custom-call | flops 1024 | bytes 1024 | tf_op jit(solution)/shard_map/pallas_call | solution.py:256
  19.3 0.2 collective-permute-start.5
  19.5 1.1 %collective-permute-done.5 = bf16[64,256]{1,0:T(8,128)(2,1)S(1)} collective-permute-done((bf16[64,256]{1,0:T(8,128)(2,1)S(1)}, bf16[64,256]{1,0:T(8,128)(2,1)S(1)}, u32[]{:S(2)}, u32[]{:S(2)}) %collective-permute-start.5) | collective-permute-done | bytes 32800 | tf_op jit(solution)/shard_map/ppermute | solution.py:75
  20.6 1.6 %collective-permute-start.6 = (bf16[64,128]{1,0:T(8,128)(2,1)S(1)}, bf16[64,128]{1,0:T(8,128)(2,1)S(1)}, u32[]{:S(2)}, u32[]{:S(2)}) collective-permute-start(bf16[64,128]{1,0:T(8,128)(2,1)S(1)} %get-tuple-element.30), channel_id=1, source_target_pairs={{0,3},{1,2},{2,1},{3,0},{4,7},{5,6},{6,5},{7,4},{8,11},{9,10},{10,... | collective-permute-start | bytes 49160 | tf_op jit(solution)/shard_map/ppermute | solution.py:75
  22.2 1.4 %collective-permute-start.8 = (bf16[64,128]{1,0:T(8,128)(2,1)S(1)}, bf16[64,128]{1,0:T(8,128)(2,1)S(1)}, u32[]{:S(2)}, u32[]{:S(2)}) collective-permute-start(bf16[64,128]{1,0:T(8,128)(2,1)S(1)} %get-tuple-element.29), channel_id=1, source_target_pairs={{0,19},{1,18},{2,17},{3,16},{4,23},{5,22},{6,21},{7,20},{8,27},{9,... | collective-permute-start | bytes 49160 | tf_op jit(solution)/shard_map/ppermute | solution.py:75
  23.6 0.1 collective-permute-start.7
  23.7 0.2 collective-permute-done.6
  23.9 2.4 %collective-permute-done.8 = bf16[64,128]{1,0:T(8,128)(2,1)S(1)} collective-permute-done((bf16[64,128]{1,0:T(8,128)(2,1)S(1)}, bf16[64,128]{1,0:T(8,128)(2,1)S(1)}, u32[]{:S(2)}, u32[]{:S(2)}) %collective-permute-start.8) | collective-permute-done | bytes 16416 | tf_op jit(solution)/shard_map/ppermute | solution.py:75
  26.3 0.5 %collective-permute-done.7 = bf16[64,128]{1,0:T(8,128)(2,1)S(1)} collective-permute-done((bf16[64,128]{1,0:T(8,128)(2,1)S(1)}, bf16[64,128]{1,0:T(8,128)(2,1)S(1)}, u32[]{:S(2)}, u32[]{:S(2)}) %collective-permute-start.7) | collective-permute-done | bytes 16416 | tf_op jit(solution)/shard_map/ppermute | solution.py:75
  26.8 1.4 %collective-permute-start.9 = (bf16[128,128]{1,0:T(8,128)(2,1)S(1)}, bf16[128,128]{1,0:T(8,128)(2,1)S(1)}, u32[]{:S(2)}, u32[]{:S(2)}) collective-permute-start(bf16[128,128]{1,0:T(8,128)(2,1)S(1)} %fusion), channel_id=1, source_target_pairs={{0,5},{1,4},{2,7},{3,6},{4,1},{5,0},{6,3},{7,2},{8,13},{9,12},{10,... | collective-permute-start | bytes 98312 | tf_op jit(solution)/shard_map/ppermute | solution.py:75
  28.2 2.0 %collective-permute-done.9 = bf16[128,128]{1,0:T(8,128)(2,1)S(1)} collective-permute-done((bf16[128,128]{1,0:T(8,128)(2,1)S(1)}, bf16[128,128]{1,0:T(8,128)(2,1)S(1)}, u32[]{:S(2)}, u32[]{:S(2)}) %collective-permute-start.9) | collective-permute-done | bytes 32800 | tf_op jit(solution)/shard_map/ppermute | solution.py:75
  30.2 2.4 %collective-permute-start.10 = (bf16[128,128]{1,0:T(8,128)(2,1)S(1)}, bf16[128,128]{1,0:T(8,128)(2,1)S(1)}, u32[]{:S(2)}, u32[]{:S(2)}) collective-permute-start(bf16[128,128]{1,0:T(8,128)(2,1)S(1)} %add_convert_fusion), channel_id=1, source_target_pairs={{0,9},{1,8},{2,11},{3,10},{4,13},{5,12},{6,15},{7,14},{8,1},{9,0},... | collective-permute-start | bytes 98312 | tf_op jit(solution)/shard_map/ppermute | solution.py:75
  32.7 1.9 %collective-permute-done.10 = bf16[128,128]{1,0:T(8,128)(2,1)S(1)} collective-permute-done((bf16[128,128]{1,0:T(8,128)(2,1)S(1)}, bf16[128,128]{1,0:T(8,128)(2,1)S(1)}, u32[]{:S(2)}, u32[]{:S(2)}) %collective-permute-start.10) | collective-permute-done | bytes 32800 | tf_op jit(solution)/shard_map/ppermute | solution.py:75
  34.6 1.0 %shard_map.77 = bf16[24,128,128]{2,1,0:T(8,128)(2,1)} custom-call(f32[128,128]{1,0:T(8,128)S(1)} %convert_add_fusion.rotated, f32[24,128,128]{2,1,0:T(8,128)S(1)} %broadcast_in_dim.2.scale), custom_call_target="tpu_custom_call" | custom-call | tf_op jit(solution)/shard_map/pallas_call | solution.py:343
  (10 shorter events, 0.1 us)
Async XLA Ops:
  0.0 10.7 %copy-start = (bf16[768,128]{1,0:T(8,128)(2,1)S(1)}, bf16[768,128]{1,0:T(8,128)(2,1)}, u32[]{:S(2)}) copy-start(bf16[768,128]{1,0:T(8,128)(2,1)} %bold.3) | copy-start | bytes 589828
  0.0 6.2 %collective-permute-start.2 = (bf16[64,4096]{1,0:T(8,128)(2,1)}, bf16[64,4096]{1,0:T(8,128)(2,1)S(1)}, u32[]{:S(2)}, u32[]{:S(2)}) collective-permute-start(bf16[64,4096]{1,0:T(8,128)(2,1)} %bitcast.2), channel_id=1, source_target_pairs={{0,1},{1,0},{2,3},{3,2},{4,5},{5,4},{6,7},{7,6},{8,9},{9,8},{10,11... | collective-permute-start | bytes 1572872 | tf_op jit(solution)/shard_map/ppermute | solution.py:75
  0.5 15.3 %collective-permute-start = (bf16[64,4096]{1,0:T(8,128)(2,1)}, bf16[64,4096]{1,0:T(8,128)(2,1)S(1)}, u32[]{:S(2)}, u32[]{:S(2)}) collective-permute-start(bf16[64,4096]{1,0:T(8,128)(2,1)} %bitcast.3), channel_id=1, source_target_pairs={{0,2},{1,3},{2,0},{3,1},{4,6},{5,7},{6,4},{7,5},{8,10},{9,11},{10,... | collective-permute-start | bytes 1572872 | tf_op jit(solution)/shard_map/ppermute | solution.py:75
  3.0 7.2 %collective-permute-start.1 = (bf16[768,128]{1,0:T(8,128)(2,1)}, bf16[768,128]{1,0:T(8,128)(2,1)S(1)}, u32[]{:S(2)}, u32[]{:S(2)}) collective-permute-start(bf16[768,128]{1,0:T(8,128)(2,1)} %bold.3), channel_id=1, source_target_pairs={{0,16},{1,17},{2,18},{3,19},{4,20},{5,21},{6,22},{7,23},{8,24},{9,... | collective-permute-start | bytes 589832 | tf_op jit(solution)/shard_map/ppermute | solution.py:75
  4.5 7.5 %copy-start.1 = (bf16[768,2048]{1,0:T(8,128)(2,1)S(1)}, bf16[768,2048]{1,0:T(8,128)(2,1)}, u32[]{:S(2)}) copy-start(bf16[768,2048]{1,0:T(8,128)(2,1)} %hidden.1) | copy-start | bytes 9437188
  10.7 5.1 %collective-permute-start.3 = (bf16[16,256]{1,0:T(8,128)(2,1)S(1)}, bf16[16,256]{1,0:T(8,128)(2,1)S(1)}, u32[]{:S(2)}, u32[]{:S(2)}) collective-permute-start(bf16[16,256]{1,0:T(8,128)(2,1)S(1)} %shard_map.74), channel_id=1, source_target_pairs={{1,0},{2,1},{3,2},{5,4},{6,5},{7,6},{9,8},{10,9},{11,10},{13,12},{... | collective-permute-start | bytes 24584 | tf_op jit(solution)/shard_map/ppermute | solution.py:20
  15.8 1.9 %collective-permute-start.4 = (bf16[64,4096]{1,0:T(8,128)(2,1)S(1)}, bf16[64,4096]{1,0:T(8,128)(2,1)S(1)}, u32[]{:S(2)}, u32[]{:S(2)}) collective-permute-start(bf16[64,4096]{1,0:T(8,128)(2,1)S(1)} %collective-permute-done.panel_t), channel_id=1, source_target_pairs={{0,1},{1,0},{2,3},{3,2},{4,5},{5,4},{6,7},{7,6},{8,9},{9,8},{10,11... | collective-permute-start | bytes 1572872 | tf_op jit(solution)/shard_map/ppermute | solution.py:75
  19.3 1.3 %collective-permute-start.5 = (bf16[64,256]{1,0:T(8,128)(2,1)S(1)}, bf16[64,256]{1,0:T(8,128)(2,1)S(1)}, u32[]{:S(2)}, u32[]{:S(2)}) collective-permute-start(bf16[64,256]{1,0:T(8,128)(2,1)S(1)} %convert_element_type.45), channel_id=1, source_target_pairs={{0,1},{1,0},{2,3},{3,2},{4,5},{5,4},{6,7},{7,6},{8,9},{9,8},{10,11... | collective-permute-start | bytes 98312 | tf_op jit(solution)/shard_map/ppermute | solution.py:75
  20.6 3.2 %collective-permute-start.6 = (bf16[64,128]{1,0:T(8,128)(2,1)S(1)}, bf16[64,128]{1,0:T(8,128)(2,1)S(1)}, u32[]{:S(2)}, u32[]{:S(2)}) collective-permute-start(bf16[64,128]{1,0:T(8,128)(2,1)S(1)} %get-tuple-element.30), channel_id=1, source_target_pairs={{0,3},{1,2},{2,1},{3,0},{4,7},{5,6},{6,5},{7,4},{8,11},{9,10},{10,... | collective-permute-start | bytes 49160 | tf_op jit(solution)/shard_map/ppermute | solution.py:75
  22.2 4.1 %collective-permute-start.8 = (bf16[64,128]{1,0:T(8,128)(2,1)S(1)}, bf16[64,128]{1,0:T(8,128)(2,1)S(1)}, u32[]{:S(2)}, u32[]{:S(2)}) collective-permute-start(bf16[64,128]{1,0:T(8,128)(2,1)S(1)} %get-tuple-element.29), channel_id=1, source_target_pairs={{0,19},{1,18},{2,17},{3,16},{4,23},{5,22},{6,21},{7,20},{8,27},{9,... | collective-permute-start | bytes 49160 | tf_op jit(solution)/shard_map/ppermute | solution.py:75
  23.6 3.2 %collective-permute-start.7 = (bf16[64,128]{1,0:T(8,128)(2,1)S(1)}, bf16[64,128]{1,0:T(8,128)(2,1)S(1)}, u32[]{:S(2)}, u32[]{:S(2)}) collective-permute-start(bf16[64,128]{1,0:T(8,128)(2,1)S(1)} %get-tuple-element.29), channel_id=1, source_target_pairs={{0,17},{1,16},{2,19},{3,18},{4,21},{5,20},{6,23},{7,22},{8,25},{9,... | collective-permute-start | bytes 49160 | tf_op jit(solution)/shard_map/ppermute | solution.py:75
  26.8 3.4 %collective-permute-start.9 = (bf16[128,128]{1,0:T(8,128)(2,1)S(1)}, bf16[128,128]{1,0:T(8,128)(2,1)S(1)}, u32[]{:S(2)}, u32[]{:S(2)}) collective-permute-start(bf16[128,128]{1,0:T(8,128)(2,1)S(1)} %fusion), channel_id=1, source_target_pairs={{0,5},{1,4},{2,7},{3,6},{4,1},{5,0},{6,3},{7,2},{8,13},{9,12},{10,... | collective-permute-start | bytes 98312 | tf_op jit(solution)/shard_map/ppermute | solution.py:75
  30.2 4.3 %collective-permute-start.10 = (bf16[128,128]{1,0:T(8,128)(2,1)S(1)}, bf16[128,128]{1,0:T(8,128)(2,1)S(1)}, u32[]{:S(2)}, u32[]{:S(2)}) collective-permute-start(bf16[128,128]{1,0:T(8,128)(2,1)S(1)} %add_convert_fusion), channel_id=1, source_target_pairs={{0,9},{1,8},{2,11},{3,10},{4,13},{5,12},{6,15},{7,14},{8,1},{9,0},... | collective-permute-start | bytes 98312 | tf_op jit(solution)/shard_map/ppermute | solution.py:75

commit v7 on v6

--- a/solution.py
+++ b/solution.py
@@ -285,7 +285,7 @@
     dma = pltpu.SemaphoreType.DMA
 
     panel_t = panel.T
-    late_t = swapped(panel_t, 0, 0, 2)
+    late_t = swapped(panel_t, 0, 0, 3)
     panel_core = swapped(panel_t, 0, 0, 1)
     bold_x = swapped(bold, 1, 0, 0)
 
@@ -310,8 +310,8 @@
     )
     ahead = passed_along(head, "tm", -1)
     hidden_late = after(hidden, head)
-    hidden_own = lax.dynamic_slice_in_dim(hidden_late, (tm ^ 2) * width, width, 1)
-    hidden_core = lax.dynamic_slice_in_dim(hidden_late, (tm ^ 3) * width, width, 1)
+    hidden_own = lax.dynamic_slice_in_dim(hidden_late, (tm ^ 3) * width, width, 1)
+    hidden_core = lax.dynamic_slice_in_dim(hidden_late, (tm ^ 2) * width, width, 1)
     late_t = after(late_t, (ahead, hidden_own, hidden_core))
     late_core = swapped(late_t, 0, 0, 1)
     earlier = call(

time: 35.7 us -> 35.2 us (0.986)
  waiting for transfers between devices: 12.1 us -> 11.2 us
  starting transfers between devices: 13 us -> 13.5 us
    ppermute x10, waiting for transfers between devices: 12.1 us -> 11.2 us  [swapped(): return lax.ppermute(value, ('voxel', 'feature', 'tm'), pairs)]
    ppermute x10, starting transfers between devices: 11.7 us -> 12.2 us  [swapped(): return lax.ppermute(value, ('voxel', 'feature', 'tm'), pairs)]
where the time goes in v7:
time: 35.2 us; the launch traced here: 35 us
  starting transfers between devices  13.5 us (38%)
  waiting for transfers between devices  11.2 us (32%)
  Pallas kernels  7.83 us (22%)
  other arithmetic  1.75 us (5%)
  local copies, waits for them, and re-layouts  0.65 us (2%)
    ppermute x10, starting transfers between devices, swapped(): return lax.ppermute(value, ('voxel', 'feature', 'tm'), pairs)  12.2 us
    ppermute x10, waiting for transfers between devices, swapped(): return lax.ppermute(value, ('voxel', 'feature', 'tm'), pairs)  11.2 us
    pallas_call x4, Pallas kernels, call(): pl.pallas_call(kernel, out_shape=out_shape, in_specs=[hbm if n in outside...  6.87 us
    ppermute x1, starting transfers between devices, passed_along(): lax.ppermute(value, axis, [(source, source + steps) for source in range(f...  1.29 us
    pallas_call x1, Pallas kernels, exchanged(): pl.pallas_call(scale_kernel, out_shape=jax.ShapeDtypeStruct(shape, BF16),...  0.95 us
    div x1, other arithmetic, exchanged(): 1.0 / (math.sqrt(total_rows) * (eigvals[None, :] + penalty[:, None]))  0.88 us
    pow x1, other arithmetic, exchanged(): penalty = 2.0 ** ((ridge_grid.astype(F32) - 8.0) * 0.5)  0.81 us
  transfers between devices with their start and end apart: 11, of which 9 were waited for; matrix products, arithmetic and copies ran while one was open for 7% of the time, Pallas kernels for 15%

profile of v7, /device:TPU:0, one launch (start us, length us, event | category | flops | bytes accessed | tf_op | source)
XLA Modules:
  0.0 35.0 jit_solution(17513508567577448775)
XLA Ops:
  0.0 0.5 %collective-permute-start.2 = (bf16[64,4096]{1,0:T(8,128)(2,1)}, bf16[64,4096]{1,0:T(8,128)(2,1)S(1)}, u32[]{:S(2)}, u32[]{:S(2)}) collective-permute-start(bf16[64,4096]{1,0:T(8,128)(2,1)} %bitcast.2), channel_id=1, source_target_pairs={{0,1},{1,0},{2,3},{3,2},{4,5},{5,4},{6,7},{7,6},{8,9},{9,8},{10,11... | collective-permute-start | bytes 1572872 | tf_op jit(solution)/shard_map/ppermute | solution.py:75
  0.5 2.6 %collective-permute-start = (bf16[64,4096]{1,0:T(8,128)(2,1)}, bf16[64,4096]{1,0:T(8,128)(2,1)S(1)}, u32[]{:S(2)}, u32[]{:S(2)}) collective-permute-start(bf16[64,4096]{1,0:T(8,128)(2,1)} %bitcast.3), channel_id=1, source_target_pairs={{0,3},{1,2},{2,1},{3,0},{4,7},{5,6},{6,5},{7,4},{8,11},{9,10},{10,... | collective-permute-start | bytes 1572872 | tf_op jit(solution)/shard_map/ppermute | solution.py:75
  3.1 1.5 %collective-permute-start.1 = (bf16[768,128]{1,0:T(8,128)(2,1)}, bf16[768,128]{1,0:T(8,128)(2,1)S(1)}, u32[]{:S(2)}, u32[]{:S(2)}) collective-permute-start(bf16[768,128]{1,0:T(8,128)(2,1)} %bold.3), channel_id=1, source_target_pairs={{0,16},{1,17},{2,18},{3,19},{4,20},{5,21},{6,22},{7,23},{8,24},{9,... | collective-permute-start | bytes 589832 | tf_op jit(solution)/shard_map/ppermute | solution.py:75
  4.6 0.8 %multiply_power_fusion = f32[24]{0:T(128)S(1)} fusion(s32[24]{0:T(128)} %param.11), kind=kLoop, calls=%fused_computation.8 | loop fusion | flops 72 | bytes 192 | tf_op jit(solution)/shard_map/pow | solution.py:305
  5.4 0.9 %multiply_divide_fusion = f32[24,128]{1,0:T(8,128)S(1)} fusion(f32[24]{0:T(128)S(1)} %multiply_power_fusion, f32[128]{0:T(128)} %param.10), kind=kLoop, calls=%fused_computation.7 | loop fusion | flops 9216 | bytes 12896 | tf_op jit(solution)/shard_map/div | solution.py:306
  6.3 0.0 collective-permute-done.2.panel_core
  6.3 3.8 %shard_map.73 = (f32[64,896]{1,0:T(8,128)S(1)}, bf16[4,256,256]{2,1,0:T(8,128)(2,1)S(1)}, f32[64,128]{1,0:T(8,128)S(1)}, bf16[1024,256]{1,0:T(8,128)(2,1)S(1)}) custom-call(s32[8]{0:T(128)} %delays_in.1, bf16[64,4096]{1,0:T(8,128)(2,1)} %bitcast.4, bf16[64,4096]{1,0:T(8,128)(2,1)S(1)} %collective-permute-done.2.panel_core, bf16[768,2048]{1,0:T(8,128)(2,1)} %hidden.1, ...), custom_call_target="tpu_custom_call" | custom-call | flops 1024 | bytes 1024 | tf_op jit(solution)/shard_map/pallas_call | solution.py:256
  10.1 0.1 collective-permute-done.1.bold_x
  10.2 0.5 %broadcast_in_dim.2.scale = f32[24,128,128]{2,1,0:T(8,128)S(1)} broadcast(f32[24,128]{1,0:T(8,128)S(1)} %multiply_divide_fusion), dimensions={0,1} | broadcast | bytes 1585152 | tf_op jit(solution)/shard_map/broadcast_in_dim | solution.py:307
  10.6 0.0 copy-done
  10.7 1.3 %collective-permute-start.3 = (bf16[16,256]{1,0:T(8,128)(2,1)S(1)}, bf16[16,256]{1,0:T(8,128)(2,1)S(1)}, u32[]{:S(2)}, u32[]{:S(2)}) collective-permute-start(bf16[16,256]{1,0:T(8,128)(2,1)S(1)} %shard_map.74), channel_id=1, source_target_pairs={{1,0},{2,1},{3,2},{5,4},{6,5},{7,6},{9,8},{10,9},{11,10},{13,12},{... | collective-permute-start | bytes 24584 | tf_op jit(solution)/shard_map/ppermute | solution.py:20
  12.0 0.0 copy-done.1
  12.0 0.2 constant_dynamic-slice_fusion
  12.2 3.4 %collective-permute-done.panel_t = bf16[64,4096]{1,0:T(8,128)(2,1)S(1)} collective-permute-done((bf16[64,4096]{1,0:T(8,128)(2,1)}, bf16[64,4096]{1,0:T(8,128)(2,1)S(1)}, u32[]{:S(2)}, u32[]{:S(2)}) %collective-permute-start) | collective-permute-done | bytes 524320 | tf_op jit(solution)/shard_map/ppermute | solution.py:75
  15.5 0.0 collective-permute-done.3.ahead
  15.5 0.2 collective-permute-start.4
  15.7 1.5 %shard_map.75.earlier = f32[64,896]{1,0:T(8,128)S(1)} custom-call(bf16[64,4096]{1,0:T(8,128)(2,1)S(1)} %collective-permute-done.panel_t, bf16[4,256,256]{2,1,0:T(8,128)(2,1)S(1)} %get-tuple-element.20.sort, bf16[768,512]{1,0:T(8,128)(2,1)S(1)} %get-tuple-element.28.hidden, f32[64,128]{1,0:T(8,128)S(1)} %get-tuple-element.21.valid, ...), custom_call_target="tpu_custom_call" | custom-call | flops 1024 | bytes 1024 | tf_op jit(solution)/shard_map/pallas_call | solution.py:256
  17.1 0.3 collective-permute-done.4.panel_t
  17.4 1.6 %shard_map.76 = f32[64,256]{1,0:T(8,128)S(1)} custom-call(bf16[64,4096]{1,0:T(8,128)(2,1)S(1)} %collective-permute-done.4.panel_t, bf16[4,256,256]{2,1,0:T(8,128)(2,1)S(1)} %get-tuple-element.20.sort, bf16[768,512]{1,0:T(8,128)(2,1)S(1)} %get-tuple-element.27.hidden, f32[64,128]{1,0:T(8,128)S(1)} %get-tuple-element.21.valid, ...), custom_call_target="tpu_custom_call" | custom-call | flops 1024 | bytes 1024 | tf_op jit(solution)/shard_map/pallas_call | solution.py:256
  19.1 0.2 collective-permute-start.5
  19.3 1.1 %collective-permute-done.5 = bf16[64,256]{1,0:T(8,128)(2,1)S(1)} collective-permute-done((bf16[64,256]{1,0:T(8,128)(2,1)S(1)}, bf16[64,256]{1,0:T(8,128)(2,1)S(1)}, u32[]{:S(2)}, u32[]{:S(2)}) %collective-permute-start.5) | collective-permute-done | bytes 32800 | tf_op jit(solution)/shard_map/ppermute | solution.py:75
  20.4 1.4 %collective-permute-start.6 = (bf16[64,128]{1,0:T(8,128)(2,1)S(1)}, bf16[64,128]{1,0:T(8,128)(2,1)S(1)}, u32[]{:S(2)}, u32[]{:S(2)}) collective-permute-start(bf16[64,128]{1,0:T(8,128)(2,1)S(1)} %get-tuple-element.30), channel_id=1, source_target_pairs={{0,3},{1,2},{2,1},{3,0},{4,7},{5,6},{6,5},{7,4},{8,11},{9,10},{10,... | collective-permute-start | bytes 49160 | tf_op jit(solution)/shard_map/ppermute | solution.py:75
  21.8 1.3 %collective-permute-start.8 = (bf16[64,128]{1,0:T(8,128)(2,1)S(1)}, bf16[64,128]{1,0:T(8,128)(2,1)S(1)}, u32[]{:S(2)}, u32[]{:S(2)}) collective-permute-start(bf16[64,128]{1,0:T(8,128)(2,1)S(1)} %get-tuple-element.29), channel_id=1, source_target_pairs={{0,19},{1,18},{2,17},{3,16},{4,23},{5,22},{6,21},{7,20},{8,27},{9,... | collective-permute-start | bytes 49160 | tf_op jit(solution)/shard_map/ppermute | solution.py:75
  23.1 0.3 collective-permute-start.7
  23.4 0.2 collective-permute-done.6
  23.6 2.3 %collective-permute-done.8 = bf16[64,128]{1,0:T(8,128)(2,1)S(1)} collective-permute-done((bf16[64,128]{1,0:T(8,128)(2,1)S(1)}, bf16[64,128]{1,0:T(8,128)(2,1)S(1)}, u32[]{:S(2)}, u32[]{:S(2)}) %collective-permute-start.8) | collective-permute-done | bytes 16416 | tf_op jit(solution)/shard_map/ppermute | solution.py:75
  25.9 0.4 %collective-permute-done.7 = bf16[64,128]{1,0:T(8,128)(2,1)S(1)} collective-permute-done((bf16[64,128]{1,0:T(8,128)(2,1)S(1)}, bf16[64,128]{1,0:T(8,128)(2,1)S(1)}, u32[]{:S(2)}, u32[]{:S(2)}) %collective-permute-start.7) | collective-permute-done | bytes 16416 | tf_op jit(solution)/shard_map/ppermute | solution.py:75
  26.3 1.6 %collective-permute-start.9 = (bf16[128,128]{1,0:T(8,128)(2,1)S(1)}, bf16[128,128]{1,0:T(8,128)(2,1)S(1)}, u32[]{:S(2)}, u32[]{:S(2)}) collective-permute-start(bf16[128,128]{1,0:T(8,128)(2,1)S(1)} %fusion), channel_id=1, source_target_pairs={{0,5},{1,4},{2,7},{3,6},{4,1},{5,0},{6,3},{7,2},{8,13},{9,12},{10,... | collective-permute-start | bytes 98312 | tf_op jit(solution)/shard_map/ppermute | solution.py:75
  27.9 1.8 %collective-permute-done.9 = bf16[128,128]{1,0:T(8,128)(2,1)S(1)} collective-permute-done((bf16[128,128]{1,0:T(8,128)(2,1)S(1)}, bf16[128,128]{1,0:T(8,128)(2,1)S(1)}, u32[]{:S(2)}, u32[]{:S(2)}) %collective-permute-start.9) | collective-permute-done | bytes 32800 | tf_op jit(solution)/shard_map/ppermute | solution.py:75
  29.7 2.6 %collective-permute-start.10 = (bf16[128,128]{1,0:T(8,128)(2,1)S(1)}, bf16[128,128]{1,0:T(8,128)(2,1)S(1)}, u32[]{:S(2)}, u32[]{:S(2)}) collective-permute-start(bf16[128,128]{1,0:T(8,128)(2,1)S(1)} %add_convert_fusion), channel_id=1, source_target_pairs={{0,9},{1,8},{2,11},{3,10},{4,13},{5,12},{6,15},{7,14},{8,1},{9,0},... | collective-permute-start | bytes 98312 | tf_op jit(solution)/shard_map/ppermute | solution.py:75
  32.3 1.7 %collective-permute-done.10 = bf16[128,128]{1,0:T(8,128)(2,1)S(1)} collective-permute-done((bf16[128,128]{1,0:T(8,128)(2,1)S(1)}, bf16[128,128]{1,0:T(8,128)(2,1)S(1)}, u32[]{:S(2)}, u32[]{:S(2)}) %collective-permute-start.10) | collective-permute-done | bytes 32800 | tf_op jit(solution)/shard_map/ppermute | solution.py:75
  34.1 1.0 %shard_map.77 = bf16[24,128,128]{2,1,0:T(8,128)(2,1)} custom-call(f32[128,128]{1,0:T(8,128)S(1)} %convert_add_fusion.rotated, f32[24,128,128]{2,1,0:T(8,128)S(1)} %broadcast_in_dim.2.scale), custom_call_target="tpu_custom_call" | custom-call | tf_op jit(solution)/shard_map/pallas_call | solution.py:343
  (10 shorter events, 0.1 us)
Async XLA Ops:
  0.0 10.6 %copy-start = (bf16[768,128]{1,0:T(8,128)(2,1)S(1)}, bf16[768,128]{1,0:T(8,128)(2,1)}, u32[]{:S(2)}) copy-start(bf16[768,128]{1,0:T(8,128)(2,1)} %bold.3) | copy-start | bytes 589828
  0.0 6.3 %collective-permute-start.2 = (bf16[64,4096]{1,0:T(8,128)(2,1)}, bf16[64,4096]{1,0:T(8,128)(2,1)S(1)}, u32[]{:S(2)}, u32[]{:S(2)}) collective-permute-start(bf16[64,4096]{1,0:T(8,128)(2,1)} %bitcast.2), channel_id=1, source_target_pairs={{0,1},{1,0},{2,3},{3,2},{4,5},{5,4},{6,7},{7,6},{8,9},{9,8},{10,11... | collective-permute-start | bytes 1572872 | tf_op jit(solution)/shard_map/ppermute | solution.py:75
  0.5 15.1 %collective-permute-start = (bf16[64,4096]{1,0:T(8,128)(2,1)}, bf16[64,4096]{1,0:T(8,128)(2,1)S(1)}, u32[]{:S(2)}, u32[]{:S(2)}) collective-permute-start(bf16[64,4096]{1,0:T(8,128)(2,1)} %bitcast.3), channel_id=1, source_target_pairs={{0,3},{1,2},{2,1},{3,0},{4,7},{5,6},{6,5},{7,4},{8,11},{9,10},{10,... | collective-permute-start | bytes 1572872 | tf_op jit(solution)/shard_map/ppermute | solution.py:75
  3.1 7.1 %collective-permute-start.1 = (bf16[768,128]{1,0:T(8,128)(2,1)}, bf16[768,128]{1,0:T(8,128)(2,1)S(1)}, u32[]{:S(2)}, u32[]{:S(2)}) collective-permute-start(bf16[768,128]{1,0:T(8,128)(2,1)} %bold.3), channel_id=1, source_target_pairs={{0,16},{1,17},{2,18},{3,19},{4,20},{5,21},{6,22},{7,23},{8,24},{9,... | collective-permute-start | bytes 589832 | tf_op jit(solution)/shard_map/ppermute | solution.py:75
  4.6 7.4 %copy-start.1 = (bf16[768,2048]{1,0:T(8,128)(2,1)S(1)}, bf16[768,2048]{1,0:T(8,128)(2,1)}, u32[]{:S(2)}) copy-start(bf16[768,2048]{1,0:T(8,128)(2,1)} %hidden.1) | copy-start | bytes 9437188
  10.7 4.9 %collective-permute-start.3 = (bf16[16,256]{1,0:T(8,128)(2,1)S(1)}, bf16[16,256]{1,0:T(8,128)(2,1)S(1)}, u32[]{:S(2)}, u32[]{:S(2)}) collective-permute-start(bf16[16,256]{1,0:T(8,128)(2,1)S(1)} %shard_map.74), channel_id=1, source_target_pairs={{1,0},{2,1},{3,2},{5,4},{6,5},{7,6},{9,8},{10,9},{11,10},{13,12},{... | collective-permute-start | bytes 24584 | tf_op jit(solution)/shard_map/ppermute | solution.py:20
  15.5 1.9 %collective-permute-start.4 = (bf16[64,4096]{1,0:T(8,128)(2,1)S(1)}, bf16[64,4096]{1,0:T(8,128)(2,1)S(1)}, u32[]{:S(2)}, u32[]{:S(2)}) collective-permute-start(bf16[64,4096]{1,0:T(8,128)(2,1)S(1)} %collective-permute-done.panel_t), channel_id=1, source_target_pairs={{0,1},{1,0},{2,3},{3,2},{4,5},{5,4},{6,7},{7,6},{8,9},{9,8},{10,11... | collective-permute-start | bytes 1572872 | tf_op jit(solution)/shard_map/ppermute | solution.py:75
  19.1 1.3 %collective-permute-start.5 = (bf16[64,256]{1,0:T(8,128)(2,1)S(1)}, bf16[64,256]{1,0:T(8,128)(2,1)S(1)}, u32[]{:S(2)}, u32[]{:S(2)}) collective-permute-start(bf16[64,256]{1,0:T(8,128)(2,1)S(1)} %convert_element_type.45), channel_id=1, source_target_pairs={{0,1},{1,0},{2,3},{3,2},{4,5},{5,4},{6,7},{7,6},{8,9},{9,8},{10,11... | collective-permute-start | bytes 98312 | tf_op jit(solution)/shard_map/ppermute | solution.py:75
  20.4 3.2 %collective-permute-start.6 = (bf16[64,128]{1,0:T(8,128)(2,1)S(1)}, bf16[64,128]{1,0:T(8,128)(2,1)S(1)}, u32[]{:S(2)}, u32[]{:S(2)}) collective-permute-start(bf16[64,128]{1,0:T(8,128)(2,1)S(1)} %get-tuple-element.30), channel_id=1, source_target_pairs={{0,3},{1,2},{2,1},{3,0},{4,7},{5,6},{6,5},{7,4},{8,11},{9,10},{10,... | collective-permute-start | bytes 49160 | tf_op jit(solution)/shard_map/ppermute | solution.py:75
  21.8 4.1 %collective-permute-start.8 = (bf16[64,128]{1,0:T(8,128)(2,1)S(1)}, bf16[64,128]{1,0:T(8,128)(2,1)S(1)}, u32[]{:S(2)}, u32[]{:S(2)}) collective-permute-start(bf16[64,128]{1,0:T(8,128)(2,1)S(1)} %get-tuple-element.29), channel_id=1, source_target_pairs={{0,19},{1,18},{2,17},{3,16},{4,23},{5,22},{6,21},{7,20},{8,27},{9,... | collective-permute-start | bytes 49160 | tf_op jit(solution)/shard_map/ppermute | solution.py:75
  23.1 3.2 %collective-permute-start.7 = (bf16[64,128]{1,0:T(8,128)(2,1)S(1)}, bf16[64,128]{1,0:T(8,128)(2,1)S(1)}, u32[]{:S(2)}, u32[]{:S(2)}) collective-permute-start(bf16[64,128]{1,0:T(8,128)(2,1)S(1)} %get-tuple-element.29), channel_id=1, source_target_pairs={{0,17},{1,16},{2,19},{3,18},{4,21},{5,20},{6,23},{7,22},{8,25},{9,... | collective-permute-start | bytes 49160 | tf_op jit(solution)/shard_map/ppermute | solution.py:75
  26.3 3.4 %collective-permute-start.9 = (bf16[128,128]{1,0:T(8,128)(2,1)S(1)}, bf16[128,128]{1,0:T(8,128)(2,1)S(1)}, u32[]{:S(2)}, u32[]{:S(2)}) collective-permute-start(bf16[128,128]{1,0:T(8,128)(2,1)S(1)} %fusion), channel_id=1, source_target_pairs={{0,5},{1,4},{2,7},{3,6},{4,1},{5,0},{6,3},{7,2},{8,13},{9,12},{10,... | collective-permute-start | bytes 98312 | tf_op jit(solution)/shard_map/ppermute | solution.py:75
  29.7 4.3 %collective-permute-start.10 = (bf16[128,128]{1,0:T(8,128)(2,1)S(1)}, bf16[128,128]{1,0:T(8,128)(2,1)S(1)}, u32[]{:S(2)}, u32[]{:S(2)}) collective-permute-start(bf16[128,128]{1,0:T(8,128)(2,1)S(1)} %add_convert_fusion), channel_id=1, source_target_pairs={{0,9},{1,8},{2,11},{3,10},{4,13},{5,12},{6,15},{7,14},{8,1},{9,0},... | collective-permute-start | bytes 98312 | tf_op jit(solution)/shard_map/ppermute | solution.py:75

commit v8 on v7

--- a/solution.py
+++ b/solution.py
@@ -76,6 +76,14 @@
 
 
 GROUPS = 4
+
+
+def as_sent(value):
+    return lax.reduce_precision(value, 8, 7)
+
+
+def received(value, voxel, feature, tm):
+    return swapped(value.astype(BF16), voxel, feature, tm).astype(F32)
 
 
 def sort_matrices(sort):
@@ -324,12 +332,12 @@
         [ordered, products, pltpu.VMEM((p_cols, reach), F32)],
     )
 
-    part = part.astype(BF16)
-    part = part.astype(F32) + swapped(part, 0, 0, 1).astype(F32)
-    mine, theirs = part[:, :v_cols].astype(BF16), part[:, v_cols:].astype(BF16)
-    from_x = swapped(theirs, 1, 0, 1)
-    from_xy = swapped(theirs, 1, 0, 3)
-    from_y = swapped(mine, 0, 0, 3)
+    part = as_sent(part)
+    part = as_sent(part + received(part, 0, 0, 1)).astype(BF16)
+    mine, theirs = part[:, :v_cols], part[:, v_cols:]
+    from_x = swapped(theirs.astype(BF16), 1, 0, 1)
+    from_xy = swapped(theirs.astype(BF16), 1, 0, 3)
+    from_y = swapped(mine.astype(BF16), 0, 0, 3)
     from_y, from_x, from_xy = lax.optimization_barrier((from_y, from_x, from_xy))
     near = mine.astype(F32) + from_y.astype(F32)
     far = from_x.astype(F32) + from_xy.astype(F32)
@@ -337,8 +345,8 @@
         voxel == 0, jnp.concatenate([near, far], 0), jnp.concatenate([far, near], 0)
     )
     for step in (1, 2):
-        rounded = rotated.astype(BF16)
-        rotated = rounded.astype(F32) + swapped(rounded, 0, step, 1).astype(F32)
+        rotated = as_sent(rotated)
+        rotated = rotated + received(rotated, 0, step, 1)
     shape = (ridge_grid.shape[0], 2 * p_cols, v_cols)
     return pl.pallas_call(
         scale_kernel,

time: 35.2 us -> 35.2 us (level)
  no operation moved by 1% of the time
where the time goes in v8:
time: 35.2 us; the launch traced here: 35 us
  starting transfers between devices  13.5 us (38%)
  waiting for transfers between devices  11.2 us (32%)
  Pallas kernels  7.83 us (22%)
  other arithmetic  1.76 us (5%)
  local copies, waits for them, and re-layouts  0.65 us (2%)
    ppermute x10, starting transfers between devices, swapped(): return lax.ppermute(value, ('voxel', 'feature', 'tm'), pairs)  12.2 us
    ppermute x10, waiting for transfers between devices, swapped(): return lax.ppermute(value, ('voxel', 'feature', 'tm'), pairs)  11.2 us
    pallas_call x4, Pallas kernels, call(): pl.pallas_call(kernel, out_shape=out_shape, in_specs=[hbm if n in outside...  6.87 us
    ppermute x1, starting transfers between devices, passed_along(): lax.ppermute(value, axis, [(source, source + steps) for source in range(f...  1.29 us
    pallas_call x1, Pallas kernels, exchanged(): pl.pallas_call(scale_kernel, out_shape=jax.ShapeDtypeStruct(shape, BF16),...  0.95 us
    div x1, other arithmetic, exchanged(): 1.0 / (math.sqrt(total_rows) * (eigvals[None, :] + penalty[:, None]))  0.88 us
    pow x1, other arithmetic, exchanged(): penalty = 2.0 ** ((ridge_grid.astype(F32) - 8.0) * 0.5)  0.81 us
  transfers between devices with their start and end apart: 11, of which 9 were waited for; matrix products, arithmetic and copies ran while one was open for 7% of the time, Pallas kernels for 15%

profile of v8, /device:TPU:0, one launch (start us, length us, event | category | flops | bytes accessed | tf_op | source)
XLA Modules:
  0.0 35.0 jit_solution(9112171502483246773)
XLA Ops:
  0.0 0.5 %collective-permute-start.2 = (bf16[64,4096]{1,0:T(8,128)(2,1)}, bf16[64,4096]{1,0:T(8,128)(2,1)S(1)}, u32[]{:S(2)}, u32[]{:S(2)}) collective-permute-start(bf16[64,4096]{1,0:T(8,128)(2,1)} %bitcast.2), channel_id=1, source_target_pairs={{0,1},{1,0},{2,3},{3,2},{4,5},{5,4},{6,7},{7,6},{8,9},{9,8},{10,11... | collective-permute-start | bytes 1572872 | tf_op jit(solution)/shard_map/ppermute | solution.py:75
  0.5 2.6 %collective-permute-start = (bf16[64,4096]{1,0:T(8,128)(2,1)}, bf16[64,4096]{1,0:T(8,128)(2,1)S(1)}, u32[]{:S(2)}, u32[]{:S(2)}) collective-permute-start(bf16[64,4096]{1,0:T(8,128)(2,1)} %bitcast.3), channel_id=1, source_target_pairs={{0,3},{1,2},{2,1},{3,0},{4,7},{5,6},{6,5},{7,4},{8,11},{9,10},{10,... | collective-permute-start | bytes 1572872 | tf_op jit(solution)/shard_map/ppermute | solution.py:75
  3.1 1.5 %collective-permute-start.1 = (bf16[768,128]{1,0:T(8,128)(2,1)}, bf16[768,128]{1,0:T(8,128)(2,1)S(1)}, u32[]{:S(2)}, u32[]{:S(2)}) collective-permute-start(bf16[768,128]{1,0:T(8,128)(2,1)} %bold.3), channel_id=1, source_target_pairs={{0,16},{1,17},{2,18},{3,19},{4,20},{5,21},{6,22},{7,23},{8,24},{9,... | collective-permute-start | bytes 589832 | tf_op jit(solution)/shard_map/ppermute | solution.py:75
  4.6 0.8 %multiply_power_fusion = f32[24]{0:T(128)S(1)} fusion(s32[24]{0:T(128)} %param.11), kind=kLoop, calls=%fused_computation.11 | loop fusion | flops 72 | bytes 192 | tf_op jit(solution)/shard_map/pow | solution.py:313
  5.4 0.9 %multiply_divide_fusion = f32[24,128]{1,0:T(8,128)S(1)} fusion(f32[24]{0:T(128)S(1)} %multiply_power_fusion, f32[128]{0:T(128)} %param.10), kind=kLoop, calls=%fused_computation.9 | loop fusion | flops 9216 | bytes 12896 | tf_op jit(solution)/shard_map/div | solution.py:314
  6.3 0.0 collective-permute-done.2.panel_core
  6.3 3.8 %shard_map.73 = (f32[64,896]{1,0:T(8,128)S(1)}, bf16[4,256,256]{2,1,0:T(8,128)(2,1)S(1)}, f32[64,128]{1,0:T(8,128)S(1)}, bf16[1024,256]{1,0:T(8,128)(2,1)S(1)}) custom-call(s32[8]{0:T(128)} %delays_in.1, bf16[64,4096]{1,0:T(8,128)(2,1)} %bitcast.4, bf16[64,4096]{1,0:T(8,128)(2,1)S(1)} %collective-permute-done.2.panel_core, bf16[768,2048]{1,0:T(8,128)(2,1)} %hidden.1, ...), custom_call_target="tpu_custom_call" | custom-call | flops 1024 | bytes 1024 | tf_op jit(solution)/shard_map/pallas_call | solution.py:264
  10.1 0.1 collective-permute-done.1.bold_x
  10.2 0.5 %broadcast_in_dim.2.scale = f32[24,128,128]{2,1,0:T(8,128)S(1)} broadcast(f32[24,128]{1,0:T(8,128)S(1)} %multiply_divide_fusion), dimensions={0,1} | broadcast | bytes 1585152 | tf_op jit(solution)/shard_map/broadcast_in_dim | solution.py:315
  10.6 0.0 copy-done
  10.7 1.3 %collective-permute-start.3 = (bf16[16,256]{1,0:T(8,128)(2,1)S(1)}, bf16[16,256]{1,0:T(8,128)(2,1)S(1)}, u32[]{:S(2)}, u32[]{:S(2)}) collective-permute-start(bf16[16,256]{1,0:T(8,128)(2,1)S(1)} %shard_map.74), channel_id=1, source_target_pairs={{1,0},{2,1},{3,2},{5,4},{6,5},{7,6},{9,8},{10,9},{11,10},{13,12},{... | collective-permute-start | bytes 24584 | tf_op jit(solution)/shard_map/ppermute | solution.py:20
  12.0 0.0 copy-done.1
  12.0 0.2 constant_dynamic-slice_fusion
  12.2 3.4 %collective-permute-done.panel_t = bf16[64,4096]{1,0:T(8,128)(2,1)S(1)} collective-permute-done((bf16[64,4096]{1,0:T(8,128)(2,1)}, bf16[64,4096]{1,0:T(8,128)(2,1)S(1)}, u32[]{:S(2)}, u32[]{:S(2)}) %collective-permute-start) | collective-permute-done | bytes 524320 | tf_op jit(solution)/shard_map/ppermute | solution.py:75
  15.5 0.0 collective-permute-done.3.ahead
  15.5 0.2 collective-permute-start.4
  15.7 1.5 %shard_map.75.earlier = f32[64,896]{1,0:T(8,128)S(1)} custom-call(bf16[64,4096]{1,0:T(8,128)(2,1)S(1)} %collective-permute-done.panel_t, bf16[4,256,256]{2,1,0:T(8,128)(2,1)S(1)} %get-tuple-element.20.sort, bf16[768,512]{1,0:T(8,128)(2,1)S(1)} %get-tuple-element.28.hidden, f32[64,128]{1,0:T(8,128)S(1)} %get-tuple-element.21.valid, ...), custom_call_target="tpu_custom_call" | custom-call | flops 1024 | bytes 1024 | tf_op jit(solution)/shard_map/pallas_call | solution.py:264
  17.1 0.3 collective-permute-done.4.panel_t
  17.4 1.6 %shard_map.76 = f32[64,256]{1,0:T(8,128)S(1)} custom-call(bf16[64,4096]{1,0:T(8,128)(2,1)S(1)} %collective-permute-done.4.panel_t, bf16[4,256,256]{2,1,0:T(8,128)(2,1)S(1)} %get-tuple-element.20.sort, bf16[768,512]{1,0:T(8,128)(2,1)S(1)} %get-tuple-element.27.hidden, f32[64,128]{1,0:T(8,128)S(1)} %get-tuple-element.21.valid, ...), custom_call_target="tpu_custom_call" | custom-call | flops 1024 | bytes 1024 | tf_op jit(solution)/shard_map/pallas_call | solution.py:264
  19.1 0.2 collective-permute-start.5
  19.3 1.1 %collective-permute-done.5 = bf16[64,256]{1,0:T(8,128)(2,1)S(1)} collective-permute-done((bf16[64,256]{1,0:T(8,128)(2,1)S(1)}, bf16[64,256]{1,0:T(8,128)(2,1)S(1)}, u32[]{:S(2)}, u32[]{:S(2)}) %collective-permute-start.5) | collective-permute-done | bytes 32800 | tf_op jit(solution)/shard_map/ppermute | solution.py:75
  20.4 1.4 %collective-permute-start.6 = (bf16[64,128]{1,0:T(8,128)(2,1)S(1)}, bf16[64,128]{1,0:T(8,128)(2,1)S(1)}, u32[]{:S(2)}, u32[]{:S(2)}) collective-permute-start(bf16[64,128]{1,0:T(8,128)(2,1)S(1)} %get-tuple-element.30), channel_id=1, source_target_pairs={{0,3},{1,2},{2,1},{3,0},{4,7},{5,6},{6,5},{7,4},{8,11},{9,10},{10,... | collective-permute-start | bytes 49160 | tf_op jit(solution)/shard_map/ppermute | solution.py:75
  21.8 1.3 %collective-permute-start.8 = (bf16[64,128]{1,0:T(8,128)(2,1)S(1)}, bf16[64,128]{1,0:T(8,128)(2,1)S(1)}, u32[]{:S(2)}, u32[]{:S(2)}) collective-permute-start(bf16[64,128]{1,0:T(8,128)(2,1)S(1)} %get-tuple-element.29), channel_id=1, source_target_pairs={{0,19},{1,18},{2,17},{3,16},{4,23},{5,22},{6,21},{7,20},{8,27},{9,... | collective-permute-start | bytes 49160 | tf_op jit(solution)/shard_map/ppermute | solution.py:75
  23.1 0.3 collective-permute-start.7
  23.4 0.2 collective-permute-done.6
  23.6 2.3 %collective-permute-done.8 = bf16[64,128]{1,0:T(8,128)(2,1)S(1)} collective-permute-done((bf16[64,128]{1,0:T(8,128)(2,1)S(1)}, bf16[64,128]{1,0:T(8,128)(2,1)S(1)}, u32[]{:S(2)}, u32[]{:S(2)}) %collective-permute-start.8) | collective-permute-done | bytes 16416 | tf_op jit(solution)/shard_map/ppermute | solution.py:75
  25.9 0.4 %collective-permute-done.7 = bf16[64,128]{1,0:T(8,128)(2,1)S(1)} collective-permute-done((bf16[64,128]{1,0:T(8,128)(2,1)S(1)}, bf16[64,128]{1,0:T(8,128)(2,1)S(1)}, u32[]{:S(2)}, u32[]{:S(2)}) %collective-permute-start.7) | collective-permute-done | bytes 16416 | tf_op jit(solution)/shard_map/ppermute | solution.py:75
  26.3 1.6 %collective-permute-start.9 = (bf16[128,128]{1,0:T(8,128)(2,1)S(1)}, bf16[128,128]{1,0:T(8,128)(2,1)S(1)}, u32[]{:S(2)}, u32[]{:S(2)}) collective-permute-start(bf16[128,128]{1,0:T(8,128)(2,1)S(1)} %fusion.2), channel_id=1, source_target_pairs={{0,5},{1,4},{2,7},{3,6},{4,1},{5,0},{6,3},{7,2},{8,13},{9,12},{10,... | collective-permute-start | bytes 98312 | tf_op jit(solution)/shard_map/ppermute | solution.py:75
  27.9 1.8 %collective-permute-done.9 = bf16[128,128]{1,0:T(8,128)(2,1)S(1)} collective-permute-done((bf16[128,128]{1,0:T(8,128)(2,1)S(1)}, bf16[128,128]{1,0:T(8,128)(2,1)S(1)}, u32[]{:S(2)}, u32[]{:S(2)}) %collective-permute-start.9) | collective-permute-done | bytes 32800 | tf_op jit(solution)/shard_map/ppermute | solution.py:75
  29.7 2.6 %collective-permute-start.10 = (bf16[128,128]{1,0:T(8,128)(2,1)S(1)}, bf16[128,128]{1,0:T(8,128)(2,1)S(1)}, u32[]{:S(2)}, u32[]{:S(2)}) collective-permute-start(bf16[128,128]{1,0:T(8,128)(2,1)S(1)} %fusion.1), channel_id=1, source_target_pairs={{0,9},{1,8},{2,11},{3,10},{4,13},{5,12},{6,15},{7,14},{8,1},{9,0},... | collective-permute-start | bytes 98312 | tf_op jit(solution)/shard_map/ppermute | solution.py:75
  32.3 1.7 %collective-permute-done.10 = bf16[128,128]{1,0:T(8,128)(2,1)S(1)} collective-permute-done((bf16[128,128]{1,0:T(8,128)(2,1)S(1)}, bf16[128,128]{1,0:T(8,128)(2,1)S(1)}, u32[]{:S(2)}, u32[]{:S(2)}) %collective-permute-start.10) | collective-permute-done | bytes 32800 | tf_op jit(solution)/shard_map/ppermute | solution.py:75
  34.1 1.0 %shard_map.77 = bf16[24,128,128]{2,1,0:T(8,128)(2,1)} custom-call(f32[128,128]{1,0:T(8,128)S(1)} %convert_add_fusion.rotated, f32[24,128,128]{2,1,0:T(8,128)S(1)} %broadcast_in_dim.2.scale), custom_call_target="tpu_custom_call" | custom-call | tf_op jit(solution)/shard_map/pallas_call | solution.py:351
  (10 shorter events, 0.1 us)
Async XLA Ops:
  0.0 10.6 %copy-start = (bf16[768,128]{1,0:T(8,128)(2,1)S(1)}, bf16[768,128]{1,0:T(8,128)(2,1)}, u32[]{:S(2)}) copy-start(bf16[768,128]{1,0:T(8,128)(2,1)} %bold.3) | copy-start | bytes 589828
  0.0 6.3 %collective-permute-start.2 = (bf16[64,4096]{1,0:T(8,128)(2,1)}, bf16[64,4096]{1,0:T(8,128)(2,1)S(1)}, u32[]{:S(2)}, u32[]{:S(2)}) collective-permute-start(bf16[64,4096]{1,0:T(8,128)(2,1)} %bitcast.2), channel_id=1, source_target_pairs={{0,1},{1,0},{2,3},{3,2},{4,5},{5,4},{6,7},{7,6},{8,9},{9,8},{10,11... | collective-permute-start | bytes 1572872 | tf_op jit(solution)/shard_map/ppermute | solution.py:75
  0.5 15.1 %collective-permute-start = (bf16[64,4096]{1,0:T(8,128)(2,1)}, bf16[64,4096]{1,0:T(8,128)(2,1)S(1)}, u32[]{:S(2)}, u32[]{:S(2)}) collective-permute-start(bf16[64,4096]{1,0:T(8,128)(2,1)} %bitcast.3), channel_id=1, source_target_pairs={{0,3},{1,2},{2,1},{3,0},{4,7},{5,6},{6,5},{7,4},{8,11},{9,10},{10,... | collective-permute-start | bytes 1572872 | tf_op jit(solution)/shard_map/ppermute | solution.py:75
  3.1 7.1 %collective-permute-start.1 = (bf16[768,128]{1,0:T(8,128)(2,1)}, bf16[768,128]{1,0:T(8,128)(2,1)S(1)}, u32[]{:S(2)}, u32[]{:S(2)}) collective-permute-start(bf16[768,128]{1,0:T(8,128)(2,1)} %bold.3), channel_id=1, source_target_pairs={{0,16},{1,17},{2,18},{3,19},{4,20},{5,21},{6,22},{7,23},{8,24},{9,... | collective-permute-start | bytes 589832 | tf_op jit(solution)/shard_map/ppermute | solution.py:75
  4.6 7.4 %copy-start.1 = (bf16[768,2048]{1,0:T(8,128)(2,1)S(1)}, bf16[768,2048]{1,0:T(8,128)(2,1)}, u32[]{:S(2)}) copy-start(bf16[768,2048]{1,0:T(8,128)(2,1)} %hidden.1) | copy-start | bytes 9437188
  10.7 4.9 %collective-permute-start.3 = (bf16[16,256]{1,0:T(8,128)(2,1)S(1)}, bf16[16,256]{1,0:T(8,128)(2,1)S(1)}, u32[]{:S(2)}, u32[]{:S(2)}) collective-permute-start(bf16[16,256]{1,0:T(8,128)(2,1)S(1)} %shard_map.74), channel_id=1, source_target_pairs={{1,0},{2,1},{3,2},{5,4},{6,5},{7,6},{9,8},{10,9},{11,10},{13,12},{... | collective-permute-start | bytes 24584 | tf_op jit(solution)/shard_map/ppermute | solution.py:20
  15.5 1.9 %collective-permute-start.4 = (bf16[64,4096]{1,0:T(8,128)(2,1)S(1)}, bf16[64,4096]{1,0:T(8,128)(2,1)S(1)}, u32[]{:S(2)}, u32[]{:S(2)}) collective-permute-start(bf16[64,4096]{1,0:T(8,128)(2,1)S(1)} %collective-permute-done.panel_t), channel_id=1, source_target_pairs={{0,1},{1,0},{2,3},{3,2},{4,5},{5,4},{6,7},{7,6},{8,9},{9,8},{10,11... | collective-permute-start | bytes 1572872 | tf_op jit(solution)/shard_map/ppermute | solution.py:75
  19.1 1.3 %collective-permute-start.5 = (bf16[64,256]{1,0:T(8,128)(2,1)S(1)}, bf16[64,256]{1,0:T(8,128)(2,1)S(1)}, u32[]{:S(2)}, u32[]{:S(2)}) collective-permute-start(bf16[64,256]{1,0:T(8,128)(2,1)S(1)} %reduce-precision_convert_fusion.1), channel_id=1, source_target_pairs={{0,1},{1,0},{2,3},{3,2},{4,5},{5,4},{6,7},{7,6},{8,9},{9,8},{10,11... | collective-permute-start | bytes 98312 | tf_op jit(solution)/shard_map/ppermute | solution.py:75
  20.4 3.2 %collective-permute-start.6 = (bf16[64,128]{1,0:T(8,128)(2,1)S(1)}, bf16[64,128]{1,0:T(8,128)(2,1)S(1)}, u32[]{:S(2)}, u32[]{:S(2)}) collective-permute-start(bf16[64,128]{1,0:T(8,128)(2,1)S(1)} %get-tuple-element.30), channel_id=1, source_target_pairs={{0,3},{1,2},{2,1},{3,0},{4,7},{5,6},{6,5},{7,4},{8,11},{9,10},{10,... | collective-permute-start | bytes 49160 | tf_op jit(solution)/shard_map/ppermute | solution.py:75
  21.8 4.1 %collective-permute-start.8 = (bf16[64,128]{1,0:T(8,128)(2,1)S(1)}, bf16[64,128]{1,0:T(8,128)(2,1)S(1)}, u32[]{:S(2)}, u32[]{:S(2)}) collective-permute-start(bf16[64,128]{1,0:T(8,128)(2,1)S(1)} %get-tuple-element.29), channel_id=1, source_target_pairs={{0,19},{1,18},{2,17},{3,16},{4,23},{5,22},{6,21},{7,20},{8,27},{9,... | collective-permute-start | bytes 49160 | tf_op jit(solution)/shard_map/ppermute | solution.py:75
  23.1 3.2 %collective-permute-start.7 = (bf16[64,128]{1,0:T(8,128)(2,1)S(1)}, bf16[64,128]{1,0:T(8,128)(2,1)S(1)}, u32[]{:S(2)}, u32[]{:S(2)}) collective-permute-start(bf16[64,128]{1,0:T(8,128)(2,1)S(1)} %get-tuple-element.29), channel_id=1, source_target_pairs={{0,17},{1,16},{2,19},{3,18},{4,21},{5,20},{6,23},{7,22},{8,25},{9,... | collective-permute-start | bytes 49160 | tf_op jit(solution)/shard_map/ppermute | solution.py:75
  26.3 3.4 %collective-permute-start.9 = (bf16[128,128]{1,0:T(8,128)(2,1)S(1)}, bf16[128,128]{1,0:T(8,128)(2,1)S(1)}, u32[]{:S(2)}, u32[]{:S(2)}) collective-permute-start(bf16[128,128]{1,0:T(8,128)(2,1)S(1)} %fusion.2), channel_id=1, source_target_pairs={{0,5},{1,4},{2,7},{3,6},{4,1},{5,0},{6,3},{7,2},{8,13},{9,12},{10,... | collective-permute-start | bytes 98312 | tf_op jit(solution)/shard_map/ppermute | solution.py:75
  29.7 4.3 %collective-permute-start.10 = (bf16[128,128]{1,0:T(8,128)(2,1)S(1)}, bf16[128,128]{1,0:T(8,128)(2,1)S(1)}, u32[]{:S(2)}, u32[]{:S(2)}) collective-permute-start(bf16[128,128]{1,0:T(8,128)(2,1)S(1)} %fusion.1), channel_id=1, source_target_pairs={{0,9},{1,8},{2,11},{3,10},{4,13},{5,12},{6,15},{7,14},{8,1},{9,0},... | collective-permute-start | bytes 98312 | tf_op jit(solution)/shard_map/ppermute | solution.py:75

commit v9 on v8

--- a/solution.py
+++ b/solution.py
@@ -314,10 +314,10 @@
     scale = 1.0 / (math.sqrt(total_rows) * (eigvals[None, :] + penalty[:, None]))
     scale = jnp.broadcast_to(scale[:, :, None], (*scale.shape, v_cols))
     head = call(
-        head_kernel, (bold, after(bold_x, (earlier, scale))), jax.ShapeDtypeStruct((16, 2 * v_cols), BF16), []
+        head_kernel, (bold, after(bold_x, earlier)), jax.ShapeDtypeStruct((16, 2 * v_cols), BF16), []
     )
     ahead = passed_along(head, "tm", -1)
-    hidden_late = after(hidden, head)
+    hidden_late = after(hidden, (head, scale))
     hidden_own = lax.dynamic_slice_in_dim(hidden_late, (tm ^ 3) * width, width, 1)
     hidden_core = lax.dynamic_slice_in_dim(hidden_late, (tm ^ 2) * width, width, 1)
     late_t = after(late_t, (ahead, hidden_own, hidden_core))

time: 35.2 us -> 35.2 us (level)
  no operation moved by 1% of the time
where the time goes in v9:
time: 35.2 us; the launch traced here: 35 us
  starting transfers between devices  13.5 us (38%)
  waiting for transfers between devices  11.2 us (32%)
  Pallas kernels  7.82 us (22%)
  other arithmetic  1.76 us (5%)
  local copies, waits for them, and re-layouts  0.65 us (2%)
    ppermute x10, starting transfers between devices, swapped(): return lax.ppermute(value, ('voxel', 'feature', 'tm'), pairs)  12.2 us
    ppermute x10, waiting for transfers between devices, swapped(): return lax.ppermute(value, ('voxel', 'feature', 'tm'), pairs)  11.2 us
    pallas_call x4, Pallas kernels, call(): pl.pallas_call(kernel, out_shape=out_shape, in_specs=[hbm if n in outside...  6.87 us
    ppermute x1, starting transfers between devices, passed_along(): lax.ppermute(value, axis, [(source, source + steps) for source in range(f...  1.28 us
    pallas_call x1, Pallas kernels, exchanged(): pl.pallas_call(scale_kernel, out_shape=jax.ShapeDtypeStruct(shape, BF16),...  0.95 us
    div x1, other arithmetic, exchanged(): 1.0 / (math.sqrt(total_rows) * (eigvals[None, :] + penalty[:, None]))  0.88 us
    pow x1, other arithmetic, exchanged(): penalty = 2.0 ** ((ridge_grid.astype(F32) - 8.0) * 0.5)  0.81 us
  transfers between devices with their start and end apart: 11, of which 9 were waited for; matrix products, arithmetic and copies ran while one was open for 7% of the time, Pallas kernels for 15%

profile of v9, /device:TPU:0, one launch (start us, length us, event | category | flops | bytes accessed | tf_op | source)
XLA Modules:
  0.0 35.0 jit_solution(6911041212490102577)
XLA Ops:
  0.0 0.5 %collective-permute-start.2 = (bf16[64,4096]{1,0:T(8,128)(2,1)}, bf16[64,4096]{1,0:T(8,128)(2,1)S(1)}, u32[]{:S(2)}, u32[]{:S(2)}) collective-permute-start(bf16[64,4096]{1,0:T(8,128)(2,1)} %bitcast.2), channel_id=1, source_target_pairs={{0,1},{1,0},{2,3},{3,2},{4,5},{5,4},{6,7},{7,6},{8,9},{9,8},{10,11... | collective-permute-start | bytes 1572872 | tf_op jit(solution)/shard_map/ppermute | solution.py:75
  0.5 2.6 %collective-permute-start = (bf16[64,4096]{1,0:T(8,128)(2,1)}, bf16[64,4096]{1,0:T(8,128)(2,1)S(1)}, u32[]{:S(2)}, u32[]{:S(2)}) collective-permute-start(bf16[64,4096]{1,0:T(8,128)(2,1)} %bitcast.3), channel_id=1, source_target_pairs={{0,3},{1,2},{2,1},{3,0},{4,7},{5,6},{6,5},{7,4},{8,11},{9,10},{10,... | collective-permute-start | bytes 1572872 | tf_op jit(solution)/shard_map/ppermute | solution.py:75
  3.1 1.5 %collective-permute-start.1 = (bf16[768,128]{1,0:T(8,128)(2,1)}, bf16[768,128]{1,0:T(8,128)(2,1)S(1)}, u32[]{:S(2)}, u32[]{:S(2)}) collective-permute-start(bf16[768,128]{1,0:T(8,128)(2,1)} %bold.3), channel_id=1, source_target_pairs={{0,16},{1,17},{2,18},{3,19},{4,20},{5,21},{6,22},{7,23},{8,24},{9,... | collective-permute-start | bytes 589832 | tf_op jit(solution)/shard_map/ppermute | solution.py:75
  4.6 0.8 %multiply_power_fusion = f32[24]{0:T(128)S(1)} fusion(s32[24]{0:T(128)} %param.11), kind=kLoop, calls=%fused_computation.11 | loop fusion | flops 72 | bytes 192 | tf_op jit(solution)/shard_map/pow | solution.py:313
  5.4 0.9 %multiply_divide_fusion = f32[24,128]{1,0:T(8,128)S(1)} fusion(f32[24]{0:T(128)S(1)} %multiply_power_fusion, f32[128]{0:T(128)} %param.10), kind=kLoop, calls=%fused_computation.9 | loop fusion | flops 9216 | bytes 12896 | tf_op jit(solution)/shard_map/div | solution.py:314
  6.3 0.0 collective-permute-done.2.panel_core
  6.3 3.8 %shard_map.73 = (f32[64,896]{1,0:T(8,128)S(1)}, bf16[4,256,256]{2,1,0:T(8,128)(2,1)S(1)}, f32[64,128]{1,0:T(8,128)S(1)}, bf16[1024,256]{1,0:T(8,128)(2,1)S(1)}) custom-call(s32[8]{0:T(128)} %delays_in.1, bf16[64,4096]{1,0:T(8,128)(2,1)} %bitcast.4, bf16[64,4096]{1,0:T(8,128)(2,1)S(1)} %collective-permute-done.2.panel_core, bf16[768,2048]{1,0:T(8,128)(2,1)} %hidden.1, ...), custom_call_target="tpu_custom_call" | custom-call | flops 1024 | bytes 1024 | tf_op jit(solution)/shard_map/pallas_call | solution.py:264
  10.1 0.1 collective-permute-done.1.bold_x
  10.2 0.0 copy-done
  10.2 1.3 %collective-permute-start.3 = (bf16[16,256]{1,0:T(8,128)(2,1)S(1)}, bf16[16,256]{1,0:T(8,128)(2,1)S(1)}, u32[]{:S(2)}, u32[]{:S(2)}) collective-permute-start(bf16[16,256]{1,0:T(8,128)(2,1)S(1)} %shard_map.74), channel_id=1, source_target_pairs={{1,0},{2,1},{3,2},{5,4},{6,5},{7,6},{9,8},{10,9},{11,10},{13,12},{... | collective-permute-start | bytes 24584 | tf_op jit(solution)/shard_map/ppermute | solution.py:20
  11.5 0.5 %broadcast_in_dim.2.scale = f32[24,128,128]{2,1,0:T(8,128)S(1)} broadcast(f32[24,128]{1,0:T(8,128)S(1)} %multiply_divide_fusion), dimensions={0,1} | broadcast | bytes 1585152 | tf_op jit(solution)/shard_map/broadcast_in_dim | solution.py:315
  11.9 0.0 copy-done.1
  11.9 0.2 constant_dynamic-slice_fusion
  12.1 3.4 %collective-permute-done.panel_t = bf16[64,4096]{1,0:T(8,128)(2,1)S(1)} collective-permute-done((bf16[64,4096]{1,0:T(8,128)(2,1)}, bf16[64,4096]{1,0:T(8,128)(2,1)S(1)}, u32[]{:S(2)}, u32[]{:S(2)}) %collective-permute-start) | collective-permute-done | bytes 524320 | tf_op jit(solution)/shard_map/ppermute | solution.py:75
  15.5 0.0 collective-permute-done.3.ahead
  15.5 0.2 collective-permute-start.4
  15.7 1.5 %shard_map.75.earlier = f32[64,896]{1,0:T(8,128)S(1)} custom-call(bf16[64,4096]{1,0:T(8,128)(2,1)S(1)} %collective-permute-done.panel_t, bf16[4,256,256]{2,1,0:T(8,128)(2,1)S(1)} %get-tuple-element.20.sort, bf16[768,512]{1,0:T(8,128)(2,1)S(1)} %get-tuple-element.28.hidden, f32[64,128]{1,0:T(8,128)S(1)} %get-tuple-element.21.valid, ...), custom_call_target="tpu_custom_call" | custom-call | flops 1024 | bytes 1024 | tf_op jit(solution)/shard_map/pallas_call | solution.py:264
  17.1 0.3 collective-permute-done.4.panel_t
  17.4 1.6 %shard_map.76 = f32[64,256]{1,0:T(8,128)S(1)} custom-call(bf16[64,4096]{1,0:T(8,128)(2,1)S(1)} %collective-permute-done.4.panel_t, bf16[4,256,256]{2,1,0:T(8,128)(2,1)S(1)} %get-tuple-element.20.sort, bf16[768,512]{1,0:T(8,128)(2,1)S(1)} %get-tuple-element.27.hidden, f32[64,128]{1,0:T(8,128)S(1)} %get-tuple-element.21.valid, ...), custom_call_target="tpu_custom_call" | custom-call | flops 1024 | bytes 1024 | tf_op jit(solution)/shard_map/pallas_call | solution.py:264
  19.1 0.2 collective-permute-start.5
  19.3 1.1 %collective-permute-done.5 = bf16[64,256]{1,0:T(8,128)(2,1)S(1)} collective-permute-done((bf16[64,256]{1,0:T(8,128)(2,1)S(1)}, bf16[64,256]{1,0:T(8,128)(2,1)S(1)}, u32[]{:S(2)}, u32[]{:S(2)}) %collective-permute-start.5) | collective-permute-done | bytes 32800 | tf_op jit(solution)/shard_map/ppermute | solution.py:75
  20.4 1.4 %collective-permute-start.6 = (bf16[64,128]{1,0:T(8,128)(2,1)S(1)}, bf16[64,128]{1,0:T(8,128)(2,1)S(1)}, u32[]{:S(2)}, u32[]{:S(2)}) collective-permute-start(bf16[64,128]{1,0:T(8,128)(2,1)S(1)} %get-tuple-element.30), channel_id=1, source_target_pairs={{0,3},{1,2},{2,1},{3,0},{4,7},{5,6},{6,5},{7,4},{8,11},{9,10},{10,... | collective-permute-start | bytes 49160 | tf_op jit(solution)/shard_map/ppermute | solution.py:75
  21.8 1.3 %collective-permute-start.8 = (bf16[64,128]{1,0:T(8,128)(2,1)S(1)}, bf16[64,128]{1,0:T(8,128)(2,1)S(1)}, u32[]{:S(2)}, u32[]{:S(2)}) collective-permute-start(bf16[64,128]{1,0:T(8,128)(2,1)S(1)} %get-tuple-element.29), channel_id=1, source_target_pairs={{0,19},{1,18},{2,17},{3,16},{4,23},{5,22},{6,21},{7,20},{8,27},{9,... | collective-permute-start | bytes 49160 | tf_op jit(solution)/shard_map/ppermute | solution.py:75
  23.1 0.3 collective-permute-start.7
  23.4 0.2 collective-permute-done.6
  23.6 2.3 %collective-permute-done.8 = bf16[64,128]{1,0:T(8,128)(2,1)S(1)} collective-permute-done((bf16[64,128]{1,0:T(8,128)(2,1)S(1)}, bf16[64,128]{1,0:T(8,128)(2,1)S(1)}, u32[]{:S(2)}, u32[]{:S(2)}) %collective-permute-start.8) | collective-permute-done | bytes 16416 | tf_op jit(solution)/shard_map/ppermute | solution.py:75
  25.9 0.4 %collective-permute-done.7 = bf16[64,128]{1,0:T(8,128)(2,1)S(1)} collective-permute-done((bf16[64,128]{1,0:T(8,128)(2,1)S(1)}, bf16[64,128]{1,0:T(8,128)(2,1)S(1)}, u32[]{:S(2)}, u32[]{:S(2)}) %collective-permute-start.7) | collective-permute-done | bytes 16416 | tf_op jit(solution)/shard_map/ppermute | solution.py:75
  26.3 1.6 %collective-permute-start.9 = (bf16[128,128]{1,0:T(8,128)(2,1)S(1)}, bf16[128,128]{1,0:T(8,128)(2,1)S(1)}, u32[]{:S(2)}, u32[]{:S(2)}) collective-permute-start(bf16[128,128]{1,0:T(8,128)(2,1)S(1)} %fusion.2), channel_id=1, source_target_pairs={{0,5},{1,4},{2,7},{3,6},{4,1},{5,0},{6,3},{7,2},{8,13},{9,12},{10,... | collective-permute-start | bytes 98312 | tf_op jit(solution)/shard_map/ppermute | solution.py:75
  27.9 1.8 %collective-permute-done.9 = bf16[128,128]{1,0:T(8,128)(2,1)S(1)} collective-permute-done((bf16[128,128]{1,0:T(8,128)(2,1)S(1)}, bf16[128,128]{1,0:T(8,128)(2,1)S(1)}, u32[]{:S(2)}, u32[]{:S(2)}) %collective-permute-start.9) | collective-permute-done | bytes 32800 | tf_op jit(solution)/shard_map/ppermute | solution.py:75
  29.7 2.6 %collective-permute-start.10 = (bf16[128,128]{1,0:T(8,128)(2,1)S(1)}, bf16[128,128]{1,0:T(8,128)(2,1)S(1)}, u32[]{:S(2)}, u32[]{:S(2)}) collective-permute-start(bf16[128,128]{1,0:T(8,128)(2,1)S(1)} %fusion.1), channel_id=1, source_target_pairs={{0,9},{1,8},{2,11},{3,10},{4,13},{5,12},{6,15},{7,14},{8,1},{9,0},... | collective-permute-start | bytes 98312 | tf_op jit(solution)/shard_map/ppermute | solution.py:75
  32.3 1.7 %collective-permute-done.10 = bf16[128,128]{1,0:T(8,128)(2,1)S(1)} collective-permute-done((bf16[128,128]{1,0:T(8,128)(2,1)S(1)}, bf16[128,128]{1,0:T(8,128)(2,1)S(1)}, u32[]{:S(2)}, u32[]{:S(2)}) %collective-permute-start.10) | collective-permute-done | bytes 32800 | tf_op jit(solution)/shard_map/ppermute | solution.py:75
  34.1 1.0 %shard_map.77 = bf16[24,128,128]{2,1,0:T(8,128)(2,1)} custom-call(f32[128,128]{1,0:T(8,128)S(1)} %convert_add_fusion.rotated, f32[24,128,128]{2,1,0:T(8,128)S(1)} %broadcast_in_dim.2.scale), custom_call_target="tpu_custom_call" | custom-call | tf_op jit(solution)/shard_map/pallas_call | solution.py:351
  (10 shorter events, 0.1 us)
Async XLA Ops:
  0.0 10.2 %copy-start = (bf16[768,128]{1,0:T(8,128)(2,1)S(1)}, bf16[768,128]{1,0:T(8,128)(2,1)}, u32[]{:S(2)}) copy-start(bf16[768,128]{1,0:T(8,128)(2,1)} %bold.3) | copy-start | bytes 589828
  0.0 6.3 %collective-permute-start.2 = (bf16[64,4096]{1,0:T(8,128)(2,1)}, bf16[64,4096]{1,0:T(8,128)(2,1)S(1)}, u32[]{:S(2)}, u32[]{:S(2)}) collective-permute-start(bf16[64,4096]{1,0:T(8,128)(2,1)} %bitcast.2), channel_id=1, source_target_pairs={{0,1},{1,0},{2,3},{3,2},{4,5},{5,4},{6,7},{7,6},{8,9},{9,8},{10,11... | collective-permute-start | bytes 1572872 | tf_op jit(solution)/shard_map/ppermute | solution.py:75
  0.5 15.1 %collective-permute-start = (bf16[64,4096]{1,0:T(8,128)(2,1)}, bf16[64,4096]{1,0:T(8,128)(2,1)S(1)}, u32[]{:S(2)}, u32[]{:S(2)}) collective-permute-start(bf16[64,4096]{1,0:T(8,128)(2,1)} %bitcast.3), channel_id=1, source_target_pairs={{0,3},{1,2},{2,1},{3,0},{4,7},{5,6},{6,5},{7,4},{8,11},{9,10},{10,... | collective-permute-start | bytes 1572872 | tf_op jit(solution)/shard_map/ppermute | solution.py:75
  3.1 7.1 %collective-permute-start.1 = (bf16[768,128]{1,0:T(8,128)(2,1)}, bf16[768,128]{1,0:T(8,128)(2,1)S(1)}, u32[]{:S(2)}, u32[]{:S(2)}) collective-permute-start(bf16[768,128]{1,0:T(8,128)(2,1)} %bold.3), channel_id=1, source_target_pairs={{0,16},{1,17},{2,18},{3,19},{4,20},{5,21},{6,22},{7,23},{8,24},{9,... | collective-permute-start | bytes 589832 | tf_op jit(solution)/shard_map/ppermute | solution.py:75
  4.6 7.4 %copy-start.1 = (bf16[768,2048]{1,0:T(8,128)(2,1)S(1)}, bf16[768,2048]{1,0:T(8,128)(2,1)}, u32[]{:S(2)}) copy-start(bf16[768,2048]{1,0:T(8,128)(2,1)} %hidden.1) | copy-start | bytes 9437188
  10.2 5.4 %collective-permute-start.3 = (bf16[16,256]{1,0:T(8,128)(2,1)S(1)}, bf16[16,256]{1,0:T(8,128)(2,1)S(1)}, u32[]{:S(2)}, u32[]{:S(2)}) collective-permute-start(bf16[16,256]{1,0:T(8,128)(2,1)S(1)} %shard_map.74), channel_id=1, source_target_pairs={{1,0},{2,1},{3,2},{5,4},{6,5},{7,6},{9,8},{10,9},{11,10},{13,12},{... | collective-permute-start | bytes 24584 | tf_op jit(solution)/shard_map/ppermute | solution.py:20
  15.5 1.9 %collective-permute-start.4 = (bf16[64,4096]{1,0:T(8,128)(2,1)S(1)}, bf16[64,4096]{1,0:T(8,128)(2,1)S(1)}, u32[]{:S(2)}, u32[]{:S(2)}) collective-permute-start(bf16[64,4096]{1,0:T(8,128)(2,1)S(1)} %collective-permute-done.panel_t), channel_id=1, source_target_pairs={{0,1},{1,0},{2,3},{3,2},{4,5},{5,4},{6,7},{7,6},{8,9},{9,8},{10,11... | collective-permute-start | bytes 1572872 | tf_op jit(solution)/shard_map/ppermute | solution.py:75
  19.1 1.3 %collective-permute-start.5 = (bf16[64,256]{1,0:T(8,128)(2,1)S(1)}, bf16[64,256]{1,0:T(8,128)(2,1)S(1)}, u32[]{:S(2)}, u32[]{:S(2)}) collective-permute-start(bf16[64,256]{1,0:T(8,128)(2,1)S(1)} %reduce-precision_convert_fusion.1), channel_id=1, source_target_pairs={{0,1},{1,0},{2,3},{3,2},{4,5},{5,4},{6,7},{7,6},{8,9},{9,8},{10,11... | collective-permute-start | bytes 98312 | tf_op jit(solution)/shard_map/ppermute | solution.py:75
  20.4 3.2 %collective-permute-start.6 = (bf16[64,128]{1,0:T(8,128)(2,1)S(1)}, bf16[64,128]{1,0:T(8,128)(2,1)S(1)}, u32[]{:S(2)}, u32[]{:S(2)}) collective-permute-start(bf16[64,128]{1,0:T(8,128)(2,1)S(1)} %get-tuple-element.30), channel_id=1, source_target_pairs={{0,3},{1,2},{2,1},{3,0},{4,7},{5,6},{6,5},{7,4},{8,11},{9,10},{10,... | collective-permute-start | bytes 49160 | tf_op jit(solution)/shard_map/ppermute | solution.py:75
  21.8 4.1 %collective-permute-start.8 = (bf16[64,128]{1,0:T(8,128)(2,1)S(1)}, bf16[64,128]{1,0:T(8,128)(2,1)S(1)}, u32[]{:S(2)}, u32[]{:S(2)}) collective-permute-start(bf16[64,128]{1,0:T(8,128)(2,1)S(1)} %get-tuple-element.29), channel_id=1, source_target_pairs={{0,19},{1,18},{2,17},{3,16},{4,23},{5,22},{6,21},{7,20},{8,27},{9,... | collective-permute-start | bytes 49160 | tf_op jit(solution)/shard_map/ppermute | solution.py:75
  23.1 3.2 %collective-permute-start.7 = (bf16[64,128]{1,0:T(8,128)(2,1)S(1)}, bf16[64,128]{1,0:T(8,128)(2,1)S(1)}, u32[]{:S(2)}, u32[]{:S(2)}) collective-permute-start(bf16[64,128]{1,0:T(8,128)(2,1)S(1)} %get-tuple-element.29), channel_id=1, source_target_pairs={{0,17},{1,16},{2,19},{3,18},{4,21},{5,20},{6,23},{7,22},{8,25},{9,... | collective-permute-start | bytes 49160 | tf_op jit(solution)/shard_map/ppermute | solution.py:75
  26.3 3.4 %collective-permute-start.9 = (bf16[128,128]{1,0:T(8,128)(2,1)S(1)}, bf16[128,128]{1,0:T(8,128)(2,1)S(1)}, u32[]{:S(2)}, u32[]{:S(2)}) collective-permute-start(bf16[128,128]{1,0:T(8,128)(2,1)S(1)} %fusion.2), channel_id=1, source_target_pairs={{0,5},{1,4},{2,7},{3,6},{4,1},{5,0},{6,3},{7,2},{8,13},{9,12},{10,... | collective-permute-start | bytes 98312 | tf_op jit(solution)/shard_map/ppermute | solution.py:75
  29.7 4.3 %collective-permute-start.10 = (bf16[128,128]{1,0:T(8,128)(2,1)S(1)}, bf16[128,128]{1,0:T(8,128)(2,1)S(1)}, u32[]{:S(2)}, u32[]{:S(2)}) collective-permute-start(bf16[128,128]{1,0:T(8,128)(2,1)S(1)} %fusion.1), channel_id=1, source_target_pairs={{0,9},{1,8},{2,11},{3,10},{4,13},{5,12},{6,15},{7,14},{8,1},{9,0},... | collective-permute-start | bytes 98312 | tf_op jit(solution)/shard_map/ppermute | solution.py:75
